TPU v7x, 32 devices: a whole 2x2x4 slice. The times are simulated.
32 devices in a mesh: section: 2 (over core), seq: 4 (over z), tensor: 4 (over y, x).
Axes of the slice: x: 2, y: 2, z: 4, core: 2. Of those that a mesh axis runs over, the one named last changes fastest.
Arguments:
- inputs: bfloat16 [3, 1024, 2048], P(None, 'seq'), may hold values from -6 to 6
- cotangent: bfloat16 [3, 1024, 2048], P(None, 'seq'), may hold values from -6 to 6
- query_proj: bfloat16 [2, 2048, 1024], P('section', 'seq', 'tensor'), may hold values from -0.125 to 0.125
- key_proj: bfloat16 [2, 2048, 1024], P('section', 'seq', 'tensor'), may hold values from -0.125 to 0.125
- value_proj: bfloat16 [2, 2048, 2048], P('section', 'seq', 'tensor'), may hold values from -0.125 to 0.125
- outgate_proj: bfloat16 [2, 2048, 2048], P('section', 'seq', 'tensor'), may hold values from -0.125 to 0.125
- output_proj: bfloat16 [2, 2048, 2048], P('section', 'seq', 'tensor'), may hold values from -0.125 to 0.125
- decay_down: bfloat16 [2, 2048, 16], P('section', 'seq'), may hold values from -0.125 to 0.125
- decay_up: bfloat16 [2, 256, 64], P('section', 'seq', 'tensor'), may hold values from -4 to 4
- decay_bias: bfloat16 [2, 256, 4], P('section', 'seq', 'tensor'), may hold values from -1 to 14
- head_gain: bfloat16 [2, 512], P('section', 'seq'), may hold values from 0.099609375 to 1.8984375
- mixer_gain: bfloat16 [2, 2048], P('section', 'seq'), may hold values from 0.099609375 to 1.8984375
- feed_gain: bfloat16 [2, 2048], P('section', 'seq'), may hold values from 0.099609375 to 1.8984375
- feed_gate: bfloat16 [2, 2048, 5632], P('section', 'seq', 'tensor'), may hold values from -0.125 to 0.125
- feed_up: bfloat16 [2, 2048, 5632], P('section', 'seq', 'tensor'), may hold values from -0.125 to 0.125
- feed_down: bfloat16 [2, 2048, 5632], P('section', 'seq', 'tensor'), may hold values from -0.078125 to 0.078125
Outputs:
- layer_outputs: bfloat16 [2, 3, 1024, 2048], P('section', None, 'seq')
- input_grads: float32 [2, 3, 1024, 2048], P('section', None, 'seq')
- query_proj_grad: float32 [2, 2048, 1024], P('section', 'seq', 'tensor')
- key_proj_grad: float32 [2, 2048, 1024], P('section', 'seq', 'tensor')
- value_proj_grad: float32 [2, 2048, 2048], P('section', 'seq', 'tensor')
- outgate_proj_grad: float32 [2, 2048, 2048], P('section', 'seq', 'tensor')
- output_proj_grad: float32 [2, 2048, 2048], P('section', 'seq', 'tensor')
- decay_down_grad: float32 [2, 2048, 16], P('section', 'seq')
- decay_up_grad: float32 [2, 256, 64], P('section', 'seq', 'tensor')
- decay_bias_grad: float32 [2, 256, 4], P('section', 'seq', 'tensor')
- head_gain_grad: float32 [2, 512], P('section', 'seq')
- mixer_gain_grad: float32 [2, 2048], P('section', 'seq')
- feed_gain_grad: float32 [2, 2048], P('section', 'seq')
- feed_gate_grad: float32 [2, 2048, 5632], P('section', 'seq', 'tensor')
- feed_up_grad: float32 [2, 2048, 5632], P('section', 'seq', 'tensor')
- feed_down_grad: float32 [2, 2048, 5632], P('section', 'seq', 'tensor')
All inputs are finite; a program needn't handle non-finite values.
Results may differ from a plain program's by a relative error of at most 0.035.
Values may be sent and summed in bfloat16 or wider, within the bound.
A program may use at most 320 MiB of HBM per device.

v0:
```python
from functools import partial

import jax
import jax.numpy as jnp
from jax import lax
from jax.sharding import PartitionSpec as P

SPAN = 64


HIGH = lax.Precision.HIGHEST
MODEL_EPS = 1e-06
HEAD_EPS = 1e-05
GATE_SCALE = 16.0


def prefix(array, axis, join, neutral):
    place = lax.axis_index(axis)
    gathered = jax.tree.map(
        lambda a, kind: lax.all_gather(a.astype(kind), axis), array, (jnp.bfloat16, jnp.bfloat16)
    )
    state = jax.tree.map(lambda a, e: jnp.zeros_like(a) + jnp.asarray(e, a.dtype), array, neutral)

    def prefix_one(hop, state):
        return join(
            state,
            jax.tree.map(
                lambda a, own: lax.dynamic_index_in_dim(a, hop, 0, False).astype(own.dtype),
                gathered,
                array,
            ),
        )

    return lax.fori_loop(0, place, prefix_one, state)


def entering(array, axis, join, neutral):
    count = lax.axis_size(axis)
    place = lax.axis_index(axis)
    ahead = count - 1 - place
    gathered = jax.tree.map(
        lambda a, kind: lax.all_gather(a.astype(kind), axis),
        array,
        jax.tree.map(lambda a: jnp.bfloat16 if a.dtype == jnp.float32 else a.dtype, array),
    )
    state = jax.tree.map(lambda a, e: jnp.zeros_like(a) + jnp.asarray(e, a.dtype), array, neutral)

    def entering_one(hop, state):
        source = count - 1 - hop
        return join(
            state,
            jax.tree.map(
                lambda a, own: lax.dynamic_index_in_dim(a, source, 0, False).astype(own.dtype),
                gathered,
                array,
            ),
        )

    return lax.fori_loop(0, ahead, entering_one, state)


def from_behind(array, axis, by):
    peers = lax.axis_size(axis)
    pairs = [(i, i + by) for i in range(peers) if 0 <= i + by < peers]
    return lax.ppermute(array, axis, pairs)


def shortened(array):
    return jax.tree.map(lambda a: a.astype(jnp.bfloat16) if a.dtype == jnp.float32 else a, array)


def dot_plain(left, right):
    return jnp.dot(left, right, preferred_element_type=jnp.float32)


def dot_left(left, right):
    return lax.dot_general(
        left, right, (((0,), (0,)), ((), ())), preferred_element_type=jnp.float32
    )


def dot_right(left, right):
    return lax.dot_general(
        left, right, (((1,), (1,)), ((), ())), preferred_element_type=jnp.float32
    )


def norm_gain(field, gain, eps):
    return gain * field * lax.rsqrt(jnp.mean(field * field, axis=-1, keepdims=True) + eps)


def head_output(inner, out_gate, gain):
    return norm_gain(inner, gain, HEAD_EPS) * jax.nn.silu(out_gate)


def swiglu(gate_v, upper_v):
    return jax.nn.silu(gate_v) * upper_v


def carry_combine(earlier, later):
    return (earlier[0] * later[0], later[1] + later[0][:, None] * earlier[1])


def span_scan(queries, keys, values, decay, state):
    length = queries.shape[0]
    count = length // SPAN
    key_dim = queries.shape[1]
    causal = (jnp.arange(SPAN)[:, None] >= jnp.arange(SPAN)[None, :]).astype(queries.dtype)

    def one_block(carry, pieces):
        query_b, key_b, value_b, decay_b = pieces
        cumul = jnp.cumsum(decay_b, axis=0)
        middle_ref = cumul[SPAN // 2]
        scores = (
            jnp.dot(
                query_b * jnp.exp(cumul - middle_ref),
                (key_b * jnp.exp(middle_ref - cumul)).T,
                precision=HIGH,
            )
            * causal
        )
        local = jnp.dot(scores, value_b, precision=HIGH)
        carried = jnp.dot(query_b * jnp.exp(cumul), carry, precision=HIGH)
        last = cumul[-1]
        moved = jnp.dot((key_b * jnp.exp(last[None, :] - cumul)).T, value_b, precision=HIGH)
        return (jnp.exp(last)[:, None] * carry + moved, local + carried)

    pieces = (
        queries.reshape(count, SPAN, key_dim),
        keys.reshape(count, SPAN, key_dim),
        values.reshape(count, SPAN, values.shape[1]),
        decay.reshape(count, SPAN, key_dim),
    )
    state_end, outputs = lax.scan(jax.checkpoint(one_block), state, pieces)
    return (outputs.reshape(length, values.shape[1]), state_end)


def mixer_core(query_f, key_f, value_f, decay, state):
    return span_scan(query_f * query_f.shape[1] ** (-0.5), key_f, value_f, decay, state)


def feed_hidden(feed_in, gate_w, upper_w):
    gate_v = dot_plain(feed_in, gate_w)
    upper_v = dot_plain(feed_in, upper_w)
    return (gate_v, upper_v, swiglu(gate_v, upper_v).astype(jnp.bfloat16))


def layer_forward(hidden, weights):
    (
        query_w,
        key_w,
        value_w,
        outgate_w,
        output_w,
        down_w,
        up_w,
        bias_w,
        head_w,
        mixer_w,
        feed_w,
        gate_w,
        upper_w,
        lower_w,
    ) = weights
    normed = norm_gain(hidden, mixer_w.astype(jnp.float32), MODEL_EPS).astype(jnp.bfloat16)
    queries = dot_plain(normed, query_w).astype(jnp.bfloat16)
    keys = dot_plain(normed, key_w).astype(jnp.bfloat16)
    values = dot_plain(normed, value_w).astype(jnp.bfloat16)
    out_gate = dot_plain(normed, outgate_w)
    rank_part = dot_plain(normed, down_w)
    logits = jnp.dot(rank_part, up_w.astype(jnp.float32).T, precision=HIGH) + bias_w[:, 0].astype(
        jnp.float32
    )
    decay = jax.nn.log_sigmoid(logits) / GATE_SCALE
    query_f = queries.astype(jnp.float32)
    key_f = keys.astype(jnp.float32)
    value_f = values.astype(jnp.float32)
    zero_state = jnp.zeros((key_f.shape[1], value_f.shape[1]), jnp.float32)
    local_out, local_state = mixer_core(query_f, key_f, value_f, decay, zero_state)
    cumul_all = jnp.cumsum(decay, axis=0)
    through = jnp.exp(cumul_all[-1])
    identity = (jnp.ones_like(through), jnp.zeros_like(local_state))
    state_in = prefix((through, local_state), "seq", carry_combine, identity)[1]
    reach = query_f * query_f.shape[1] ** (-0.5) * jnp.exp(cumul_all)
    inner = local_out + jnp.dot(reach, state_in, precision=HIGH)
    gated = head_output(inner, out_gate, head_w.astype(jnp.float32)).astype(jnp.bfloat16)
    middle = hidden + lax.psum(dot_right(gated, output_w), "tensor")
    feed_in = norm_gain(middle, feed_w.astype(jnp.float32), MODEL_EPS).astype(jnp.bfloat16)
    gate_v, upper_v, hidden_ff = feed_hidden(feed_in, gate_w, upper_w)
    sent = (middle + lax.psum(dot_right(hidden_ff, lower_w), "tensor")).astype(jnp.bfloat16)
    kept = dict(
        hidden=hidden,
        normed=normed,
        queries=queries,
        keys=keys,
        values=values,
        out_gate=out_gate,
        rank_part=rank_part,
        logits=logits,
        decay=decay,
        state_in=state_in,
        inner=inner,
        gated=gated,
        middle=middle,
        feed_in=feed_in,
        gate_v=gate_v,
        upper_v=upper_v,
        hidden_ff=hidden_ff,
    )
    return (sent, kept)


def layer_backward(grad_out, kept, weights):
    (
        query_w,
        key_w,
        value_w,
        outgate_w,
        output_w,
        down_w,
        up_w,
        bias_w,
        head_w,
        mixer_w,
        feed_w,
        gate_w,
        upper_w,
        lower_w,
    ) = weights
    d_feed = grad_out.astype(jnp.bfloat16)
    d_hidden_ff = dot_plain(d_feed, lower_w)
    unused, swiglu_pull = jax.vjp(swiglu, kept["gate_v"], kept["upper_v"])
    d_gate_f, d_upper_f = swiglu_pull(d_hidden_ff)
    d_gate = d_gate_f.astype(jnp.bfloat16)
    d_upper = d_upper_f.astype(jnp.bfloat16)
    feed_part = dot_right(d_gate, gate_w) + dot_right(d_upper, upper_w)
    unused, feed_pull = jax.vjp(
        partial(norm_gain, eps=MODEL_EPS), kept["middle"], feed_w.astype(jnp.float32)
    )
    d_feed_in = lax.psum(feed_part.astype(jnp.bfloat16), "tensor").astype(jnp.float32)
    d_middle_norm, feed_gain_part = feed_pull(d_feed_in)
    d_middle = grad_out + d_middle_norm
    d_mixed = d_middle.astype(jnp.bfloat16)
    d_gated = dot_plain(d_mixed, output_w)
    unused, head_pull = jax.vjp(
        head_output, kept["inner"], kept["out_gate"], head_w.astype(jnp.float32)
    )
    d_inner, d_outgate_f, head_gain_part = head_pull(d_gated)
    d_outgate = d_outgate_f.astype(jnp.bfloat16)
    query_f = kept["queries"].astype(jnp.float32)
    key_f = kept["keys"].astype(jnp.float32)
    value_f = kept["values"].astype(jnp.float32)
    decay = kept["decay"]
    cumul_all = jnp.cumsum(decay, axis=0)
    through = jnp.exp(cumul_all[-1])
    reach = query_f * query_f.shape[1] ** (-0.5) * jnp.exp(cumul_all)
    pulled = jnp.dot(reach.T, d_inner, precision=HIGH)
    identity = (jnp.ones_like(through), jnp.zeros_like(pulled))
    state_grad = entering((through, pulled), "seq", carry_combine, identity)[1]
    unused, core_pull = jax.vjp(mixer_core, query_f, key_f, value_f, decay, kept["state_in"])
    d_query_f, d_key_f, d_value_f, d_decay, d_start = core_pull((d_inner, state_grad))
    d_logits = d_decay * jax.nn.sigmoid(-kept["logits"]) / GATE_SCALE
    rank_grad_part = jnp.dot(d_logits, up_w.astype(jnp.float32), precision=HIGH)
    d_query = d_query_f.astype(jnp.bfloat16)
    d_key = d_key_f.astype(jnp.bfloat16)
    d_value = d_value_f.astype(jnp.bfloat16)
    mixer_part = (
        dot_right(d_query, query_w)
        + dot_right(d_key, key_w)
        + dot_right(d_value, value_w)
        + dot_right(d_outgate, outgate_w)
    )
    unused, mixer_pull = jax.vjp(
        partial(norm_gain, eps=MODEL_EPS), kept["hidden"], mixer_w.astype(jnp.float32)
    )
    d_normed_sum, d_rank, head_gain_grad = (
        lax.psum(mixer_part.astype(jnp.bfloat16), "tensor").astype(jnp.float32),
        lax.psum(rank_grad_part.astype(jnp.bfloat16), "tensor").astype(jnp.float32),
        lax.psum(head_gain_part.astype(jnp.bfloat16), "tensor").astype(jnp.float32),
    )
    d_normed = d_normed_sum + jnp.dot(d_rank, down_w.astype(jnp.float32).T, precision=HIGH)
    d_hidden_norm, mixer_gain_grad = mixer_pull(d_normed)
    grad_in = d_middle + d_hidden_norm
    saved = dict(
        normed=kept["normed"],
        d_query=d_query,
        d_key=d_key,
        d_value=d_value,
        d_outgate=d_outgate,
        rank_part=kept["rank_part"],
        d_logits=d_logits,
        d_rank=d_rank,
        gated=kept["gated"],
        d_mixed=d_mixed,
        feed_in=kept["feed_in"],
        d_gate=d_gate,
        d_upper=d_upper,
        hidden_ff=kept["hidden_ff"],
        d_feed=d_feed,
        head_sum=head_gain_grad[None],
        mixer_sum=mixer_gain_grad[None],
        feed_gain_sum=feed_gain_part[None],
    )
    return (grad_in, saved)


def weight_grads(rows):
    query_grad = dot_left(rows["normed"], rows["d_query"])
    key_grad = dot_left(rows["normed"], rows["d_key"])
    value_grad = dot_left(rows["normed"], rows["d_value"])
    outgate_grad = dot_left(rows["normed"], rows["d_outgate"])
    output_grad = dot_left(rows["d_mixed"], rows["gated"])
    down_grad = jnp.dot(rows["normed"].astype(jnp.float32).T, rows["d_rank"], precision=HIGH)
    up_grad = jnp.dot(rows["d_logits"].T, rows["rank_part"], precision=HIGH)
    bias_grad = jnp.sum(rows["d_logits"], axis=0)[:, None]
    head_grad = jnp.sum(rows["head_sum"], axis=0)
    mixer_grad = jnp.sum(rows["mixer_sum"], axis=0)
    feed_norm_grad = jnp.sum(rows["feed_gain_sum"], axis=0)
    gate_grad = dot_left(rows["feed_in"], rows["d_gate"])
    upper_grad = dot_left(rows["feed_in"], rows["d_upper"])
    lower_grad = dot_left(rows["d_feed"], rows["hidden_ff"])
    return (
        query_grad[None],
        key_grad[None],
        value_grad[None],
        outgate_grad[None],
        output_grad[None],
        down_grad[None],
        up_grad[None],
        bias_grad[None],
        head_grad[None],
        mixer_grad[None],
        feed_norm_grad[None],
        gate_grad[None],
        upper_grad[None],
        lower_grad[None],
    )


def pick_steps(items, take_later, count):
    return jnp.where(take_later, jnp.stack(items[1:]), jnp.stack(items[:count]))


def shards(
    inputs,
    cotangent,
    query_proj,
    key_proj,
    value_proj,
    outgate_proj,
    output_proj,
    decay_down,
    decay_up,
    decay_bias,
    head_gain,
    mixer_gain,
    feed_gain,
    feed_gate,
    feed_up,
    feed_down,
):
    gathered = (
        lax.all_gather(query_proj, "seq", axis=1, tiled=True),
        lax.all_gather(key_proj, "seq", axis=1, tiled=True),
        lax.all_gather(value_proj, "seq", axis=1, tiled=True),
        lax.all_gather(outgate_proj, "seq", axis=1, tiled=True),
        lax.all_gather(output_proj, "seq", axis=1, tiled=True),
        lax.all_gather(decay_down, "seq", axis=1, tiled=True),
        lax.all_gather(decay_up, "seq", axis=1, tiled=True),
        lax.all_gather(decay_bias, "seq", axis=1, tiled=True),
        lax.all_gather(head_gain, "seq", axis=1, tiled=True),
        lax.all_gather(mixer_gain, "seq", axis=1, tiled=True),
        lax.all_gather(feed_gain, "seq", axis=1, tiled=True),
        lax.all_gather(feed_gate, "seq", axis=1, tiled=True),
        lax.all_gather(feed_up, "seq", axis=1, tiled=True),
        lax.all_gather(feed_down, "seq", axis=1, tiled=True),
    )
    layer_weights = tuple((piece[0] for piece in gathered))
    first_section = lax.axis_index("section") == 0
    micro = inputs.shape[0]
    received = jnp.zeros(inputs.shape[1:], jnp.bfloat16)
    kept_list = []
    outputs_list = []
    for step in range(micro + 1):
        own = inputs[min(step, micro - 1)].astype(jnp.float32)
        layer_in = jnp.where(first_section, own, received.astype(jnp.float32))
        sent, kept = layer_forward(layer_in, layer_weights)
        outputs_list.append(sent)
        kept_list.append(kept)
        if step < micro:
            received = from_behind(sent, "section", 1)
    grad_received = jnp.zeros(inputs.shape[1:], jnp.bfloat16)
    grads_list = []
    saved_list = []
    for step in range(micro + 1):
        own = cotangent[min(step, micro - 1)].astype(jnp.float32)
        grad_out = jnp.where(first_section, grad_received.astype(jnp.float32), own)
        kept = jax.tree.map(
            lambda early, late: jnp.where(first_section, early, late),
            kept_list[max(step - 1, 0)],
            kept_list[min(step + 1, micro)],
        )
        grad_in, saved = layer_backward(grad_out, kept, layer_weights)
        grads_list.append(grad_in)
        saved_list.append(saved)
        if step < micro:
            grad_received = from_behind(grad_in.astype(jnp.bfloat16), "section", -1)
    layer_outputs = pick_steps(outputs_list, jnp.logical_not(first_section), micro)[None]
    input_grads = pick_steps(grads_list, first_section, micro)[None]
    chosen = jax.tree.map(lambda *items: pick_steps(list(items), first_section, micro), *saved_list)
    rows = jax.tree.map(lambda item: item.reshape((-1,) + item.shape[2:]), chosen)
    summed = jax.tree.map(
        lambda part: part.astype(jnp.float32),
        lax.psum_scatter(shortened(weight_grads(rows)), "seq", scatter_dimension=1, tiled=True),
    )
    return (
        layer_outputs,
        input_grads,
        summed[0],
        summed[1],
        summed[2],
        summed[3],
        summed[4],
        summed[5],
        summed[6],
        summed[7],
        summed[8],
        summed[9],
        summed[10],
        summed[11],
        summed[12],
        summed[13],
    )


def solution(mesh):
    return jax.shard_map(
        shards,
        mesh=mesh,
        in_specs=(
            P(None, "seq", None),
            P(None, "seq", None),
            P("section", "seq", "tensor"),
            P("section", "seq", "tensor"),
            P("section", "seq", "tensor"),
            P("section", "seq", "tensor"),
            P("section", "seq", "tensor"),
            P("section", "seq", None),
            P("section", "seq", "tensor"),
            P("section", "seq", "tensor"),
            P("section", "seq"),
            P("section", "seq"),
            P("section", "seq"),
            P("section", "seq", "tensor"),
            P("section", "seq", "tensor"),
            P("section", "seq", "tensor"),
        ),
        out_specs=(
            P("section", None, "seq", None),
            P("section", None, "seq", None),
            P("section", "seq", "tensor"),
            P("section", "seq", "tensor"),
            P("section", "seq", "tensor"),
            P("section", "seq", "tensor"),
            P("section", "seq", "tensor"),
            P("section", "seq", None),
            P("section", "seq", "tensor"),
            P("section", "seq", "tensor"),
            P("section", "seq"),
            P("section", "seq"),
            P("section", "seq"),
            P("section", "seq", "tensor"),
            P("section", "seq", "tensor"),
            P("section", "seq", "tensor"),
        ),
        check_vma=False,
    )
```

profile of v0, /device:TPU:24, one launch (start us, length us, event | category | flops | bytes accessed | tf_op | source)
XLA Modules:
  0.0 3019.7 jit_solution(4373467443858688506)
XLA Ops:
  9.5 10.8 all_gather.123
  32.2 13.7 all_gather.125
  46.0 14.1 all_gather.124
  74.0 40.1 %all-gather.35.cloned.1.call-done = bf16[1,2048,512]{2,1,0:T(8,128)(2,1)} async-done(((bf16[1,512,512]{2,1,0:T(8,128)(2,1)}), bf16[1,2048,512]{2,1,0:T(8,128)(2,1)}) %all-gather.35.cloned.1.call-update) | async-done | bytes 2097168 | tf_op jit(solution)/shard_map/all_gather | solution.py:365
  118.2 31.7 %while.312 = (s32[]{:T(128)}, f32[256,512]{1,0:T(8,128)}, f32[4,64,512]{2,1,0:T(8,128)}, f32[4,64,256]{2,1,0:T(8,128)}, f32[4,64,256]{2,1,0:T(8,128)}, /*index=5...) while((s32[]{:T(128)}, f32[256,512]{1,0:T(8,128)}, ...), condition=%wide.region_3.4_spmd.clone, body=%wide.region_1.3_spmd.clone.sunk | while | flops 240787456 | bytes 3061890 | solution.py:134
  160.0 9.0 all-gather.8
  169.0 8.4 all_gather.122
  189.2 36.4 %all-gather.39.cloned.1.call-done = bf16[1,2048,512]{2,1,0:T(8,128)(2,1)} async-done(((bf16[1,512,512]{2,1,0:T(8,128)(2,1)}), bf16[1,2048,512]{2,1,0:T(8,128)(2,1)}) %all-gather.39.cloned.1.call-update) | async-done | bytes 2097168 | tf_op jit(solution)/shard_map/all_gather | solution.py:366
  228.8 42.8 %all-gather.41.cloned.1.call-done = bf16[1,2048,512]{2,1,0:T(8,128)(2,1)} async-done(((bf16[1,512,512]{2,1,0:T(8,128)(2,1)}), bf16[1,2048,512]{2,1,0:T(8,128)(2,1)}) %all-gather.41.cloned.1.call-update) | async-done | bytes 2097168 | tf_op jit(solution)/shard_map/all_gather | solution.py:367
  277.6 11.1 all_gather.135
  288.6 57.5 %all-reduce.27.cloned.1.call-done = f32[256,2048]{1,0:T(8,128)} async-done(((f32[256,2048]{1,0:T(8,128)}), f32[256,2048]{1,0:T(8,128)}) %all-reduce.27.cloned.1.call-update) | async-done | bytes 2097168 | tf_op jit(solution)/shard_map/psum | solution.py:187
  349.4 102.2 %all-gather.43.cloned.1.call-done = bf16[1,2048,1408]{2,1,0:T(8,128)(2,1)} async-done(((bf16[1,512,1408]{2,1,0:T(8,128)(2,1)}), bf16[1,2048,1408]{2,1,0:T(8,128)(2,1)}) %all-gather.43.cloned.1.call-update) | async-done | bytes 5767184 | tf_op jit(solution)/shard_map/all_gather | solution.py:374
  457.7 100.5 %all-gather.45.cloned.1.call-done = bf16[1,2048,1408]{2,1,0:T(8,128)(2,1)} async-done(((bf16[1,512,1408]{2,1,0:T(8,128)(2,1)}), bf16[1,2048,1408]{2,1,0:T(8,128)(2,1)}) %all-gather.45.cloned.1.call-update) | async-done | bytes 5767184 | tf_op jit(solution)/shard_map/all_gather | solution.py:375
  565.1 99.7 %all-gather.47.cloned.1.call-done = bf16[1,2048,1408]{2,1,0:T(8,128)(2,1)} async-done(((bf16[1,512,1408]{2,1,0:T(8,128)(2,1)}), bf16[1,2048,1408]{2,1,0:T(8,128)(2,1)}) %all-gather.47.cloned.1.call-update) | async-done | bytes 5767184 | tf_op jit(solution)/shard_map/all_gather | solution.py:376
  670.9 71.0 %all-reduce.29.cloned.1.call-done = f32[256,2048]{1,0:T(8,128)} async-done(((f32[256,2048]{1,0:T(8,128)}), f32[256,2048]{1,0:T(8,128)}) %all-reduce.29.cloned.1.call-update) | async-done | bytes 2097168 | tf_op jit(solution)/shard_map/psum | solution.py:190
  770.0 31.7 %while.313 = (s32[]{:T(128)}, f32[256,512]{1,0:T(8,128)}, f32[4,64,512]{2,1,0:T(8,128)}, f32[4,64,256]{2,1,0:T(8,128)}, f32[4,64,256]{2,1,0:T(8,128)}, /*index=5...) while((s32[]{:T(128)}, f32[256,512]{1,0:T(8,128)}, ...), condition=%wide.region_15.16_spmd.clone, body=%wide.region_13.15_spmd.clone.sunk | while | flops 240787456 | bytes 3061890 | solution.py:134
  820.2 10.1 all-gather.51.cloned.1.call-done
  865.0 51.0 %all-reduce.31.cloned.1.call-done = f32[256,2048]{1,0:T(8,128)} async-done(((f32[256,2048]{1,0:T(8,128)}), f32[256,2048]{1,0:T(8,128)}) %all-reduce.31.cloned.1.call-update) | async-done | bytes 2097168 | tf_op jit(solution)/shard_map/psum | solution.py:187
  950.9 42.6 %all-reduce.43.cloned.1.call-done = bf16[256,2048]{1,0:T(8,128)(2,1)} async-done(((bf16[256,2048]{1,0:T(8,128)(2,1)}), bf16[256,2048]{1,0:T(8,128)(2,1)}) %all-reduce.43.cloned.1.call-update) | async-done | bytes 1048592 | tf_op jit(solution)/shard_map/psum | solution.py:240
  1004.8 13.5 while.301
  1018.3 48.7 %all-reduce.33.cloned.1.call-done = f32[256,2048]{1,0:T(8,128)} async-done(((f32[256,2048]{1,0:T(8,128)}), f32[256,2048]{1,0:T(8,128)}) %all-reduce.33.cloned.1.call-update) | async-done | bytes 2097168 | tf_op jit(solution)/shard_map/psum | solution.py:190
  1072.7 22.3 all-gather.57.cloned.1.call-done
  1096.5 40.9 %while.308 = (s32[]{:T(128)}, f32[256,512]{1,0:T(8,128)S(1)}, f32[4,64,256]{2,1,0:T(8,128)}, bf16[4,64,256]{2,1,0:T(8,128)(2,1)}, bf16[4,64,512]{2,1,0:T(8,128)(...) while((s32[]{:T(128)}, f32[256,512]{1,0:T(8,128)S(1)}, ...), condition=%wide.region_67.68_spmd.clone, body=%wide.region_60.67_spmd.clone.sunk | while | flops 494190592 | bytes 10729725 | solution.py:134
  1147.7 10.6 psum.178
  1158.4 41.4 %all-reduce.45.cloned.1.call-done = bf16[256,2048]{1,0:T(8,128)(2,1)} async-done(((bf16[256,2048]{1,0:T(8,128)(2,1)}), bf16[256,2048]{1,0:T(8,128)(2,1)}) %all-reduce.45.cloned.1.call-update) | async-done | bytes 1048592 | tf_op jit(solution)/shard_map/psum | solution.py:277
  1222.8 31.7 %while.314 = (s32[]{:T(128)}, f32[256,512]{1,0:T(8,128)}, f32[4,64,512]{2,1,0:T(8,128)}, f32[4,64,256]{2,1,0:T(8,128)}, f32[4,64,256]{2,1,0:T(8,128)}, /*index=5...) while((s32[]{:T(128)}, f32[256,512]{1,0:T(8,128)}, ...), condition=%wide.region_27.28_spmd.clone, body=%wide.region_25.27_spmd.clone.sunk | while | flops 240787456 | bytes 3061890 | solution.py:134
  1273.0 10.1 all-gather.53.cloned.1.call-done
  1298.6 70.4 %all-reduce.35.cloned.1.call-done = f32[256,2048]{1,0:T(8,128)} async-done(((f32[256,2048]{1,0:T(8,128)}), f32[256,2048]{1,0:T(8,128)}) %all-reduce.35.cloned.1.call-update) | async-done | bytes 2097168 | tf_op jit(solution)/shard_map/psum | solution.py:187
  1390.1 69.8 %all-reduce.37.cloned.1.call-done = f32[256,2048]{1,0:T(8,128)} async-done(((f32[256,2048]{1,0:T(8,128)}), f32[256,2048]{1,0:T(8,128)}) %all-reduce.37.cloned.1.call-update) | async-done | bytes 2097168 | tf_op jit(solution)/shard_map/psum | solution.py:190
  1501.6 41.9 %all-reduce.47.cloned.1.call-done = bf16[256,2048]{1,0:T(8,128)(2,1)} async-done(((bf16[256,2048]{1,0:T(8,128)(2,1)}), bf16[256,2048]{1,0:T(8,128)(2,1)}) %all-reduce.47.cloned.1.call-update) | async-done | bytes 1048592 | tf_op jit(solution)/shard_map/psum | solution.py:240
  1555.1 10.4 while.303
  1565.6 15.9 all-gather.59.cloned.1.call-done
  1583.2 43.1 %while.309 = (s32[]{:T(128)}, f32[256,512]{1,0:T(8,128)S(1)}, f32[4,64,256]{2,1,0:T(8,128)}, bf16[4,64,256]{2,1,0:T(8,128)(2,1)}, bf16[4,64,512]{2,1,0:T(8,128)(...) while((s32[]{:T(128)}, f32[256,512]{1,0:T(8,128)S(1)}, ...), condition=%wide.region_91.92_spmd.clone, body=%wide.region_84.91_spmd.clone.sunk | while | flops 494190592 | bytes 10733849 | solution.py:134
  1636.7 10.8 psum.181
  1647.5 41.3 %all-reduce.49.cloned.1.call-done = bf16[256,2048]{1,0:T(8,128)(2,1)} async-done(((bf16[256,2048]{1,0:T(8,128)(2,1)}), bf16[256,2048]{1,0:T(8,128)(2,1)}) %all-reduce.49.cloned.1.call-update) | async-done | bytes 1048592 | tf_op jit(solution)/shard_map/psum | solution.py:277
  1714.5 31.7 %while.315 = (s32[]{:T(128)}, f32[256,512]{1,0:T(8,128)}, f32[4,64,512]{2,1,0:T(8,128)}, f32[4,64,256]{2,1,0:T(8,128)}, f32[4,64,256]{2,1,0:T(8,128)}, /*index=5...) while((s32[]{:T(128)}, f32[256,512]{1,0:T(8,128)}, ...), condition=%wide.region_39.40_spmd.clone, body=%wide.region_37.39_spmd.clone.sunk | while | flops 240787456 | bytes 3061890 | solution.py:134
  1760.1 14.6 all-gather.55.cloned.1.call-done
  1804.3 55.9 %all-reduce.39.cloned.1.call-done = f32[256,2048]{1,0:T(8,128)} async-done(((f32[256,2048]{1,0:T(8,128)}), f32[256,2048]{1,0:T(8,128)}) %all-reduce.39.cloned.1.call-update) | async-done | bytes 2097168 | tf_op jit(solution)/shard_map/psum | solution.py:187
  1902.2 53.7 %all-reduce.41.cloned.1.call-done = f32[256,2048]{1,0:T(8,128)} async-done(((f32[256,2048]{1,0:T(8,128)}), f32[256,2048]{1,0:T(8,128)}) %all-reduce.41.cloned.1.call-update) | async-done | bytes 2097168 | tf_op jit(solution)/shard_map/psum | solution.py:190
  1960.7 50.8 %all-reduce.51.cloned.1.call-done = bf16[256,2048]{1,0:T(8,128)(2,1)} async-done(((bf16[256,2048]{1,0:T(8,128)(2,1)}), bf16[256,2048]{1,0:T(8,128)(2,1)}) %all-reduce.51.cloned.1.call-update) | async-done | bytes 1048592 | tf_op jit(solution)/shard_map/psum | solution.py:240
  2026.3 10.6 while.305
  2036.9 14.4 all-gather.61.cloned.1.call-done
  2052.8 43.3 %while.310 = (s32[]{:T(128)}, f32[256,512]{1,0:T(8,128)S(1)}, f32[4,64,256]{2,1,0:T(8,128)}, bf16[4,64,256]{2,1,0:T(8,128)(2,1)}, bf16[4,64,512]{2,1,0:T(8,128)(...) while((s32[]{:T(128)}, f32[256,512]{1,0:T(8,128)S(1)}, ...), condition=%wide.region_115.116_spmd.clone, body=%wide.region_108.115_spmd.clone.sunk | while | flops 494190592 | bytes 10733849 | solution.py:134
  2105.9 10.5 psum.184
  2116.4 42.1 %all-reduce.53.cloned.1.call-done = bf16[256,2048]{1,0:T(8,128)(2,1)} async-done(((bf16[256,2048]{1,0:T(8,128)(2,1)}), bf16[256,2048]{1,0:T(8,128)(2,1)}) %all-reduce.53.cloned.1.call-update) | async-done | bytes 1048592 | tf_op jit(solution)/shard_map/psum | solution.py:277
  2194.1 41.6 %all-reduce.55.cloned.1.call-done = bf16[256,2048]{1,0:T(8,128)(2,1)} async-done(((bf16[256,2048]{1,0:T(8,128)(2,1)}), bf16[256,2048]{1,0:T(8,128)(2,1)}) %all-reduce.55.cloned.1.call-update) | async-done | bytes 1048592 | tf_op jit(solution)/shard_map/psum | solution.py:240
  2250.6 13.5 while.307
  2264.1 11.5 all-gather.63.cloned.1.call-done
  2277.3 38.7 %while.311 = (s32[]{:T(128)}, f32[256,512]{1,0:T(8,128)S(1)}, f32[4,64,256]{2,1,0:T(8,128)}, bf16[4,64,256]{2,1,0:T(8,128)(2,1)S(1)}, bf16[4,64,512]{2,1,0:T(8,1...) while((s32[]{:T(128)}, f32[256,512]{1,0:T(8,128)S(1)}, ...), condition=%wide.region_139.140_spmd.clone, body=%wide.region_132.139_spmd.clone.sunk | while | flops 494190592 | bytes 9681093 | solution.py:134
  2330.0 16.2 all-reduce.9
  2357.3 21.3 all-reduce.57.cloned.1.call-done
  2415.1 10.1 fusion.260
  2425.3 12.0 fusion.261
  2440.0 9.9 fusion.262
  2460.7 17.4 reduce-scatter.35.cloned.1.call-done
  2487.2 13.5 reduce-scatter.49.cloned.1.call-done
  2502.3 27.3 reduce-scatter.25.cloned.1.call-done
  2531.3 27.0 reduce-scatter.27.cloned.1.call-done
  2560.1 43.5 %reduce-scatter.31.cloned.1.call-done = bf16[1,512,512]{2,1,0:T(8,128)(2,1)} async-done(((bf16[1,2048,512]{2,1,0:T(8,128)(2,1)}), bf16[1,512,512]{2,1,0:T(8,128)(2,1)}) %reduce-scatter.31.cloned.1.call-update) | async-done | bytes 524304 | tf_op jit(solution)/shard_map/reduce_scatter | solution.py:414
  2605.8 43.5 %reduce-scatter.33.cloned.1.call-done = bf16[1,512,512]{2,1,0:T(8,128)(2,1)} async-done(((bf16[1,2048,512]{2,1,0:T(8,128)(2,1)}), bf16[1,512,512]{2,1,0:T(8,128)(2,1)}) %reduce-scatter.33.cloned.1.call-update) | async-done | bytes 524304 | tf_op jit(solution)/shard_map/reduce_scatter | solution.py:414
  2651.5 43.2 %reduce-scatter.29.cloned.1.call-done = bf16[1,512,512]{2,1,0:T(8,128)(2,1)} async-done(((bf16[1,2048,512]{2,1,0:T(8,128)(2,1)}), bf16[1,512,512]{2,1,0:T(8,128)(2,1)}) %reduce-scatter.29.cloned.1.call-update) | async-done | bytes 524304 | tf_op jit(solution)/shard_map/reduce_scatter | solution.py:414
  2696.8 103.0 %reduce-scatter.37.cloned.1.call-done = bf16[1,512,1408]{2,1,0:T(8,128)(2,1)} async-done(((bf16[1,2048,1408]{2,1,0:T(8,128)(2,1)}), bf16[1,512,1408]{2,1,0:T(8,128)(2,1)}) %reduce-scatter.37.cloned.1.call-update) | async-done | bytes 1441808 | tf_op jit(solution)/shard_map/reduce_scatter | solution.py:414
  2802.9 101.9 %reduce-scatter.39.cloned.1.call-done = bf16[1,512,1408]{2,1,0:T(8,128)(2,1)} async-done(((bf16[1,2048,1408]{2,1,0:T(8,128)(2,1)}), bf16[1,512,1408]{2,1,0:T(8,128)(2,1)}) %reduce-scatter.39.cloned.1.call-update) | async-done | bytes 1441808 | tf_op jit(solution)/shard_map/reduce_scatter | solution.py:414
  2908.0 101.9 %reduce-scatter.41.cloned.1.call-done = bf16[1,512,1408]{2,1,0:T(8,128)(2,1)} async-done(((bf16[1,2048,1408]{2,1,0:T(8,128)(2,1)}), bf16[1,512,1408]{2,1,0:T(8,128)(2,1)}) %reduce-scatter.41.cloned.1.call-update) | async-done | bytes 1441808 | tf_op jit(solution)/shard_map/reduce_scatter | solution.py:414
  (1825 shorter events, 1032.4 us)
Async XLA Ops:
  7.2 61.2 %all-gather.33.cloned.1.call-start = ((), (), s32[]{:S(2)}) async-start(), calls=%async_computation.14 | async-start | bytes 1310720 | tf_op jit(solution)/shard_map/all_gather | solution.py:364
  7.9 63.6 %all-gather.37.cloned.1.call-start = ((), (), s32[]{:S(2)}) async-start(), calls=%async_computation.16 | async-start | bytes 1310720 | tf_op jit(solution)/shard_map/all_gather | solution.py:363
  8.7 105.4 %all-gather.35.cloned.1.call-start = ((), (), s32[]{:S(2)}) async-start(), calls=%async_computation.15 | async-start | bytes 2621440 | tf_op jit(solution)/shard_map/all_gather | solution.py:365
  9.4 170.0 %all-gather.49.cloned.1.call-start = ((), (), s32[]{:S(2)}) async-start(), calls=%async_computation.47 | async-start | bytes 1310720 | tf_op jit(solution)/shard_map/all_gather | solution.py:20
  31.5 725.1 %copy-start.263 = (f32[256]{0:T(256)}, f32[256]{0:T(256)S(1)}, u32[]{:S(2)}) copy-start(f32[256]{0:T(256)S(1)} %convert_element_type.1235) | copy-start | bytes 3076
  46.0 1163.5 %copy-start.203 = (bf16[1,256,16]{1,2,0:T(8,128)(2,1)}, bf16[1,256,16]{1,2,0:T(8,128)(2,1)S(1)}, u32[]{:S(2)}) copy-start(bf16[1,256,16]{1,2,0:T(8,128)(2,1)S(1)} %copy.332) | copy-start | bytes 24580
  60.1 2098.4 %copy-start.138 = (bf16[1,2048,16]{1,2,0:T(8,128)(2,1)}, bf16[1,2048,16]{1,2,0:T(8,128)(2,1)S(1)}, u32[]{:S(2)}) copy-start(bf16[1,2048,16]{1,2,0:T(8,128)(2,1)S(1)} %all_gather.124) | copy-start | bytes 196612
  61.7 690.5 %copy-start.255 = (f32[256]{0:T(256)}, f32[256]{0:T(256)S(1)}, u32[]{:S(2)}) copy-start(f32[256]{0:T(256)S(1)} %add_rsqrt_fusion.11) | copy-start | bytes 3076
  151.8 73.8 %all-gather.39.cloned.1.call-start = ((), (), s32[]{:S(2)}) async-start(), calls=%async_computation.17 | async-start | bytes 2621440 | tf_op jit(solution)/shard_map/all_gather | solution.py:366
  152.4 119.3 %all-gather.41.cloned.1.call-start = ((), (), s32[]{:S(2)}) async-start(), calls=%async_computation.18 | async-start | bytes 2621440 | tf_op jit(solution)/shard_map/all_gather | solution.py:367
  152.9 193.2 %all-reduce.27.cloned.1.call-start = ((), (), s32[]{:S(2)}) async-start(), calls=%async_computation.19 | async-start | bytes 4194304 | tf_op jit(solution)/shard_map/psum | solution.py:187
  177.4 1116.5 %copy-start.218 = (f32[1,512]{1,0:T(1,128)}, f32[1,512]{1,0:T(1,128)S(1)}, u32[]{:S(2)}) copy-start(f32[1,512]{1,0:T(1,128)S(1)} %mul.2555) | copy-start | bytes 6148
  275.4 176.1 %all-gather.43.cloned.1.call-start = ((), (), s32[]{:S(2)}) async-start(), calls=%async_computation.20 | async-start | bytes 7208960 | tf_op jit(solution)/shard_map/all_gather | solution.py:374
  276.2 282.1 %all-gather.45.cloned.1.call-start = ((), (), s32[]{:S(2)}) async-start(), calls=%async_computation.21 | async-start | bytes 7208960 | tf_op jit(solution)/shard_map/all_gather | solution.py:375
  276.9 387.9 %all-gather.47.cloned.1.call-start = ((), (), s32[]{:S(2)}) async-start(), calls=%async_computation.22 | async-start | bytes 7208960 | tf_op jit(solution)/shard_map/all_gather | solution.py:376
  277.5 464.4 %all-reduce.29.cloned.1.call-start = ((), (), s32[]{:S(2)}) async-start(), calls=%async_computation.23 | async-start | bytes 4194304 | tf_op jit(solution)/shard_map/psum | solution.py:190
  349.4 571.2 %copy-start.247 = (f32[256]{0:T(256)}, f32[256]{0:T(256)S(1)}, u32[]{:S(2)}) copy-start(f32[256]{0:T(256)S(1)} %add_rsqrt_fusion.9) | copy-start | bytes 3076
  670.8 159.5 %all-gather.51.cloned.1.call-start = ((), (), s32[]{:S(2)}) async-start(), calls=%async_computation.48 | async-start | bytes 1310720 | tf_op jit(solution)/shard_map/all_gather | solution.py:20
  745.3 4.3 collective-permute-start
  803.5 112.5 %all-reduce.31.cloned.1.call-start = ((), (), s32[]{:S(2)}) async-start(), calls=%async_computation.24 | async-start | bytes 4194304 | tf_op jit(solution)/shard_map/psum | solution.py:187
  845.3 148.2 %all-reduce.43.cloned.1.call-start = ((), (), s32[]{:S(2)}) async-start(), calls=%async_computation.30 | async-start | bytes 2097152 | tf_op jit(solution)/shard_map/psum | solution.py:240
  940.8 126.2 %all-reduce.33.cloned.1.call-start = ((), (), s32[]{:S(2)}) async-start(), calls=%async_computation.25 | async-start | bytes 4194304 | tf_op jit(solution)/shard_map/psum | solution.py:190
  950.8 144.1 %all-gather.57.cloned.1.call-start = ((), (), s32[]{:S(2)}) async-start(), calls=%async_computation.51 | async-start | bytes 1310720 | tf_op jit(solution)/shard_map/all_gather | solution.py:42
  1003.1 196.7 %all-reduce.45.cloned.1.call-start = ((), (), s32[]{:S(2)}) async-start(), calls=%async_computation.31 | async-start | bytes 2097152 | tf_op jit(solution)/shard_map/psum | solution.py:277
  1004.8 62.2 %copy-start.8 = (f32[256,2048]{1,0:T(8,128)S(1)}, f32[256,2048]{1,0:T(8,128)}, u32[]{:S(2)}) copy-start(f32[256,2048]{1,0:T(8,128)} %copy-done.7) | copy-start | bytes 6291460
  1069.8 88.6 %collective-permute-start.1 = (bf16[256,2048]{1,0:T(8,128)(2,1)}, bf16[256,2048]{1,0:T(8,128)(2,1)}, u32[]{:S(2)}, u32[]{:S(2)}) collective-permute-start(bf16[256,2048]{1,0:T(8,128)(2,1)} %add_convert_fusion.2), channel_id=1, source_target_pairs={{0,16},{1,17},{2,18},{3,19},{4,20},{5,21},{6,22},{7,23},{8,24},{9,... | collective-permute-start | bytes 3145736 | tf_op jit(solution)/shard_map/ppermute | solution.py:65
  1142.2 57.6 %copy-start.1 = (bf16[3,256,2048]{2,1,0:T(8,128)(2,1)S(1)}, bf16[3,256,2048]{2,1,0:T(8,128)(2,1)}, u32[]{:S(2)}) copy-start(bf16[3,256,2048]{2,1,0:T(8,128)(2,1)} %param.56) | copy-start | bytes 9437188
  1143.9 139.2 %all-gather.53.cloned.1.call-start = ((), (), s32[]{:S(2)}) async-start(), calls=%async_computation.49 | async-start | bytes 1310720 | tf_op jit(solution)/shard_map/all_gather | solution.py:20
  1158.4 46.7 %copy-start.237 = (bf16[256,16]{0,1:T(8,128)(2,1)}, bf16[256,16]{0,1:T(8,128)(2,1)S(1)}, u32[]{:S(2)}) copy-start(bf16[256,16]{0,1:T(8,128)(2,1)S(1)} %psum.178) | copy-start | bytes 24580
  1256.4 112.7 %all-reduce.35.cloned.1.call-start = ((), (), s32[]{:S(2)}) async-start(), calls=%async_computation.26 | async-start | bytes 4194304 | tf_op jit(solution)/shard_map/psum | solution.py:187
  1298.4 161.5 %all-reduce.37.cloned.1.call-start = ((), (), s32[]{:S(2)}) async-start(), calls=%async_computation.27 | async-start | bytes 4194304 | tf_op jit(solution)/shard_map/psum | solution.py:190
  1390.1 153.4 %all-reduce.47.cloned.1.call-start = ((), (), s32[]{:S(2)}) async-start(), calls=%async_computation.32 | async-start | bytes 2097152 | tf_op jit(solution)/shard_map/psum | solution.py:240
  1462.5 4.0 collective-permute-start.2
  1471.9 4.8 collective-permute-start.3
  1490.8 90.7 %all-gather.59.cloned.1.call-start = ((), (), s32[]{:S(2)}) async-start(), calls=%async_computation.52 | async-start | bytes 1310720 | tf_op jit(solution)/shard_map/all_gather | solution.py:42
  1554.8 134.0 %all-reduce.49.cloned.1.call-start = ((), (), s32[]{:S(2)}) async-start(), calls=%async_computation.33 | async-start | bytes 2097152 | tf_op jit(solution)/shard_map/psum | solution.py:277
  1631.2 57.6 %copy-start.2 = (bf16[3,256,2048]{2,1,0:T(8,128)(2,1)S(1)}, bf16[3,256,2048]{2,1,0:T(8,128)(2,1)}, u32[]{:S(2)}) copy-start(bf16[3,256,2048]{2,1,0:T(8,128)(2,1)} %param.56) | copy-start | bytes 9437188
  1632.9 141.7 %all-gather.55.cloned.1.call-start = ((), (), s32[]{:S(2)}) async-start(), calls=%async_computation.50 | async-start | bytes 1310720 | tf_op jit(solution)/shard_map/all_gather | solution.py:20
  1647.5 46.8 %copy-start.239 = (bf16[256,16]{0,1:T(8,128)(2,1)}, bf16[256,16]{0,1:T(8,128)(2,1)S(1)}, u32[]{:S(2)}) copy-start(bf16[256,16]{0,1:T(8,128)(2,1)S(1)} %psum.181) | copy-start | bytes 24580
  1748.0 112.2 %all-reduce.39.cloned.1.call-start = ((), (), s32[]{:S(2)}) async-start(), calls=%async_computation.28 | async-start | bytes 4194304 | tf_op jit(solution)/shard_map/psum | solution.py:187
  1789.4 166.5 %all-reduce.41.cloned.1.call-start = ((), (), s32[]{:S(2)}) async-start(), calls=%async_computation.29 | async-start | bytes 4194304 | tf_op jit(solution)/shard_map/psum | solution.py:190
  1871.0 13.4 collective-permute-start.4
  1884.4 127.1 %all-reduce.51.cloned.1.call-start = ((), (), s32[]{:S(2)}) async-start(), calls=%async_computation.34 | async-start | bytes 2097152 | tf_op jit(solution)/shard_map/psum | solution.py:240
  1901.8 149.5 %all-gather.61.cloned.1.call-start = ((), (), s32[]{:S(2)}) async-start(), calls=%async_computation.53 | async-start | bytes 1310720 | tf_op jit(solution)/shard_map/all_gather | solution.py:42
  2024.6 133.9 %all-reduce.53.cloned.1.call-start = ((), (), s32[]{:S(2)}) async-start(), calls=%async_computation.35 | async-start | bytes 2097152 | tf_op jit(solution)/shard_map/psum | solution.py:277
  2102.7 133.0 %all-reduce.55.cloned.1.call-start = ((), (), s32[]{:S(2)}) async-start(), calls=%async_computation.36 | async-start | bytes 2097152 | tf_op jit(solution)/shard_map/psum | solution.py:240
  2105.7 56.3 %copy-start.119 = (f32[256,256]{1,0:T(8,128)}, f32[256,256]{1,0:T(8,128)S(1)}, u32[]{:S(2)}) copy-start(f32[256,256]{1,0:T(8,128)S(1)} %fusion.615) | copy-start | bytes 786436
  2164.3 4.8 collective-permute-start.5
  2182.8 92.8 %all-gather.63.cloned.1.call-start = ((), (), s32[]{:S(2)}) async-start(), calls=%async_computation.54 | async-start | bytes 1310720 | tf_op jit(solution)/shard_map/all_gather | solution.py:42
  2248.9 129.7 %all-reduce.57.cloned.1.call-start = ((), (), s32[]{:S(2)}) async-start(), calls=%async_computation.37 | async-start | bytes 2097152 | tf_op jit(solution)/shard_map/psum | solution.py:277
  2322.5 132.2 %reduce-scatter.51.cloned.1.call-start = ((), (), s32[]{:S(2)}) async-start(), calls=%async_computation.59 | async-start | bytes 655360
  2329.5 126.8 %reduce-scatter.45.cloned.1.call-start = ((), (), s32[]{:S(2)}) async-start(), calls=%async_computation.56 | async-start | bytes 81920
  2347.9 110.0 %reduce-scatter.47.cloned.1.call-start = ((), (), s32[]{:S(2)}) async-start(), calls=%async_computation.57 | async-start | bytes 163840
  2348.8 110.5 %reduce-scatter.43.cloned.1.call-start = ((), (), s32[]{:S(2)}) async-start(), calls=%async_computation.55 | async-start | bytes 81920
  2353.2 124.9 %reduce-scatter.35.cloned.1.call-start = ((), (), s32[]{:S(2)}) async-start(), calls=%async_computation.43 | async-start | bytes 81920 | tf_op jit(solution)/shard_map/reduce_scatter | solution.py:414
  2357.2 143.5 %reduce-scatter.49.cloned.1.call-start = ((), (), s32[]{:S(2)}) async-start(), calls=%async_computation.58 | async-start | bytes 655360
  2384.8 144.8 %reduce-scatter.25.cloned.1.call-start = ((), (), s32[]{:S(2)}) async-start(), calls=%async_computation.38 | async-start | bytes 1310720 | tf_op jit(solution)/shard_map/reduce_scatter | solution.py:414
  2389.2 169.2 %reduce-scatter.27.cloned.1.call-start = ((), (), s32[]{:S(2)}) async-start(), calls=%async_computation.39 | async-start | bytes 1310720 | tf_op jit(solution)/shard_map/reduce_scatter | solution.py:414
  2393.4 210.3 %reduce-scatter.31.cloned.1.call-start = ((), (), s32[]{:S(2)}) async-start(), calls=%async_computation.41 | async-start | bytes 2621440 | tf_op jit(solution)/shard_map/reduce_scatter | solution.py:414
  2398.9 250.4 %reduce-scatter.33.cloned.1.call-start = ((), (), s32[]{:S(2)}) async-start(), calls=%async_computation.42 | async-start | bytes 2621440 | tf_op jit(solution)/shard_map/reduce_scatter | solution.py:414
  2406.7 288.0 %reduce-scatter.29.cloned.1.call-start = ((), (), s32[]{:S(2)}) async-start(), calls=%async_computation.40 | async-start | bytes 2621440 | tf_op jit(solution)/shard_map/reduce_scatter | solution.py:414
  2412.2 387.6 %reduce-scatter.37.cloned.1.call-start = ((), (), s32[]{:S(2)}) async-start(), calls=%async_computation.44 | async-start | bytes 7208960 | tf_op jit(solution)/shard_map/reduce_scatter | solution.py:414
  2425.2 479.6 %reduce-scatter.39.cloned.1.call-start = ((), (), s32[]{:S(2)}) async-start(), calls=%async_computation.45 | async-start | bytes 7208960 | tf_op jit(solution)/shard_map/reduce_scatter | solution.py:414
  2437.2 572.6 %reduce-scatter.41.cloned.1.call-start = ((), (), s32[]{:S(2)}) async-start(), calls=%async_computation.46 | async-start | bytes 7208960 | tf_op jit(solution)/shard_map/reduce_scatter | solution.py:414
  (320 other events, 1825.2 us)
Sparse Core Ops, SparseCore 0:
  9.6 28.3 all-gather.32
  39.5 28.1 all-gather.36
  69.3 44.7 all-gather.34
  151.9 27.4 all-gather.48
  180.8 44.6 all-gather.38
  226.9 44.6 all-gather.40
  275.5 70.5 all-reduce.26
  347.8 103.7 all-gather.42
  453.2 104.9 all-gather.44
  559.7 104.9 all-gather.46
  670.9 70.9 all-reduce.28
  803.7 26.5 all-gather.50
  845.4 70.5 all-reduce.30
  940.9 52.5 all-reduce.42
  997.3 69.6 all-reduce.32
  1068.4 26.4 all-gather.56
  1144.0 55.7 all-reduce.44
  1256.5 26.5 all-gather.52
  1298.5 70.5 all-reduce.34
  1390.2 69.6 all-reduce.36
  1490.9 52.5 all-reduce.46
  1554.9 26.4 all-gather.58
  1633.0 55.7 all-reduce.48
  1748.1 26.5 all-gather.54
  1789.6 70.5 all-reduce.38
  1884.5 71.4 all-reduce.40
  1958.8 52.5 all-reduce.50
  2024.7 26.4 all-gather.60
  2102.9 55.6 all-reduce.52
  2182.9 52.7 all-reduce.54
  2249.1 26.4 all-gather.62
  2322.7 55.9 all-reduce.56
  2381.3 18.6 reduce-scatter.50
  2402.2 17.3 reduce-scatter.44
  2422.0 17.3 reduce-scatter.46
  2441.5 17.2 reduce-scatter.42
  2461.0 17.1 reduce-scatter.34
  2481.0 19.6 reduce-scatter.48
  2503.4 26.0 reduce-scatter.24
  2532.5 25.7 reduce-scatter.26
  2560.7 42.9 reduce-scatter.30
  2606.1 43.1 reduce-scatter.32
  2651.5 43.1 reduce-scatter.28
  2697.0 102.6 reduce-scatter.36
  2802.0 102.7 reduce-scatter.38
  2907.1 102.7 reduce-scatter.40
where the time goes:
time: 3040 us; the launch traced here: 3020 us
  waiting for transfers between devices  1860 us (61%)
  matrix products  494 us (16%)
  other arithmetic  247 us (8%)
  local copies, waits for them, and re-layouts  208 us (7%)
  blocking collectives  175 us (6%)
    reduce_scatter x9, waiting for transfers between devices, shards(): lax.psum_scatter(shortened(weight_grads(rows)), 'seq', scatter_dimension=...  509 us
    psum x4, waiting for transfers between devices, layer_forward(): lax.psum(dot_right(hidden_ff, lower_w), 'tensor')  243 us
    psum x4, waiting for transfers between devices, layer_forward(): middle = hidden + lax.psum(dot_right(gated, output_w), 'tensor')  235 us
    psum x4, waiting for transfers between devices, layer_backward(): lax.psum(feed_part.astype(jnp.bfloat16), 'tensor').astype(jnp.float32)  177 us
    psum x4, waiting for transfers between devices, layer_backward(): lax.psum(mixer_part.astype(jnp.bfloat16), 'tensor').astype(jnp.float32)  146 us
    dot_general x36, matrix products, dot_plain(): return jnp.dot(left, right, preferred_element_type=jnp.float32)  109 us
    all_gather x1, waiting for transfers between devices, shards(): lax.all_gather(feed_gate, 'seq', axis=1, tiled=True)  102 us
    all_gather x1, waiting for transfers between devices, shards(): lax.all_gather(feed_up, 'seq', axis=1, tiled=True)  100 us
  transfers between devices with their start and end apart: 52, of which 44 were waited for; matrix products, arithmetic and copies ran while one was open for 13% of the time, Pallas kernels for 0%

commit v1 on v0

v1 whole, which is shorter than its diff:
```python
from functools import partial

import jax
import jax.numpy as jnp
from jax import lax
from jax.experimental import pallas as pl
from jax.experimental.pallas import tpu as pltpu
from jax.sharding import Mesh
from jax.sharding import PartitionSpec as P

SPAN = 64
FINE = 8

HIGH = lax.Precision.HIGHEST
MODEL_EPS = 1e-06
HEAD_EPS = 1e-05
GATE_SCALE = 16.0

f32 = jnp.float32
bf16 = jnp.bfloat16
GROUP = ("section", "q")


def dot_plain(left, right):
    return jnp.dot(left, right, preferred_element_type=f32)


def dot_left(left, right):
    return lax.dot_general(left, right, (((0,), (0,)), ((), ())), preferred_element_type=f32)


def dot_right(left, right):
    return lax.dot_general(left, right, (((1,), (1,)), ((), ())), preferred_element_type=f32)


def normed_rows(u, gain):
    return gain * u * lax.rsqrt(jnp.mean(u * u, axis=-1, keepdims=True) + MODEL_EPS)


def norm_back(d, u, gain):
    s = lax.rsqrt(jnp.mean(u * u, axis=-1, keepdims=True) + MODEL_EPS)
    w = gain * d
    d_u = s * w - u * (s * s * s) * jnp.mean(w * u, axis=-1, keepdims=True)
    return d_u, jnp.sum(d * u * s, axis=0, keepdims=True)


class Peers:
    def __init__(self, peers):
        self.peers = peers
        self.me = lax.axis_index("tensor")

    def at(self, d):
        return lax.rem(self.me + d, self.peers)

    def enter(self, relay_to):
        barrier = pltpu.get_barrier_semaphore()
        for d in range(1, self.peers):
            pl.semaphore_signal(barrier, inc=1, device_id={"tensor": self.at(d)})
        if relay_to is None:
            pl.semaphore_wait(barrier, self.peers - 1)
            return
        stage = lax.axis_index("stage")

        @pl.when(stage == relay_to)
        def _():
            pl.semaphore_signal(barrier, inc=1, device_id={"stage": 1 - relay_to})
            pl.semaphore_wait(barrier, self.peers - 1)

        @pl.when(stage != relay_to)
        def _():
            pl.semaphore_wait(barrier, self.peers)


def reduce_rows(peers, part, send, land, sems, total, fine=None, fine_sems=None):
    copies = []
    for d in range(1, peers.peers):
        peer = peers.at(d)
        send[d - 1] = part[peer].astype(bf16)
        copy = pltpu.make_async_remote_copy(
            src_ref=send.at[d - 1],
            dst_ref=land.at[d - 1],
            send_sem=sems.at[0, d - 1],
            recv_sem=sems.at[1, d - 1],
            device_id={"tensor": peer},
        )
        copy.start()
        copies.append(copy)
    if fine is not None:
        for d in range(1, peers.peers):

            @pl.when(peers.at(d) == 0)
            def _():
                fine_copy(part, fine, fine_sems, d).start()

    acc = part[peers.me].astype(f32)
    for d in range(1, peers.peers):
        copies[d - 1].wait()
        acc = acc + land[d - 1].astype(f32)
    total[...] = acc
    if fine is not None:
        for d in range(1, peers.peers):

            @pl.when(peers.at(d) == 0)
            def _():
                fine_copy(part, fine, fine_sems, d).wait_send()

        @pl.when(peers.me == 0)
        def _():
            top = part[0, 0:FINE, :]
            for d in range(1, peers.peers):
                fine_copy(part, fine, fine_sems, d).wait_recv()
                top = top + fine[d - 1]
            total[0:FINE, :] = top


def fine_copy(part, fine, fine_sems, d):
    return pltpu.make_async_remote_copy(
        src_ref=part.at[0, pl.ds(0, FINE), :],
        dst_ref=fine.at[d - 1],
        send_sem=fine_sems.at[0, d - 1],
        recv_sem=fine_sems.at[1, d - 1],
        device_id={"tensor": 0},
    )


def share_rows(peers, full, sems):
    copies = []
    for d in range(1, peers.peers):
        copy = pltpu.make_async_remote_copy(
            src_ref=full.at[peers.me],
            dst_ref=full.at[peers.me],
            send_sem=sems.at[0, d - 1],
            recv_sem=sems.at[1, d - 1],
            device_id={"tensor": peers.at(d)},
        )
        copy.start()
        copies.append(copy)
    for copy in copies:
        copy.wait()


def relay_rows(src, land, sems, relay_to):
    return pltpu.make_async_remote_copy(
        src_ref=src,
        dst_ref=land,
        send_sem=sems.at[0],
        recv_sem=sems.at[1],
        device_id={"stage": relay_to},
    )


def first_kernel(peers_n, norm, h, gain, full, share_sems):
    peers = Peers(peers_n)
    peers.enter(None)
    if norm:
        full[peers.me] = normed_rows(h[...].astype(f32), gain[...]).astype(bf16)
    else:
        full[peers.me] = h[...]
    share_rows(peers, full, share_sems)


def forward_mid_kernel(
    peers_n, part, h, gain, middle, full, send, land, fine, total, sems, fine_sems, share_sems
):
    peers = Peers(peers_n)
    peers.enter(None)
    reduce_rows(peers, part, send, land, sems, total, fine, fine_sems)
    value = h[...].astype(f32) + total[...]
    middle[...] = value
    full[peers.me] = normed_rows(value, gain[...]).astype(bf16)
    share_rows(peers, full, share_sems)


def forward_end_kernel(
    peers_n,
    part,
    middle,
    gain,
    own,
    y,
    h,
    full,
    send,
    land,
    fine,
    total,
    relayed,
    sems,
    fine_sems,
    share_sems,
    relay_sems,
):
    peers = Peers(peers_n)
    stage = lax.axis_index("stage")
    peers.enter(1)
    reduce_rows(peers, part, send, land, sems, total, fine, fine_sems)
    y[...] = (middle[...] + total[...]).astype(bf16)
    relay = relay_rows(y, relayed, relay_sems, 1)

    @pl.when(stage == 0)
    def _():
        relay.start()
        h[...] = own[...]

    @pl.when(stage == 1)
    def _():
        relay.wait_recv()
        h[...] = relayed[...]

    full[peers.me] = normed_rows(h[...].astype(f32), gain[...]).astype(bf16)
    share_rows(peers, full, share_sems)

    @pl.when(stage == 0)
    def _():
        relay.wait_send()


def forward_last_kernel(
    peers_n, part, middle, y, send, land, fine, total, sems, fine_sems
):
    peers = Peers(peers_n)
    peers.enter(None)
    reduce_rows(peers, part, send, land, sems, total, fine, fine_sems)
    y[...] = (middle[...] + total[...]).astype(bf16)


def backward_mid_kernel(
    peers_n, part, gy, middle, gain, d_middle, gain_part, full, send, land, total, sems, share_sems
):
    peers = Peers(peers_n)
    peers.enter(None)
    reduce_rows(peers, part, send, land, sems, total)
    d_u, g = norm_back(total[...], middle[...], gain[...])
    value = gy[...].astype(f32) + d_u
    d_middle[...] = value
    gain_part[...] = g
    full[peers.me] = value.astype(bf16)
    share_rows(peers, full, share_sems)


def backward_end_kernel(
    peers_n,
    part,
    d_middle,
    h,
    gain,
    own,
    grad,
    gain_part,
    gy,
    full,
    send,
    land,
    total,
    relayed,
    sems,
    share_sems,
    relay_sems,
):
    peers = Peers(peers_n)
    stage = lax.axis_index("stage")
    peers.enter(0)
    reduce_rows(peers, part, send, land, sems, total)
    d_u, g = norm_back(total[...], h[...].astype(f32), gain[...])
    value = d_middle[...] + d_u
    grad[...] = value.astype(bf16)
    gain_part[...] = g
    relay = relay_rows(grad, relayed, relay_sems, 0)

    @pl.when(stage == 1)
    def _():
        relay.start()
        gy[...] = own[...]

    @pl.when(stage == 0)
    def _():
        relay.wait_recv()
        gy[...] = relayed[...]

    full[peers.me] = gy[...]
    share_rows(peers, full, share_sems)

    @pl.when(stage == 1)
    def _():
        relay.wait_send()


def backward_last_kernel(
    peers_n, part, d_middle, h, gain, grad, gain_part, send, land, total, sems
):
    peers = Peers(peers_n)
    peers.enter(None)
    reduce_rows(peers, part, send, land, sems, total)
    d_u, g = norm_back(total[...], h[...].astype(f32), gain[...])
    grad[...] = (d_middle[...] + d_u).astype(bf16)
    gain_part[...] = g


def in_vmem(count):
    return [pl.BlockSpec(memory_space=pltpu.VMEM)] * count


def kernel_call(body, outs, scratch, ident, *args):
    single = not isinstance(outs, list)
    return pl.pallas_call(
        body,
        out_shape=outs,
        in_specs=in_vmem(len(args)),
        out_specs=in_vmem(1)[0] if single else in_vmem(len(outs)),
        scratch_shapes=scratch,
        compiler_params=pltpu.CompilerParams(
            collective_id=ident, has_side_effects=True, vmem_limit_bytes=40 * 1024 * 1024
        ),
    )(*args)


def shape(dims, kind):
    return jax.ShapeDtypeStruct(dims, kind)


class Rows:
    def __init__(self, rows, width, peers):
        self.rows, self.width, self.peers = rows, width, peers
        self.slice_b = shape((rows, width), bf16)
        self.slice_f = shape((rows, width), f32)
        self.gain_f = shape((1, width), f32)
        self.full = shape((peers, rows, width), bf16)
        self.pair = pltpu.SemaphoreType.DMA((2, peers - 1))
        self.reduce = [
            pltpu.VMEM((peers - 1, rows, width), bf16),
            pltpu.VMEM((peers - 1, rows, width), bf16),
        ]
        self.fine = [pltpu.VMEM((peers - 1, FINE, width), f32)]
        self.total = [pltpu.VMEM((rows, width), f32)]
        self.relayed = [pltpu.VMEM((rows, width), bf16)]
        self.relay = pltpu.SemaphoreType.DMA((2,))

    def parts(self, part):
        return part.reshape(self.peers, self.rows, self.width)

    def flat(self, full):
        return full.reshape(self.peers * self.rows, self.width)

    def first(self, h, gain, norm, ident):
        body = partial(first_kernel, self.peers, norm)
        return self.flat(kernel_call(body, self.full, [self.pair], ident, h, gain))

    def forward_mid(self, part, h, gain):
        middle, full = kernel_call(
            partial(forward_mid_kernel, self.peers),
            [self.slice_f, self.full],
            self.reduce + self.fine + self.total + [self.pair] * 3,
            3,
            self.parts(part),
            h,
            gain,
        )
        return middle, self.flat(full)

    def forward_end(self, part, middle, gain, own):
        y, h, full = kernel_call(
            partial(forward_end_kernel, self.peers),
            [self.slice_b, self.slice_b, self.full],
            self.reduce + self.fine + self.total + self.relayed + [self.pair] * 3 + [self.relay],
            4,
            self.parts(part),
            middle,
            gain,
            own,
        )
        return y, h, self.flat(full)

    def forward_last(self, part, middle):
        return kernel_call(
            partial(forward_last_kernel, self.peers),
            self.slice_b,
            self.reduce + self.fine + self.total + [self.pair] * 2,
            5,
            self.parts(part),
            middle,
        )

    def backward_mid(self, part, gy, middle, gain):
        d_middle, gain_part, full = kernel_call(
            partial(backward_mid_kernel, self.peers),
            [self.slice_f, self.gain_f, self.full],
            self.reduce + self.total + [self.pair] * 2,
            6,
            self.parts(part),
            gy,
            middle,
            gain,
        )
        return d_middle, gain_part, self.flat(full)

    def backward_end(self, part, d_middle, h, gain, own):
        grad, gain_part, gy, full = kernel_call(
            partial(backward_end_kernel, self.peers),
            [self.slice_b, self.gain_f, self.slice_b, self.full],
            self.reduce + self.total + self.relayed + [self.pair] * 2 + [self.relay],
            7,
            self.parts(part),
            d_middle,
            h,
            gain,
            own,
        )
        return grad, gain_part, gy, self.flat(full)

    def backward_last(self, part, d_middle, h, gain):
        return kernel_call(
            partial(backward_last_kernel, self.peers),
            [self.slice_b, self.gain_f],
            self.reduce + self.total + [self.pair],
            8,
            self.parts(part),
            d_middle,
            h,
            gain,
        )


PAD = 16


class Chain:
    def __init__(self, ranges, half):
        self.ranges, self.half = ranges, half
        self.me = lax.axis_index("section") * half + lax.axis_index("q")

    def place(self, d):
        other = lax.rem(self.me + d, self.ranges)
        return {"section": other // self.half, "q": lax.rem(other, self.half)}

    def enter(self):
        barrier = pltpu.get_barrier_semaphore()
        for d in range(1, self.ranges):
            pl.semaphore_signal(barrier, inc=1, device_id=self.place(d))
        pl.semaphore_wait(barrier, self.ranges - 1)

    def copy(self, land, sems, d):
        return pltpu.make_async_remote_copy(
            src_ref=land.at[self.me],
            dst_ref=land.at[self.me],
            send_sem=sems.at[0, d - 1],
            recv_sem=sems.at[1, d - 1],
            device_id=self.place(d),
        )

    def start(self, land, sems, state, through):
        high = state.shape[0]
        land[self.me, 0:high, :] = state.astype(bf16)
        land[self.me, high : high + PAD, :] = jnp.broadcast_to(
            through, (PAD, through.shape[1])
        ).astype(bf16)
        for d in range(1, self.ranges):
            self.copy(land, sems, d).start()

    def finish(self, land, sems, high, later):
        for d in range(1, self.ranges):
            self.copy(land, sems, d).wait()

        def step(n, state):
            place = self.ranges - 1 - n if later else n
            taken = (place > self.me) if later else (place < self.me)
            through = land[place, high : high + PAD, :].astype(f32)[0:1, :]
            joined = through * state + land[place, 0:high, :].astype(f32)
            return jnp.where(taken, joined, state)

        zero = jnp.zeros((high, land.shape[2]), f32)
        state = zero
        for n in range(self.ranges):
            state = step(n, state)
        return state


def triangle(size):
    row = lax.broadcasted_iota(jnp.int32, (size, size), 0)
    col = lax.broadcasted_iota(jnp.int32, (size, size), 1)
    return row, col


def scores_of(q, k, c):
    row, col = triangle(SPAN)
    middle = c[SPAN // 2 : SPAN // 2 + 1, :]
    up, down = jnp.exp(c - middle), jnp.exp(middle - c)
    a, b = (q * up).astype(bf16), (k * down).astype(bf16)
    own = jnp.sum(q * k, axis=1, keepdims=True)
    scores = jnp.where(row == col, own, jnp.where(row > col, dot_right(a, b), 0.0))
    return scores, a, b, up, down


def mixer_forward_kernel(
    ranges, half, q_ref, k_ref, v_ref, og_ref, g_ref, hg_ref, inner_ref, gated_ref, c_ref, s_ref,
    moved, out, land, sems,
):
    chain = Chain(ranges, half)
    chain.enter()
    length, key_dim = q_ref.shape
    value_dim = v_ref.shape[1]
    spans = length // SPAN
    scale = key_dim ** (-0.5)
    row, col = triangle(SPAN)
    lower = (row >= col).astype(f32)
    state = jnp.zeros((value_dim, key_dim), f32)
    reach = jnp.zeros((1, key_dim), f32)
    for i in range(spans):
        rows = slice(i * SPAN, (i + 1) * SPAN)
        c = jnp.dot(lower, g_ref[rows, :], precision=HIGH, preferred_element_type=f32)
        c_ref[rows, :] = c
        last = c[SPAN - 1 : SPAN, :]
        fading = (k_ref[rows, :].astype(f32) * jnp.exp(last - c)).astype(bf16)
        step = dot_left(v_ref[rows, :], fading)
        moved[i] = step
        state = jnp.exp(last) * state + step
        reach = reach + last
    chain.start(land, sems, state, jnp.exp(reach))
    for i in range(spans):
        rows = slice(i * SPAN, (i + 1) * SPAN)
        q = q_ref[rows, :].astype(f32) * scale
        k = k_ref[rows, :].astype(f32)
        scores = scores_of(q, k, c_ref[rows, :])[0]
        out[rows, :] = dot_plain(scores.astype(bf16), v_ref[rows, :])
    state = chain.finish(land, sems, value_dim, False)
    for i in range(spans):
        rows = slice(i * SPAN, (i + 1) * SPAN)
        c = c_ref[rows, :]
        held = state.astype(bf16)
        s_ref[i] = held
        q = (q_ref[rows, :].astype(f32) * scale * jnp.exp(c)).astype(bf16)
        inner = out[rows, :] + dot_right(q, held)
        inner_ref[rows, :] = inner
        r = lax.rsqrt(jnp.mean(inner * inner, axis=-1, keepdims=True) + HEAD_EPS)
        og = og_ref[rows, :]
        gated = hg_ref[...] * inner * r * (og / (1.0 + jnp.exp(-og)))
        gated_ref[rows, :] = gated.astype(bf16)
        state = jnp.exp(c[SPAN - 1 : SPAN, :]) * state + moved[i]
    s_ref[spans] = state.astype(bf16)


def mixer_backward_kernel(
    ranges, half, dgated_ref, inner_ref, og_ref, hg_ref, q_ref, k_ref, v_ref, c_ref, s_ref,
    dq_ref, dk_ref, dv_ref, dog_ref, dg_ref, hgp_ref, pulled, o_ref, dqs, dks, dvs, land, sems,
):
    chain = Chain(ranges, half)
    chain.enter()
    length, key_dim = q_ref.shape
    value_dim = v_ref.shape[1]
    spans = length // SPAN
    scale = key_dim ** (-0.5)
    row, col = triangle(SPAN)
    upper = (row <= col).astype(f32)
    state = jnp.zeros((value_dim, key_dim), f32)
    reach = jnp.zeros((1, key_dim), f32)
    hg = hg_ref[...]
    head_part = jnp.zeros((1, value_dim), f32)
    for i in reversed(range(spans)):
        rows = slice(i * SPAN, (i + 1) * SPAN)
        inner, og, dgated = inner_ref[rows, :], og_ref[rows, :], dgated_ref[rows, :]
        r = lax.rsqrt(jnp.mean(inner * inner, axis=-1, keepdims=True) + HEAD_EPS)
        sg = 1.0 / (1.0 + jnp.exp(-og))
        d_norm = dgated * (og * sg)
        unit = inner * r
        head_part = head_part + jnp.sum(d_norm * unit, axis=0, keepdims=True)
        w = d_norm * hg
        d_inner = r * w - inner * (r * r * r) * jnp.mean(w * inner, axis=-1, keepdims=True)
        dog = dgated * unit * hg * (sg * (1.0 + og * (1.0 - sg)))
        dog_ref[rows, :] = dog.astype(bf16)
        o = d_inner.astype(bf16)
        o_ref[rows, :] = o
        c = c_ref[rows, :]
        q = (q_ref[rows, :].astype(f32) * scale * jnp.exp(c)).astype(bf16)
        step = dot_left(o, q)
        pulled[i] = step
        last = c[SPAN - 1 : SPAN, :]
        state = jnp.exp(last) * state + step
        reach = reach + last
    hgp_ref[...] = head_part
    chain.start(land, sems, state, jnp.exp(reach))
    for i in range(spans):
        rows = slice(i * SPAN, (i + 1) * SPAN)
        q = q_ref[rows, :].astype(f32) * scale
        k = k_ref[rows, :].astype(f32)
        scores, a, b, up, down = scores_of(q, k, c_ref[rows, :])
        o, v = o_ref[rows, :], v_ref[rows, :]
        d_scores = jnp.where(row >= col, dot_right(o, v), 0.0).astype(bf16)
        dvs[rows, :] = dot_left(scores.astype(bf16), o)
        dqs[rows, :] = up * dot_plain(d_scores, b) + jnp.exp(c_ref[rows, :]) * dot_plain(o, s_ref[i])
        dks[rows, :] = down * dot_left(d_scores, a)
    state = chain.finish(land, sems, value_dim, True)
    for i in reversed(range(spans)):
        rows = slice(i * SPAN, (i + 1) * SPAN)
        c = c_ref[rows, :]
        last = c[SPAN - 1 : SPAN, :]
        fade = jnp.exp(last - c)
        held = state.astype(bf16)
        k = k_ref[rows, :].astype(f32)
        dk = dks[rows, :] + fade * dot_plain(v_ref[rows, :], held)
        dv = dvs[rows, :] + dot_right((k * fade).astype(bf16), held)
        dq = dqs[rows, :]
        dq_ref[rows, :] = (dq * scale).astype(bf16)
        dk_ref[rows, :] = dk.astype(bf16)
        dv_ref[rows, :] = dv.astype(bf16)
        ended = jnp.sum(state * s_ref[i + 1].astype(f32), axis=0, keepdims=True)
        terms = q_ref[rows, :].astype(f32) * scale * dq - k * dk
        dg_ref[rows, :] = jnp.dot(upper, terms, precision=HIGH, preferred_element_type=f32) + ended
        state = jnp.exp(last) * state + pulled[i]


def mixer_forward(ranges, half, q, k, v, og, g, hg):
    length, key_dim = q.shape
    value_dim = v.shape[1]
    spans = length // SPAN
    return kernel_call(
        partial(mixer_forward_kernel, ranges, half),
        [
            shape((length, value_dim), f32),
            shape((length, value_dim), bf16),
            shape((length, key_dim), f32),
            shape((spans + 1, value_dim, key_dim), bf16),
        ],
        [
            pltpu.VMEM((spans, value_dim, key_dim), f32),
            pltpu.VMEM((length, value_dim), f32),
            pltpu.VMEM((ranges, value_dim + PAD, key_dim), bf16),
            pltpu.SemaphoreType.DMA((2, ranges - 1)),
        ],
        9,
        q, k, v, og, g, hg,
    )


def mixer_backward(ranges, half, dgated, inner, og, hg, q, k, v, c, s):
    length, key_dim = q.shape
    value_dim = v.shape[1]
    spans = length // SPAN
    return kernel_call(
        partial(mixer_backward_kernel, ranges, half),
        [
            shape((length, key_dim), bf16),
            shape((length, key_dim), bf16),
            shape((length, value_dim), bf16),
            shape((length, value_dim), bf16),
            shape((length, key_dim), f32),
            shape((1, value_dim), f32),
        ],
        [
            pltpu.VMEM((spans, value_dim, key_dim), f32),
            pltpu.VMEM((length, value_dim), bf16),
            pltpu.VMEM((length, key_dim), f32),
            pltpu.VMEM((length, key_dim), f32),
            pltpu.VMEM((length, value_dim), f32),
            pltpu.VMEM((ranges, value_dim + PAD, key_dim), bf16),
            pltpu.SemaphoreType.DMA((2, ranges - 1)),
        ],
        10,
        dgated, inner, og, hg, q, k, v, c, s,
    )


def swapped(array):
    return lax.ppermute(array, ("section", "stage"), [(0, 0), (1, 2), (2, 1), (3, 3)])


def work_weights(weights):
    return [lax.all_gather(swapped(w), GROUP, axis=0, tiled=True) for w in weights]


def shards(
    inputs,
    cotangent,
    query_proj,
    key_proj,
    value_proj,
    outgate_proj,
    output_proj,
    decay_down,
    decay_up,
    decay_bias,
    head_gain,
    mixer_gain,
    feed_gain,
    feed_gate,
    feed_up,
    feed_down,
):
    micro, length, width = inputs.shape
    peers = lax.axis_size("tensor")
    half = lax.axis_size("q")
    ranges = 2 * half
    stage = lax.axis_index("stage")
    me = lax.axis_index("tensor")
    rows = length // peers
    calls = Rows(rows, width, peers)

    def own_rows(array):
        return swapped(lax.dynamic_slice_in_dim(array, me * rows, rows, 1))

    own_in = own_rows(inputs)
    small = [decay_up[0], decay_bias[0], head_gain[0], mixer_gain[0], feed_gain[0], decay_down[0]]
    sizes = [a.size for a in small]
    packed = lax.all_gather(
        swapped(jnp.concatenate([a.reshape(-1) for a in small])), GROUP, axis=0
    )
    cuts = [sum(sizes[:n]) for n in range(len(sizes) + 1)]
    pieces = [packed[:, cuts[n] : cuts[n + 1]] for n in range(len(sizes))]
    up_w = pieces[0].reshape(-1, decay_up.shape[2]).astype(f32)
    bias_w = pieces[1].reshape(1, -1).astype(f32)
    head_w = pieces[2].reshape(1, -1).astype(f32)
    mixer_w = pieces[3].reshape(1, -1).astype(f32)
    feed_w = pieces[4].reshape(1, -1).astype(f32)
    down_w = pieces[5].reshape(-1, decay_down.shape[2])
    query_w, key_w, value_w, outgate_w, output_w, gate_w, upper_w, lower_w = work_weights(
        [
            query_proj[0],
            key_proj[0],
            value_proj[0],
            outgate_proj[0],
            output_proj[0],
            feed_gate[0],
            feed_up[0],
            feed_down[0],
        ]
    )
    own_cot = own_rows(cotangent)

    kept, ys = [], []
    h = jnp.where(stage == 0, own_in[0], jnp.zeros_like(own_in[0]))
    normed = calls.first(h, mixer_w, True, 1)
    for step in range(micro + 1):
        q = dot_plain(normed, query_w).astype(bf16)
        k = dot_plain(normed, key_w).astype(bf16)
        v = dot_plain(normed, value_w).astype(bf16)
        out_gate = dot_plain(normed, outgate_w)
        rank_part = dot_plain(normed, down_w)
        logits = jnp.dot(rank_part, up_w.T, precision=HIGH) + bias_w
        decay = jax.nn.log_sigmoid(logits) / GATE_SCALE
        inner, gated, cumul, states = mixer_forward(
            ranges, half, q, k, v, out_gate, decay, head_w
        )
        middle, feed_in = calls.forward_mid(dot_right(gated, output_w), h, feed_w)
        gate_v = dot_plain(feed_in, gate_w)
        upper_v = dot_plain(feed_in, upper_w)
        hidden_ff = (jax.nn.silu(gate_v) * upper_v).astype(bf16)
        kept.append(
            dict(
                h=h, normed=normed, q=q, k=k, v=v, out_gate=out_gate, rank_part=rank_part,
                logits=logits, inner=inner, gated=gated, cumul=cumul, states=states,
                middle=middle, feed_in=feed_in, gate_v=gate_v, upper_v=upper_v,
                hidden_ff=hidden_ff,
            )
        )
        part = dot_right(hidden_ff, lower_w)
        if step < micro:
            y, h, normed = calls.forward_end(
                part, middle, mixer_w, own_in[min(step + 1, micro - 1)]
            )
        else:
            y = calls.forward_last(part, middle)
        ys.append(y)

    grads, saved = [], []
    gy = jnp.where(stage == 1, own_cot[micro - 1], jnp.zeros_like(own_cot[0]))
    d_feed = calls.first(gy, mixer_w, False, 2)
    for step in range(micro + 1):
        now = kept[micro - step]
        d_hidden = dot_plain(d_feed, lower_w)
        sig = jax.nn.sigmoid(now["gate_v"])
        d_gate = (
            d_hidden * now["upper_v"] * (sig * (1.0 + now["gate_v"] * (1.0 - sig)))
        ).astype(bf16)
        d_upper = (d_hidden * (now["gate_v"] * sig)).astype(bf16)
        part = dot_right(d_gate, gate_w) + dot_right(d_upper, upper_w)
        d_middle, feed_part, d_mixed = calls.backward_mid(part, gy, now["middle"], feed_w)
        d_gated = dot_plain(d_mixed, output_w)
        d_q, d_k, d_v, d_outgate, d_decay, head_part = mixer_backward(
            ranges, half, d_gated, now["inner"], now["out_gate"], head_w,
            now["q"], now["k"], now["v"], now["cumul"], now["states"],
        )
        d_logits = d_decay * jax.nn.sigmoid(-now["logits"]) / GATE_SCALE
        d_rank = jnp.dot(d_logits, up_w, precision=HIGH)
        part = (
            dot_right(d_q, query_w)
            + dot_right(d_k, key_w)
            + dot_right(d_v, value_w)
            + dot_right(d_outgate, outgate_w)
            + dot_right(d_rank.astype(bf16), down_w)
        )
        saved.append(
            dict(
                d_feed=d_feed, d_gate=d_gate, d_upper=d_upper, d_mixed=d_mixed, d_q=d_q, d_k=d_k,
                d_v=d_v, d_outgate=d_outgate, d_logits=d_logits, d_rank=d_rank,
            )
        )
        if step < micro:
            later = micro - 2 - step
            own = own_cot[later] if later >= 0 else jnp.zeros_like(own_cot[0])
            grad, mixer_part, gy, d_feed = calls.backward_end(part, d_middle, now["h"], mixer_w, own)
        else:
            grad, mixer_part = calls.backward_last(part, d_middle, now["h"], mixer_w)
        grads.append(grad)
        saved[-1].update(head=head_part, mixer=mixer_part, feed=feed_part)

    def rows_of(name):
        if name in kept[0]:
            return jnp.concatenate([item[name] for item in kept])
        return jnp.concatenate([item[name] for item in reversed(saved)])

    def home(whole):
        return swapped(
            lax.psum_scatter(whole.astype(bf16), GROUP, scatter_dimension=0, tiled=True)
        )[None].astype(f32)

    normed, feed_in, d_feed = rows_of("normed"), rows_of("feed_in"), rows_of("d_feed")
    gate_grad = home(dot_left(feed_in, rows_of("d_gate")))
    upper_grad = home(dot_left(feed_in, rows_of("d_upper")))
    lower_grad = home(dot_left(d_feed, rows_of("hidden_ff")))
    output_grad = home(dot_left(rows_of("d_mixed"), rows_of("gated")))
    query_grad = home(dot_left(normed, rows_of("d_q")))
    key_grad = home(dot_left(normed, rows_of("d_k")))
    value_grad = home(dot_left(normed, rows_of("d_v")))
    outgate_grad = home(dot_left(normed, rows_of("d_outgate")))

    d_logits = rows_of("d_logits")
    small_grads = [
        jnp.dot(d_logits.T, rows_of("rank_part"), precision=HIGH),
        jnp.sum(d_logits, axis=0),
        sum(item["head"] for item in saved),
        sum(item["mixer"] for item in saved),
        sum(item["feed"] for item in saved),
        dot_left(normed, rows_of("d_rank").astype(bf16)),
    ]
    small_sum = swapped(
        lax.psum_scatter(
            jnp.concatenate([g.reshape(ranges, -1) for g in small_grads], axis=1),
            GROUP,
            scatter_dimension=0,
            tiled=True,
        )
    )[0]
    shared = lax.psum(small_sum[cuts[2] :], "tensor")

    def piece(n, like):
        source = small_sum if n < 2 else shared
        begin = cuts[n] if n < 2 else cuts[n] - cuts[2]
        return source[begin : begin + sizes[n]].reshape(like.shape)

    def placed(early, late):
        mine = swapped(jnp.where(stage == 0, jnp.stack(early), jnp.stack(late)))
        return lax.all_gather(mine, "tensor", axis=1, tiled=True)[None]

    layer_outputs = placed(ys[:micro], ys[1:])
    input_grads = placed(grads[:0:-1], grads[micro - 1 :: -1]).astype(f32)
    return (
        layer_outputs,
        input_grads,
        query_grad,
        key_grad,
        value_grad,
        outgate_grad,
        output_grad,
        piece(5, decay_down),
        piece(0, decay_up),
        piece(1, decay_bias),
        piece(2, head_gain),
        piece(3, mixer_gain),
        piece(4, feed_gain),
        gate_grad,
        upper_grad,
        lower_grad,
    )


def solution(mesh):
    sections, ranges, peers = (mesh.shape[a] for a in ("section", "seq", "tensor"))
    staged = Mesh(
        mesh.devices.reshape(sections, 2, ranges // 2, peers), ("section", "stage", "q", "tensor")
    )
    seq = ("stage", "q")
    whole = P("section", seq, "tensor")
    row = P("section", seq)
    rows = P("section", None, seq, None)
    tokens = P(None, seq, None)
    narrow = P("section", seq, None)
    return jax.shard_map(
        shards,
        mesh=staged,
        in_specs=(tokens, tokens)
        + (whole,) * 5
        + (narrow, whole, whole, row, row, row)
        + (whole,) * 3,
        out_specs=(rows, rows) + (whole,) * 5 + (narrow, whole, whole, row, row, row) + (whole,) * 3,
        check_vma=False,
    )
```

time: 3040 us -> 2100 us (0.69)
  waiting for transfers between devices: 1860 us -> 1040 us
  Pallas kernels: 0 us -> 644 us
  matrix products: 494 us -> 222 us
  other arithmetic: 247 us -> 24.7 us
  local copies, waits for them, and re-layouts: 208 us -> 48.1 us
  blocking collectives: 175 us -> 15.2 us
  starting transfers between devices: 14.6 us -> 76.2 us
    psum x16 -> x0, waiting for transfers between devices: 801 us -> none  [the longest x4 243 us: layer_forward(): lax.psum(dot_right(hidden_ff, lower_w), 'tensor')]
    pallas_call x0 -> x26, Pallas kernels: none -> 644 us  [kernel_call(): pl.pallas_call(body, out_shape=outs, in_specs=in_vmem(len(args)), out_spe...]
    dot_general x282 -> x45, matrix products: 364 us -> 92.3 us  [the longest x36 85.7 us: dot_plain(): return jnp.dot(left, right, preferred_element_type=f32)]
    ppermute x6 -> x22, waiting for transfers between devices: 7.03 us -> 227 us  [swapped(): lax.ppermute(array, ('section', 'stage'), [(0, 0), (1, 2), (2, 1), (3, 3)])]
    all_gather x16 -> x10, waiting for transfers between devices: 523 us -> 396 us  [the longest x8 310 us: work_weights(): lax.all_gather(swapped(w), GROUP, axis=0, tiled=True)]
    all_gather x13 -> x0, blocking collectives: 119 us -> none  [the longest x4 31.2 us: prefix(): lax.all_gather(a.astype(kind), axis)]
    reduce_scatter x9 -> x8, waiting for transfers between devices: 509 us -> 418 us  [home(): lax.psum_scatter(whole.astype(bf16), GROUP, scatter_dimension=0, tiled=True)]
    squeeze x96 -> x0, local copies, waits for them, and re-layouts: 84.2 us -> none  [span_scan(): state_end, outputs = lax.scan(jax.checkpoint(one_block), state, pieces)]
  transfers between devices with their start and end apart: 52 -> 42, of which waited for: 44 -> 23; matrix products, arithmetic and copies ran while one was open for 13% -> 6% of each run, Pallas kernels for 0% -> 4%
where the time goes in v1:
time: 2100 us; the launch traced here: 2090 us
  waiting for transfers between devices  1040 us (50%)
  Pallas kernels  644 us (31%)
  matrix products  222 us (11%)
  starting transfers between devices  76.2 us (4%)
  local copies, waits for them, and re-layouts  48.1 us (2%)
  other arithmetic  24.7 us (1%)
    pallas_call x26, Pallas kernels, kernel_call(): pl.pallas_call(body, out_shape=outs, in_specs=in_vmem(len(args)), out_spe...  644 us
    reduce_scatter x8, waiting for transfers between devices, home(): lax.psum_scatter(whole.astype(bf16), GROUP, scatter_dimension=0, tiled=True)  418 us
    all_gather x8, waiting for transfers between devices, work_weights(): lax.all_gather(swapped(w), GROUP, axis=0, tiled=True)  310 us
    ppermute x22, waiting for transfers between devices, swapped(): lax.ppermute(array, ('section', 'stage'), [(0, 0), (1, 2), (2, 1), (3, 3)])  227 us
    dot_general x36, matrix products, dot_plain(): return jnp.dot(left, right, preferred_element_type=f32)  85.7 us
    all_gather x2, waiting for transfers between devices, placed(): return lax.all_gather(mine, 'tensor', axis=1, tiled=True)[None]  85.4 us
    ppermute x22, starting transfers between devices, swapped(): lax.ppermute(array, ('section', 'stage'), [(0, 0), (1, 2), (2, 1), (3, 3)])  74.8 us
    dot_general x36, matrix products, dot_right(): lax.dot_general(left, right, (((1,), (1,)), ((), ())), preferred_element_...  68.9 us
  transfers between devices with their start and end apart: 42, of which 23 were waited for; matrix products, arithmetic and copies ran while one was open for 6% of the time, Pallas kernels for 4%

profile of v1, /device:TPU:24, one launch (start us, length us, event | category | flops | bytes accessed | tf_op | source)
XLA Modules:
  0.0 2088.5 jit_solution(9603010470016499852)
XLA Ops:
  26.6 7.7 collective-permute-done.2
  37.0 14.9 collective-permute-done.4
  53.9 14.3 collective-permute-done.5
  70.2 18.2 collective-permute-done.6
  93.4 32.5 %collective-permute-done.7 = bf16[512,1408]{1,0:T(8,128)(2,1)} collective-permute-done((bf16[512,1408]{1,0:T(8,128)(2,1)}, bf16[512,1408]{1,0:T(8,128)(2,1)}, u32[]{:S(2)}, u32[]{:S(2)}) %collective-permute-start.7) | collective-permute-done | bytes 1441824 | tf_op jit(solution)/shard_map/ppermute | solution.py:662
  127.9 34.8 %collective-permute-done.8 = bf16[512,1408]{1,0:T(8,128)(2,1)} collective-permute-done((bf16[512,1408]{1,0:T(8,128)(2,1)}, bf16[512,1408]{1,0:T(8,128)(2,1)}, u32[]{:S(2)}, u32[]{:S(2)}) %collective-permute-start.8) | collective-permute-done | bytes 1441824 | tf_op jit(solution)/shard_map/ppermute | solution.py:662
  164.7 32.0 %collective-permute-done.9 = bf16[512,1408]{1,0:T(8,128)(2,1)} collective-permute-done((bf16[512,1408]{1,0:T(8,128)(2,1)}, bf16[512,1408]{1,0:T(8,128)(2,1)}, u32[]{:S(2)}, u32[]{:S(2)}) %collective-permute-start.9) | collective-permute-done | bytes 1441824 | tf_op jit(solution)/shard_map/ppermute | solution.py:662
  209.0 20.2 collective-permute-done
  230.1 10.4 shard_map.279
  241.5 9.9 shard_map.292
  259.3 12.4 all-gather.18.cloned.1.call-done
  274.0 21.4 %shard_map.280 = (f32[256,512]{1,0:T(8,128)S(1)}, bf16[256,512]{1,0:T(8,128)(2,1)S(1)}, f32[256,256]{1,0:T(8,128)S(1)}, bf16[5,512,256]{2,1,0:T(8,128)(2,1)S(1)}) custom-call(bf16[256,256]{1,0:T(8,128)(2,1)S(1)} %copy-done.16, bf16[256,256]{1,0:T(8,128)(2,1)S(1)} %convolution_convert_fusion.17.k_ref, bf16[256,512]{1,0:T(8,128)(2,1)S(1)} %convolution_convert_fusion.10.v_ref, ...), custom_call_target="tpu_custom_call" | custom-call | tf_op jit(solution)/shard_map/pallas_call | solution.py:305
  298.0 25.7 %all-gather.20.cloned.1.call-done = bf16[2048,512]{1,0:T(8,128)(2,1)} async-done(((bf16[512,512]{1,0:T(8,128)(2,1)}), bf16[2048,512]{1,0:T(8,128)(2,1)}) %all-gather.20.cloned.1.call-update) | async-done | bytes 2097168 | tf_op jit(solution)/shard_map/all_gather | solution.py:666
  326.1 29.9 %shard_map.281 = (f32[64,2048]{1,0:T(8,128)S(1)}, bf16[4,64,2048]{2,1,0:T(8,128)(2,1)S(1)}) custom-call(f32[4,64,2048]{2,1,0:T(8,128)S(1)} %bitcast.308, bf16[64,2048]{1,0:T(8,128)(2,1)S(1)} %get-tuple-element.236.h, f32[1,2048]{1,0:T(1,128)S(1)} %bitcast.336), custom_call_target="tpu_custom_call" | custom-call | tf_op jit(solution)/shard_map/pallas_call | solution.py:305
  356.8 72.9 %all-gather.22.cloned.1.call-done = bf16[2048,1408]{1,0:T(8,128)(2,1)} async-done(((bf16[512,1408]{1,0:T(8,128)(2,1)}), bf16[2048,1408]{1,0:T(8,128)(2,1)}) %all-gather.22.cloned.1.call-update) | async-done | bytes 5767184 | tf_op jit(solution)/shard_map/all_gather | solution.py:666
  429.6 5.5 fusion.142
  435.2 100.0 %all-gather.24.cloned.1.call-done = bf16[2048,1408]{1,0:T(8,128)(2,1)} async-done(((bf16[512,1408]{1,0:T(8,128)(2,1)}), bf16[2048,1408]{1,0:T(8,128)(2,1)}) %all-gather.24.cloned.1.call-update) | async-done | bytes 5767184 | tf_op jit(solution)/shard_map/all_gather | solution.py:666
  535.2 6.0 multiply_convert_fusion.11
  541.1 99.6 %all-gather.26.cloned.1.call-done = bf16[2048,1408]{1,0:T(8,128)(2,1)} async-done(((bf16[512,1408]{1,0:T(8,128)(2,1)}), bf16[2048,1408]{1,0:T(8,128)(2,1)}) %all-gather.26.cloned.1.call-update) | async-done | bytes 5767184 | tf_op jit(solution)/shard_map/all_gather | solution.py:666
  645.3 41.2 %shard_map.282 = (bf16[64,2048]{1,0:T(8,128)(2,1)S(1)}, bf16[64,2048]{1,0:T(8,128)(2,1)S(1)}, bf16[4,64,2048]{2,1,0:T(8,128)(2,1)S(1)}) custom-call(f32[4,64,2048]{2,1,0:T(8,128)S(1)} %bitcast.320, f32[64,2048]{1,0:T(8,128)S(1)} %copy-done.13, f32[1,2048]{1,0:T(1,128)S(1)} %bitcast.329, bf16[64,2048]{1,0:T(8,128)(2,1)S(1)} %copy-done.25), custom_call_target="tpu_custom_call" | custom-call | tf_op jit(solution)/shard_map/pallas_call | solution.py:305
  690.7 16.0 shard_map.283
  707.5 29.4 %shard_map.284 = (f32[64,2048]{1,0:T(8,128)S(1)}, bf16[4,64,2048]{2,1,0:T(8,128)(2,1)S(1)}) custom-call(f32[4,64,2048]{2,1,0:T(8,128)S(1)} %bitcast.309, bf16[64,2048]{1,0:T(8,128)(2,1)S(1)} %get-tuple-element.105.h, f32[1,2048]{1,0:T(1,128)S(1)} %bitcast.337), custom_call_target="tpu_custom_call" | custom-call | tf_op jit(solution)/shard_map/pallas_call | solution.py:305
  746.8 36.7 %shard_map.285 = (bf16[64,2048]{1,0:T(8,128)(2,1)S(1)}, bf16[64,2048]{1,0:T(8,128)(2,1)S(1)}, bf16[4,64,2048]{2,1,0:T(8,128)(2,1)S(1)}) custom-call(f32[4,64,2048]{2,1,0:T(8,128)S(1)} %bitcast.321, f32[64,2048]{1,0:T(8,128)S(1)} %get-tuple-element.107.middle, f32[1,2048]{1,0:T(1,128)S(1)} %bitcast.330, bf16[64,2048]{1,0:T(8,128)(2,1)S(1)} %copy-done.7), custom_call_target="tpu_custom_call" | custom-call | tf_op jit(solution)/shard_map/pallas_call | solution.py:305
  787.5 16.0 shard_map.286
  806.0 31.0 %shard_map.287 = (f32[64,2048]{1,0:T(8,128)S(1)}, bf16[4,64,2048]{2,1,0:T(8,128)(2,1)S(1)}) custom-call(f32[4,64,2048]{2,1,0:T(8,128)S(1)} %bitcast.310, bf16[64,2048]{1,0:T(8,128)(2,1)S(1)} %get-tuple-element.111.h, f32[1,2048]{1,0:T(1,128)S(1)} %bitcast.338), custom_call_target="tpu_custom_call" | custom-call | tf_op jit(solution)/shard_map/pallas_call | solution.py:305
  841.9 6.2 multiply_convert_fusion.9
  850.0 41.5 %shard_map.288 = (bf16[64,2048]{1,0:T(8,128)(2,1)S(1)}, bf16[64,2048]{1,0:T(8,128)(2,1)S(1)}, bf16[4,64,2048]{2,1,0:T(8,128)(2,1)S(1)}) custom-call(f32[4,64,2048]{2,1,0:T(8,128)S(1)} %bitcast.322, f32[64,2048]{1,0:T(8,128)S(1)} %get-tuple-element.113.middle, f32[1,2048]{1,0:T(1,128)S(1)} %bitcast.331, bf16[64,2048]{1,0:T(8,128)(2,1)S(1)} %copy-done.7), custom_call_target="tpu_custom_call" | custom-call | tf_op jit(solution)/shard_map/pallas_call | solution.py:305
  896.0 16.0 shard_map.289
  914.5 31.1 %shard_map.290 = (f32[64,2048]{1,0:T(8,128)S(1)}, bf16[4,64,2048]{2,1,0:T(8,128)(2,1)S(1)}) custom-call(f32[4,64,2048]{2,1,0:T(8,128)S(1)} %bitcast.311, bf16[64,2048]{1,0:T(8,128)(2,1)S(1)} %get-tuple-element.117.h, f32[1,2048]{1,0:T(1,128)S(1)} %bitcast.339), custom_call_target="tpu_custom_call" | custom-call | tf_op jit(solution)/shard_map/pallas_call | solution.py:305
  945.6 5.0 fusion.157
  965.4 29.0 %shard_map.293 = (f32[64,2048]{1,0:T(8,128)S(1)}, f32[1,2048]{1,0:T(1,128)S(1)}, bf16[4,64,2048]{2,1,0:T(8,128)(2,1)S(1)}) custom-call(f32[4,64,2048]{2,1,0:T(8,128)S(1)} %bitcast.317, bf16[64,2048]{1,0:T(8,128)(2,1)S(1)} %copy-done.6, f32[64,2048]{1,0:T(8,128)S(1)} %get-tuple-element.119.middle, f32[1,2048]{1,0:T(1,128)S(1)} %bitcast.340), custom_call_target="tpu_custom_call" | custom-call | tf_op jit(solution)/shard_map/pallas_call | solution.py:305
  997.1 16.4 shard_map.294
  1019.2 29.5 %shard_map.295 = (bf16[64,2048]{1,0:T(8,128)(2,1)S(1)}, f32[1,2048]{1,0:T(1,128)S(1)}, bf16[64,2048]{1,0:T(8,128)(2,1)S(1)}, bf16[4,64,2048]{2,1,0:T(8,128)(2,1)S(1)}) custom-call(f32[4,64,2048]{2,1,0:T(8,128)S(1)} %bitcast.314, f32[64,2048]{1,0:T(8,128)S(1)} %get-tuple-element.129.d_middle, bf16[64,2048]{1,0:T(8,128)(2,1)S(1)} %get-tuple-element.117.h, ...), custom_call_target="tpu_custom_call" | custom-call | tf_op jit(solution)/shard_map/pallas_call | solution.py:305
  1048.7 6.0 multiply_convert_fusion.5
  1061.1 27.6 %shard_map.296 = (f32[64,2048]{1,0:T(8,128)S(1)}, f32[1,2048]{1,0:T(1,128)S(1)}, bf16[4,64,2048]{2,1,0:T(8,128)(2,1)S(1)}) custom-call(f32[4,64,2048]{2,1,0:T(8,128)S(1)} %bitcast.318, bf16[64,2048]{1,0:T(8,128)(2,1)S(1)} %get-tuple-element.131.gy, f32[64,2048]{1,0:T(8,128)S(1)} %get-tuple-element.113.middle, f32[1,2048]{1,0:T(1,128)S(1)} %bitcast.341), custom_call_target="tpu_custom_call" | custom-call | tf_op jit(solution)/shard_map/pallas_call | solution.py:305
  1091.4 16.4 shard_map.297
  1113.5 39.4 %shard_map.298 = (bf16[64,2048]{1,0:T(8,128)(2,1)S(1)}, f32[1,2048]{1,0:T(1,128)S(1)}, bf16[64,2048]{1,0:T(8,128)(2,1)S(1)}, bf16[4,64,2048]{2,1,0:T(8,128)(2,1)S(1)}) custom-call(f32[4,64,2048]{2,1,0:T(8,128)S(1)} %bitcast.312, f32[64,2048]{1,0:T(8,128)S(1)} %get-tuple-element.141.d_middle, bf16[64,2048]{1,0:T(8,128)(2,1)S(1)} %get-tuple-element.111.h, ...), custom_call_target="tpu_custom_call" | custom-call | tf_op jit(solution)/shard_map/pallas_call | solution.py:305
  1152.9 5.6 multiply_convert_fusion.3
  1168.1 26.4 %shard_map.299 = (f32[64,2048]{1,0:T(8,128)S(1)}, f32[1,2048]{1,0:T(1,128)S(1)}, bf16[4,64,2048]{2,1,0:T(8,128)(2,1)S(1)}) custom-call(f32[4,64,2048]{2,1,0:T(8,128)S(1)} %bitcast.319, bf16[64,2048]{1,0:T(8,128)(2,1)S(1)} %get-tuple-element.143.gy, f32[64,2048]{1,0:T(8,128)S(1)} %get-tuple-element.107.middle, f32[1,2048]{1,0:T(1,128)S(1)} %bitcast.342), custom_call_target="tpu_custom_call" | custom-call | tf_op jit(solution)/shard_map/pallas_call | solution.py:305
  1197.2 16.4 shard_map.300
  1218.8 42.2 %shard_map.301 = (bf16[64,2048]{1,0:T(8,128)(2,1)S(1)}, f32[1,2048]{1,0:T(1,128)S(1)}, bf16[64,2048]{1,0:T(8,128)(2,1)S(1)}, bf16[4,64,2048]{2,1,0:T(8,128)(2,1)S(1)}) custom-call(f32[4,64,2048]{2,1,0:T(8,128)S(1)} %bitcast.313, f32[64,2048]{1,0:T(8,128)S(1)} %get-tuple-element.153.d_middle, bf16[64,2048]{1,0:T(8,128)(2,1)S(1)} %get-tuple-element.105.h, ...), custom_call_target="tpu_custom_call" | custom-call | tf_op jit(solution)/shard_map/pallas_call | solution.py:305
  1261.1 5.2 multiply_convert_fusion.1
  1275.8 26.8 %shard_map.302 = (f32[64,2048]{1,0:T(8,128)S(1)}, f32[1,2048]{1,0:T(1,128)S(1)}, bf16[4,64,2048]{2,1,0:T(8,128)(2,1)S(1)}) custom-call(f32[4,64,2048]{2,1,0:T(8,128)S(1)} %bitcast.316, bf16[64,2048]{1,0:T(8,128)(2,1)S(1)} %get-tuple-element.155.gy, f32[64,2048]{1,0:T(8,128)S(1)} %copy-done.13, f32[1,2048]{1,0:T(1,128)S(1)} %bitcast.343), custom_call_target="tpu_custom_call" | custom-call | tf_op jit(solution)/shard_map/pallas_call | solution.py:305
  1305.6 16.3 shard_map.303
  1338.7 15.8 shard_map.304
  1365.9 6.1 fusion.15
  1372.9 5.1 convolution_convert_fusion.3
  1379.0 5.1 convolution_convert_fusion.4
  1385.7 11.7 convolution_convert_fusion
  1399.2 11.2 convolution_convert_fusion.1
  1410.7 11.5 convolution_convert_fusion.2
  1423.5 16.1 collective-permute-start.12
  1439.6 23.9 %collective-permute-done.12 = bf16[3,64,2048]{2,1,0:T(8,128)(2,1)S(1)} collective-permute-done((bf16[3,64,2048]{2,1,0:T(8,128)(2,1)S(1)}, bf16[3,64,2048]{2,1,0:T(8,128)(2,1)S(1)}, u32[]{:S(2)}, u32[]{:S(2)}) %collective-permute-start.12) | collective-permute-done | bytes 786464 | tf_op jit(solution)/shard_map/ppermute | solution.py:662
  1469.3 11.1 shard_map.291
  1484.4 26.3 %collective-permute-done.10 = bf16[3,64,2048]{2,1,0:T(8,128)(2,1)S(1)} collective-permute-done((bf16[3,64,2048]{2,1,0:T(8,128)(2,1)S(1)}, bf16[3,64,2048]{2,1,0:T(8,128)(2,1)S(1)}, u32[]{:S(2)}, u32[]{:S(2)}) %collective-permute-start.10) | collective-permute-done | bytes 786464 | tf_op jit(solution)/shard_map/ppermute | solution.py:662
  1520.3 15.2 psum.7
  1547.1 31.7 %reduce-scatter.15.cloned.1.call-done = bf16[512,512]{1,0:T(8,128)(2,1)} async-done(((bf16[2048,512]{1,0:T(8,128)(2,1)}), bf16[512,512]{1,0:T(8,128)(2,1)}) %reduce-scatter.15.cloned.1.call-update) | async-done | bytes 524304 | tf_op jit(solution)/shard_map/reduce_scatter | solution.py:811
  1582.5 46.3 %reduce-scatter.13.cloned.1.call-done = bf16[512,512]{1,0:T(8,128)(2,1)} async-done(((bf16[2048,512]{1,0:T(8,128)(2,1)}), bf16[512,512]{1,0:T(8,128)(2,1)}) %reduce-scatter.13.cloned.1.call-update) | async-done | bytes 524304 | tf_op jit(solution)/shard_map/reduce_scatter | solution.py:811
  1631.1 107.7 %reduce-scatter.23.cloned.1.call-done = bf16[512,1408]{1,0:T(8,128)(2,1)} async-done(((bf16[2048,1408]{1,0:T(8,128)(2,1)}), bf16[512,1408]{1,0:T(8,128)(2,1)}) %reduce-scatter.23.cloned.1.call-update) | async-done | bytes 1441808 | tf_op jit(solution)/shard_map/reduce_scatter | solution.py:811
  1742.9 115.6 %reduce-scatter.21.cloned.1.call-done = bf16[512,1408]{1,0:T(8,128)(2,1)} async-done(((bf16[2048,1408]{1,0:T(8,128)(2,1)}), bf16[512,1408]{1,0:T(8,128)(2,1)}) %reduce-scatter.21.cloned.1.call-update) | async-done | bytes 1441808 | tf_op jit(solution)/shard_map/reduce_scatter | solution.py:811
  1862.6 116.3 %reduce-scatter.19.cloned.1.call-done = bf16[512,1408]{1,0:T(8,128)(2,1)} async-done(((bf16[2048,1408]{1,0:T(8,128)(2,1)}), bf16[512,1408]{1,0:T(8,128)(2,1)}) %reduce-scatter.19.cloned.1.call-update) | async-done | bytes 1441808 | tf_op jit(solution)/shard_map/reduce_scatter | solution.py:811
  1980.8 45.0 %all-gather.30.cloned.1.call-done = bf16[3,256,2048]{2,1,0:T(8,128)(2,1)} async-done(((bf16[3,64,2048]{2,1,0:T(8,128)(2,1)}), bf16[3,256,2048]{2,1,0:T(8,128)(2,1)}) %all-gather.30.cloned.1.call-update) | async-done | bytes 3145744 | tf_op jit(solution)/shard_map/all_gather | solution.py:850
  2025.7 5.4 bitcast_convert_fusion
  2031.2 40.4 %all-gather.28.cloned.1.call-done = bf16[3,256,2048]{2,1,0:T(8,128)(2,1)} async-done(((bf16[3,64,2048]{2,1,0:T(8,128)(2,1)}), bf16[3,256,2048]{2,1,0:T(8,128)(2,1)}) %all-gather.28.cloned.1.call-update) | async-done | bytes 3145744 | tf_op jit(solution)/shard_map/all_gather | solution.py:850
  (577 shorter events, 261.4 us)
Async XLA Ops:
  7.2 189.6 %copy-start = (bf16[3,256,2048]{2,1,0:T(8,128)(2,1)S(1)}, bf16[3,256,2048]{2,1,0:T(8,128)(2,1)}, u32[]{:S(2)}) copy-start(bf16[3,256,2048]{2,1,0:T(8,128)(2,1)} %param.16) | copy-start | bytes 9437188
  7.2 199.3 %all-reduce.5.cloned.1.call-start = ((), (), s32[]{:S(2)}) async-start(), calls=%async_computation.26 | async-start | bytes 167936
  7.2 14.7 collective-permute-start.3
  14.1 6.5 collective-permute-start.1
  21.9 231.1 %all-gather.14.cloned.1.call-start = ((), (), s32[]{:S(2)}) async-start(), calls=%async_computation.9 | async-start | bytes 1310720 | tf_op jit(solution)/shard_map/all_gather | solution.py:666
  22.6 232.0 %all-gather.12.cloned.1.call-start = ((), (), s32[]{:S(2)}) async-start(), calls=%async_computation.8 | async-start | bytes 1310720 | tf_op jit(solution)/shard_map/all_gather | solution.py:666
  22.7 11.6 collective-permute-start.2
  35.0 222.0 %all-gather.16.cloned.1.call-start = ((), (), s32[]{:S(2)}) async-start(), calls=%async_computation.10 | async-start | bytes 2621440 | tf_op jit(solution)/shard_map/all_gather | solution.py:666
  35.1 16.8 collective-permute-start.4
  51.9 219.7 %all-gather.18.cloned.1.call-start = ((), (), s32[]{:S(2)}) async-start(), calls=%async_computation.11 | async-start | bytes 2621440 | tf_op jit(solution)/shard_map/all_gather | solution.py:666
  51.9 16.3 collective-permute-start.5
  68.2 255.5 %all-gather.20.cloned.1.call-start = ((), (), s32[]{:S(2)}) async-start(), calls=%async_computation.12 | async-start | bytes 2621440 | tf_op jit(solution)/shard_map/all_gather | solution.py:666
  68.3 20.1 collective-permute-start.6
  88.4 341.2 %all-gather.22.cloned.1.call-start = ((), (), s32[]{:S(2)}) async-start(), calls=%async_computation.13 | async-start | bytes 7208960 | tf_op jit(solution)/shard_map/all_gather | solution.py:666
  88.5 37.4 %collective-permute-start.7 = (bf16[512,1408]{1,0:T(8,128)(2,1)}, bf16[512,1408]{1,0:T(8,128)(2,1)}, u32[]{:S(2)}, u32[]{:S(2)}) collective-permute-start(bf16[512,1408]{1,0:T(8,128)(2,1)} %bitcast.405), channel_id=1, source_target_pairs={{0,0},{8,16},{16,8},{24,24},{1,1},{9,17},{17,9},{25,25},{2,2},{10,... | collective-permute-start | bytes 4325384 | tf_op jit(solution)/shard_map/ppermute | solution.py:662
  125.9 409.3 %all-gather.24.cloned.1.call-start = ((), (), s32[]{:S(2)}) async-start(), calls=%async_computation.14 | async-start | bytes 7208960 | tf_op jit(solution)/shard_map/all_gather | solution.py:666
  126.0 36.7 %collective-permute-start.8 = (bf16[512,1408]{1,0:T(8,128)(2,1)}, bf16[512,1408]{1,0:T(8,128)(2,1)}, u32[]{:S(2)}, u32[]{:S(2)}) collective-permute-start(bf16[512,1408]{1,0:T(8,128)(2,1)} %bitcast.406), channel_id=1, source_target_pairs={{0,0},{8,16},{16,8},{24,24},{1,1},{9,17},{17,9},{25,25},{2,2},{10,... | collective-permute-start | bytes 4325384 | tf_op jit(solution)/shard_map/ppermute | solution.py:662
  162.7 478.0 %all-gather.26.cloned.1.call-start = ((), (), s32[]{:S(2)}) async-start(), calls=%async_computation.15 | async-start | bytes 7208960 | tf_op jit(solution)/shard_map/all_gather | solution.py:666
  162.8 33.9 %collective-permute-start.9 = (bf16[512,1408]{1,0:T(8,128)(2,1)}, bf16[512,1408]{1,0:T(8,128)(2,1)}, u32[]{:S(2)}, u32[]{:S(2)}) collective-permute-start(bf16[512,1408]{1,0:T(8,128)(2,1)} %bitcast.407), channel_id=1, source_target_pairs={{0,0},{8,16},{16,8},{24,24},{1,1},{9,17},{17,9},{25,25},{2,2},{10,... | collective-permute-start | bytes 4325384 | tf_op jit(solution)/shard_map/ppermute | solution.py:662
  196.7 1315.0 %all-reduce.7.cloned.1.call-start = ((), (), s32[]{:S(2)}) async-start(), calls=%async_computation.27 | async-start | bytes 335872
  197.7 31.5 %collective-permute-start = (bf16[3,64,2048]{2,1,0:T(8,128)(2,1)}, bf16[3,64,2048]{2,1,0:T(8,128)(2,1)S(1)}, u32[]{:S(2)}, u32[]{:S(2)}) collective-permute-start(bf16[3,64,2048]{2,1,0:T(8,128)(2,1)} %constant_dynamic-slice_fusion.2), channel_id=1, source_target_pairs={{0,0},{8,16},{16,8},{24,24},{1,1},{9,17},{17,9},{25,25},{2,2},{10,... | collective-permute-start | bytes 2359304 | tf_op jit(solution)/shard_map/ppermute | solution.py:662
  204.6 36.0 %collective-permute-start.11 = (bf16[3,64,2048]{2,1,0:T(8,128)(2,1)}, bf16[3,64,2048]{2,1,0:T(8,128)(2,1)S(1)}, u32[]{:S(2)}, u32[]{:S(2)}) collective-permute-start(bf16[3,64,2048]{2,1,0:T(8,128)(2,1)} %constant_dynamic-slice_fusion.1), channel_id=1, source_target_pairs={{0,0},{8,16},{16,8},{24,24},{1,1},{9,17},{17,9},{25,25},{2,2},{10,... | collective-permute-start | bytes 2359304 | tf_op jit(solution)/shard_map/ppermute | solution.py:662
  208.1 43.2 %copy-start.114 = (bf16[2048,16]{1,0:T(8,128)(2,1)}, bf16[2048,16]{1,0:T(8,128)(2,1)S(1)}, u32[]{:S(2)}) copy-start(bf16[2048,16]{1,0:T(8,128)(2,1)S(1)} %reshape.260) | copy-start | bytes 196612
  208.2 43.5 %copy-start.131 = (bf16[256,16]{1,0:T(8,128)(2,1)}, bf16[256,16]{1,0:T(8,128)(2,1)S(1)}, u32[]{:S(2)}) copy-start(bf16[256,16]{1,0:T(8,128)(2,1)S(1)} %reshape.261) | copy-start | bytes 24580
  208.3 43.4 %copy-start.148 = (f32[256]{0:T(256)}, f32[256]{0:T(256)S(1)}, u32[]{:S(2)}) copy-start(f32[256]{0:T(256)S(1)} %reshape.305) | copy-start | bytes 3076
  240.5 31.1 %copy-start.2 = (bf16[4,64,2048]{2,1,0:T(8,128)(2,1)}, bf16[4,64,2048]{2,1,0:T(8,128)(2,1)S(1)}, u32[]{:S(2)}) copy-start(bf16[4,64,2048]{2,1,0:T(8,128)(2,1)S(1)} %shard_map.279) | copy-start | bytes 3145732
  259.3 36.1 %copy-start.18 = (bf16[256,512]{1,0:T(8,128)(2,1)}, bf16[256,512]{1,0:T(8,128)(2,1)S(1)}, u32[]{:S(2)}) copy-start(bf16[256,512]{1,0:T(8,128)(2,1)S(1)} %convolution_convert_fusion.10.v_ref) | copy-start | bytes 786436
  274.0 49.7 %copy-start.8 = (f32[256,512]{1,0:T(8,128)}, f32[256,512]{1,0:T(8,128)S(1)}, u32[]{:S(2)}) copy-start(f32[256,512]{1,0:T(8,128)S(1)} %fusion.139.og_ref) | copy-start | bytes 1572868
  298.0 28.0 %copy-start.30 = (bf16[256,512]{1,0:T(8,128)(2,1)}, bf16[256,512]{1,0:T(8,128)(2,1)S(1)}, u32[]{:S(2)}) copy-start(bf16[256,512]{1,0:T(8,128)(2,1)S(1)} %get-tuple-element.99) | copy-start | bytes 786436
  356.8 178.4 %copy-start.95 = (bf16[4,64,2048]{2,1,0:T(8,128)(2,1)}, bf16[4,64,2048]{2,1,0:T(8,128)(2,1)S(1)}, u32[]{:S(2)}) copy-start(bf16[4,64,2048]{2,1,0:T(8,128)(2,1)S(1)} %get-tuple-element.100) | copy-start | bytes 3145732
  541.1 104.1 %copy-start.154 = (bf16[256,1408]{1,0:T(8,128)(2,1)}, bf16[256,1408]{1,0:T(8,128)(2,1)S(1)}, u32[]{:S(2)}) copy-start(bf16[256,1408]{1,0:T(8,128)(2,1)S(1)} %get-tuple-element.245) | copy-start | bytes 2162692
  645.3 41.3 %copy-start.115 = (bf16[2048,16]{1,0:T(8,128)(2,1)S(1)}, bf16[2048,16]{1,0:T(8,128)(2,1)}, u32[]{:S(2)}) copy-start(bf16[2048,16]{1,0:T(8,128)(2,1)} %copy-done.114) | copy-start | bytes 196612
  645.3 41.6 %copy-start.132 = (bf16[256,16]{1,0:T(8,128)(2,1)S(1)}, bf16[256,16]{1,0:T(8,128)(2,1)}, u32[]{:S(2)}) copy-start(bf16[256,16]{1,0:T(8,128)(2,1)} %copy-done.131) | copy-start | bytes 24580
  645.3 41.6 %copy-start.149 = (f32[256]{0:T(256)S(1)}, f32[256]{0:T(256)}, u32[]{:S(2)}) copy-start(f32[256]{0:T(256)} %copy-done.148) | copy-start | bytes 3076
  645.3 42.1 %copy-start.120 = (bf16[2048,512]{1,0:T(8,128)(2,1)S(1)}, bf16[2048,512]{1,0:T(8,128)(2,1)}, u32[]{:S(2)}) copy-start(bf16[2048,512]{1,0:T(8,128)(2,1)} %all-gather.18.cloned.1.call-done) | copy-start | bytes 6291460
  707.5 34.4 %slice-start.6 = ((s8[5767168]{0:T(1024)(128)(4,1)}), s8[1572864]{0:T(1024)(128)(4,1)S(1)}, s32[]{:S(2)}) async-start(s8[5767168]{0:T(1024)(128)(4,1)} %bitcast.401), calls=%async_computation.34 | async-start | bytes 3145728
  803.6 38.3 %copy-start.33 = (bf16[256,512]{1,0:T(8,128)(2,1)}, bf16[256,512]{1,0:T(8,128)(2,1)S(1)}, u32[]{:S(2)}) copy-start(bf16[256,512]{1,0:T(8,128)(2,1)S(1)} %get-tuple-element.110) | copy-start | bytes 786436
  891.5 430.8 %copy-start.4 = (bf16[4,64,2048]{2,1,0:T(8,128)(2,1)}, bf16[4,64,2048]{2,1,0:T(8,128)(2,1)S(1)}, u32[]{:S(2)}) copy-start(bf16[4,64,2048]{2,1,0:T(8,128)(2,1)S(1)} %get-tuple-element.115) | copy-start | bytes 3145732
  1018.2 36.5 %slice-start.8 = ((s8[5767168]{0:T(1024)(128)(4,1)}), s8[1572864]{0:T(1024)(128)(4,1)S(1)}, s32[]{:S(2)}) async-start(s8[5767168]{0:T(1024)(128)(4,1)} %bitcast.403), calls=%async_computation.36 | async-start | bytes 3145728
  1113.3 39.7 %copy-start.163 = (f32[256,1408]{1,0:T(8,128)S(1)}, f32[256,1408]{1,0:T(8,128)}, u32[]{:S(2)}) copy-start(f32[256,1408]{1,0:T(8,128)} %copy-done.162) | copy-start | bytes 4325380
  1218.8 42.3 %copy-start.161 = (f32[256,1408]{1,0:T(8,128)S(1)}, f32[256,1408]{1,0:T(8,128)}, u32[]{:S(2)}) copy-start(f32[256,1408]{1,0:T(8,128)} %fusion.142) | copy-start | bytes 4325380
  1218.8 42.3 %copy-start.165 = (f32[256,1408]{1,0:T(8,128)S(1)}, f32[256,1408]{1,0:T(8,128)}, u32[]{:S(2)}) copy-start(f32[256,1408]{1,0:T(8,128)} %get-tuple-element.246) | copy-start | bytes 4325380
  1275.8 27.7 %copy-start.128 = (bf16[2048,512]{1,0:T(8,128)(2,1)S(1)}, bf16[2048,512]{1,0:T(8,128)(2,1)}, u32[]{:S(2)}) copy-start(bf16[2048,512]{1,0:T(8,128)(2,1)} %all-gather.20.cloned.1.call-done) | copy-start | bytes 6291460
  1358.4 178.2 %reduce-scatter.11.cloned.1.call-start = ((), (), s32[]{:S(2)}) async-start(), calls=%async_computation.19 | async-start | bytes 1310720 | tf_op jit(solution)/shard_map/reduce_scatter | solution.py:811
  1362.1 176.9 %reduce-scatter.9.cloned.1.call-start = ((), (), s32[]{:S(2)}) async-start(), calls=%async_computation.18 | async-start | bytes 1310720 | tf_op jit(solution)/shard_map/reduce_scatter | solution.py:811
  1365.8 177.7 %reduce-scatter.17.cloned.1.call-start = ((), (), s32[]{:S(2)}) async-start(), calls=%async_computation.22 | async-start | bytes 2621440 | tf_op jit(solution)/shard_map/reduce_scatter | solution.py:811
  1372.0 206.8 %reduce-scatter.15.cloned.1.call-start = ((), (), s32[]{:S(2)}) async-start(), calls=%async_computation.21 | async-start | bytes 2621440 | tf_op jit(solution)/shard_map/reduce_scatter | solution.py:811
  1378.0 250.8 %reduce-scatter.13.cloned.1.call-start = ((), (), s32[]{:S(2)}) async-start(), calls=%async_computation.20 | async-start | bytes 2621440 | tf_op jit(solution)/shard_map/reduce_scatter | solution.py:811
  1384.1 354.6 %reduce-scatter.23.cloned.1.call-start = ((), (), s32[]{:S(2)}) async-start(), calls=%async_computation.25 | async-start | bytes 7208960 | tf_op jit(solution)/shard_map/reduce_scatter | solution.py:811
  1397.4 461.1 %reduce-scatter.21.cloned.1.call-start = ((), (), s32[]{:S(2)}) async-start(), calls=%async_computation.24 | async-start | bytes 7208960 | tf_op jit(solution)/shard_map/reduce_scatter | solution.py:811
  1410.5 568.4 %reduce-scatter.19.cloned.1.call-start = ((), (), s32[]{:S(2)}) async-start(), calls=%async_computation.23 | async-start | bytes 7208960 | tf_op jit(solution)/shard_map/reduce_scatter | solution.py:811
  1422.2 603.5 %all-gather.30.cloned.1.call-start = ((), (), s32[]{:S(2)}) async-start(), calls=%async_computation.17 | async-start | bytes 3932160 | tf_op jit(solution)/shard_map/all_gather | solution.py:850
  1423.5 40.0 %collective-permute-start.12 = (bf16[3,64,2048]{2,1,0:T(8,128)(2,1)S(1)}, bf16[3,64,2048]{2,1,0:T(8,128)(2,1)S(1)}, u32[]{:S(2)}, u32[]{:S(2)}) collective-permute-start(bf16[3,64,2048]{2,1,0:T(8,128)(2,1)S(1)} %maximum_select_fusion.1), channel_id=1, source_target_pairs={{0,0},{8,16},{16,8},{24,24},{1,1},{9,17},{17,9},{25,25},{2,2},{10,... | collective-permute-start | bytes 2359304 | tf_op jit(solution)/shard_map/ppermute | solution.py:662
  1464.4 607.1 %all-gather.28.cloned.1.call-start = ((), (), s32[]{:S(2)}) async-start(), calls=%async_computation.16 | async-start | bytes 3932160 | tf_op jit(solution)/shard_map/all_gather | solution.py:850
  1480.6 30.1 %collective-permute-start.10 = (bf16[3,64,2048]{2,1,0:T(8,128)(2,1)S(1)}, bf16[3,64,2048]{2,1,0:T(8,128)(2,1)S(1)}, u32[]{:S(2)}, u32[]{:S(2)}) collective-permute-start(bf16[3,64,2048]{2,1,0:T(8,128)(2,1)S(1)} %maximum_select_fusion), channel_id=1, source_target_pairs={{0,0},{8,16},{16,8},{24,24},{1,1},{9,17},{17,9},{25,25},{2,2},{10,... | collective-permute-start | bytes 2359304 | tf_op jit(solution)/shard_map/ppermute | solution.py:662
  1513.4 6.7 collective-permute-start.18
  1536.5 44.3 %collective-permute-start.14 = (bf16[512,256]{1,0:T(8,128)(2,1)}, bf16[512,256]{1,0:T(8,128)(2,1)S(1)}, u32[]{:S(2)}, u32[]{:S(2)}) collective-permute-start(bf16[512,256]{1,0:T(8,128)(2,1)} %reduce-scatter.11.cloned.1.call-done), channel_id=1, source_target_pairs={{0,0},{8,16},{16,8},{24,24},{1,1},{9,17},{17,9},{25,25},{2,2},{10,... | collective-permute-start | bytes 786440 | tf_op jit(solution)/shard_map/ppermute | solution.py:662
  1539.0 42.7 %collective-permute-start.13 = (bf16[512,256]{1,0:T(8,128)(2,1)}, bf16[512,256]{1,0:T(8,128)(2,1)S(1)}, u32[]{:S(2)}, u32[]{:S(2)}) collective-permute-start(bf16[512,256]{1,0:T(8,128)(2,1)} %reduce-scatter.9.cloned.1.call-done), channel_id=1, source_target_pairs={{0,0},{8,16},{16,8},{24,24},{1,1},{9,17},{17,9},{25,25},{2,2},{10,... | collective-permute-start | bytes 786440 | tf_op jit(solution)/shard_map/ppermute | solution.py:662
  1543.5 197.1 %collective-permute-start.17 = (bf16[512,512]{1,0:T(8,128)(2,1)}, bf16[512,512]{1,0:T(8,128)(2,1)S(1)}, u32[]{:S(2)}, u32[]{:S(2)}) collective-permute-start(bf16[512,512]{1,0:T(8,128)(2,1)} %reduce-scatter.17.cloned.1.call-done), channel_id=1, source_target_pairs={{0,0},{8,16},{16,8},{24,24},{1,1},{9,17},{17,9},{25,25},{2,2},{10,... | collective-permute-start | bytes 1572872 | tf_op jit(solution)/shard_map/ppermute | solution.py:662
  1578.8 163.0 %collective-permute-start.16 = (bf16[512,512]{1,0:T(8,128)(2,1)}, bf16[512,512]{1,0:T(8,128)(2,1)S(1)}, u32[]{:S(2)}, u32[]{:S(2)}) collective-permute-start(bf16[512,512]{1,0:T(8,128)(2,1)} %reduce-scatter.15.cloned.1.call-done), channel_id=1, source_target_pairs={{0,0},{8,16},{16,8},{24,24},{1,1},{9,17},{17,9},{25,25},{2,2},{10,... | collective-permute-start | bytes 1572872 | tf_op jit(solution)/shard_map/ppermute | solution.py:662
  1628.8 231.6 %collective-permute-start.15 = (bf16[512,512]{1,0:T(8,128)(2,1)}, bf16[512,512]{1,0:T(8,128)(2,1)}, u32[]{:S(2)}, u32[]{:S(2)}) collective-permute-start(bf16[512,512]{1,0:T(8,128)(2,1)} %reduce-scatter.13.cloned.1.call-done), channel_id=1, source_target_pairs={{0,0},{8,16},{16,8},{24,24},{1,1},{9,17},{17,9},{25,25},{2,2},{10,... | collective-permute-start | bytes 1572872 | tf_op jit(solution)/shard_map/ppermute | solution.py:662
  1738.8 332.8 %collective-permute-start.21 = (bf16[512,1408]{1,0:T(8,128)(2,1)}, bf16[512,1408]{1,0:T(8,128)(2,1)S(1)}, u32[]{:S(2)}, u32[]{:S(2)}) collective-permute-start(bf16[512,1408]{1,0:T(8,128)(2,1)} %reduce-scatter.23.cloned.1.call-done), channel_id=1, source_target_pairs={{0,0},{8,16},{16,8},{24,24},{1,1},{9,17},{17,9},{25,25},{2,2},{10,... | collective-permute-start | bytes 4325384 | tf_op jit(solution)/shard_map/ppermute | solution.py:662
  1858.5 214.9 %collective-permute-start.20 = (bf16[512,1408]{1,0:T(8,128)(2,1)}, bf16[512,1408]{1,0:T(8,128)(2,1)S(1)}, u32[]{:S(2)}, u32[]{:S(2)}) collective-permute-start(bf16[512,1408]{1,0:T(8,128)(2,1)} %reduce-scatter.21.cloned.1.call-done), channel_id=1, source_target_pairs={{0,0},{8,16},{16,8},{24,24},{1,1},{9,17},{17,9},{25,25},{2,2},{10,... | collective-permute-start | bytes 4325384 | tf_op jit(solution)/shard_map/ppermute | solution.py:662
  1978.8 96.3 %collective-permute-start.19 = (bf16[512,1408]{1,0:T(8,128)(2,1)}, bf16[512,1408]{1,0:T(8,128)(2,1)}, u32[]{:S(2)}, u32[]{:S(2)}) collective-permute-start(bf16[512,1408]{1,0:T(8,128)(2,1)} %reduce-scatter.19.cloned.1.call-done), channel_id=1, source_target_pairs={{0,0},{8,16},{16,8},{24,24},{1,1},{9,17},{17,9},{25,25},{2,2},{10,... | collective-permute-start | bytes 4325384 | tf_op jit(solution)/shard_map/ppermute | solution.py:662
  (154 other events, 804.5 us)
Sparse Core Ops, SparseCore 0:
  22.0 36.0 all-reduce.4
  60.3 32.1 all-gather.13
  94.7 42.2 all-gather.11
  138.5 79.2 all-gather.15
  219.4 52.2 all-gather.17
  273.1 50.5 all-gather.19
  325.3 104.2 all-gather.21
  431.3 103.8 all-gather.23
  536.8 103.8 all-gather.25
  1358.5 43.8 all-reduce.6
  1405.2 25.5 reduce-scatter.10
  1433.7 33.5 reduce-scatter.8
  1470.2 51.7 reduce-scatter.16
  1524.8 53.9 reduce-scatter.14
  1581.5 47.2 reduce-scatter.12
  1631.1 107.5 reduce-scatter.22
  1741.0 117.4 reduce-scatter.20
  1861.3 117.4 reduce-scatter.18
  1980.8 44.8 all-gather.29
  2027.6 43.9 all-gather.27

commit v2 on v1

v2 whole, which is shorter than its diff:
```python
from functools import partial

import jax
import jax.numpy as jnp
from jax import lax
from jax.experimental import pallas as pl
from jax.experimental.pallas import tpu as pltpu
from jax.sharding import Mesh
from jax.sharding import PartitionSpec as P

SPAN = 64
LANES = 128
STRIP = 64
CHUNKS = 2
DIRECT, SUMMED, PASSED = 0, 1, 2
WINDOW = 2

HIGH = lax.Precision.HIGHEST
MODEL_EPS = 1e-06
HEAD_EPS = 1e-05
GATE_SCALE = 16.0

f32 = jnp.float32
bf16 = jnp.bfloat16
GROUP = ("section", "q")


def dot_plain(left, right):
    return jnp.dot(left, right, preferred_element_type=f32)


def dot_left(left, right):
    return lax.dot_general(left, right, (((0,), (0,)), ((), ())), preferred_element_type=f32)


def dot_right(left, right):
    return lax.dot_general(left, right, (((1,), (1,)), ((), ())), preferred_element_type=f32)


def head_output(inner, out_gate, gain):
    r = lax.rsqrt(jnp.mean(inner * inner, axis=-1, keepdims=True) + HEAD_EPS)
    return gain * inner * r * jax.nn.silu(out_gate)


def normed_rows(u, gain):
    return gain * u * lax.rsqrt(jnp.mean(u * u, axis=-1, keepdims=True) + MODEL_EPS)


def norm_back(d, u, gain):
    s = lax.rsqrt(jnp.mean(u * u, axis=-1, keepdims=True) + MODEL_EPS)
    w = gain * d
    d_u = s * w - u * (s * s * s) * jnp.mean(w * u, axis=-1, keepdims=True)
    return d_u, jnp.sum(d * u * s, axis=0, keepdims=True)


def greet(signals, waits, extra=None):
    if extra is not None:
        signals, waits = {**extra.signals, **signals}, {**extra.waits, **waits}
    barrier = pltpu.get_barrier_semaphore()
    for condition, device in signals.values():
        if condition is None:
            pl.semaphore_signal(barrier, inc=1, device_id=device)
        else:

            @pl.when(condition)
            def _():
                pl.semaphore_signal(barrier, inc=1, device_id=device)

    due = sum(1 for condition in waits.values() if condition is None)
    for condition in waits.values():
        if condition is not None:
            due = due + condition.astype(jnp.int32)
    pl.semaphore_wait(barrier, due)


class Peers:
    def __init__(self, peers):
        assert peers == 4, peers
        self.peers = peers
        self.me = lax.axis_index("tensor")
        low, high = lax.rem(self.me, 2), self.me // 2
        self.beside = (high * 2 + 1 - low, (1 - high) * 2 + low)
        self.opposite = 3 - self.me

    def at(self, d):
        return lax.rem(self.me + d, self.peers)

    def enter(self, relay_to=None, extra=None):
        signals = {("tensor", d): (None, {"tensor": self.at(d)}) for d in range(1, self.peers)}
        waits = dict.fromkeys(signals)
        if relay_to is not None:
            stage = lax.axis_index("stage")
            signals["stage"] = (stage == relay_to, {"stage": 1 - relay_to})
            waits["stage"] = stage != relay_to
        greet(signals, waits, extra)


class Sum:
    def __init__(self, peers, part, send, land, sems, fine=None, fine_sems=None):
        self.peers, self.part, self.send, self.land, self.sems = peers, part, send, land, sems
        self.fine, self.fine_sems = fine, fine_sems
        self.pieces = part.shape[2] // LANES
        self.step = part.shape[1] // CHUNKS

    def rows(self, c):
        return slice(c * self.step, (c + 1) * self.step)

    def copy(self, kind, c):
        target = self.peers.beside[1 - c if kind == SUMMED else c]
        return pltpu.make_async_remote_copy(
            src_ref=self.send.at[kind, c],
            dst_ref=self.land.at[kind, c],
            send_sem=self.sems.at[0, kind, c],
            recv_sem=self.sems.at[1, kind, c],
            device_id={"tensor": target},
        )

    def fine_copy(self, d):
        return pltpu.make_async_remote_copy(
            src_ref=self.fine.at[0],
            dst_ref=self.fine.at[d],
            send_sem=self.fine_sems.at[0, d - 1],
            recv_sem=self.fine_sems.at[1, d - 1],
            device_id={"tensor": 0},
        )

    def lanes(self, n):
        return slice(n * LANES, (n + 1) * LANES)

    def start(self):
        peers = self.peers
        for c in range(CHUNKS):
            self.send[PASSED, c] = self.part[peers.opposite, self.rows(c), :].astype(bf16)
            self.copy(PASSED, c).start()
        for c in range(CHUNKS):
            self.send[DIRECT, c] = self.part[peers.beside[c], self.rows(c), :].astype(bf16)
            self.copy(DIRECT, c).start()
        if self.fine is not None:
            for n in range(self.pieces):
                self.fine[0, n : n + 1, :] = self.part[0, 0:1, self.lanes(n)]
            for d in range(1, peers.peers):

                @pl.when(peers.at(d) == 0)
                def _():
                    self.fine_copy(d).start()

        for c in range(CHUNKS):
            self.copy(PASSED, c).wait_recv()
            own = self.part[peers.beside[1 - c], self.rows(c), :].astype(f32)
            self.send[SUMMED, c] = (own + self.land[PASSED, c].astype(f32)).astype(bf16)
            self.copy(SUMMED, c).start()

    def finish(self, c, total):
        self.copy(DIRECT, c).wait_recv()
        acc = self.part[self.peers.me, self.rows(c), :].astype(f32)
        acc = acc + self.land[DIRECT, c].astype(f32)
        self.copy(SUMMED, c).wait_recv()
        total[self.rows(c), :] = acc + self.land[SUMMED, c].astype(f32)
        if c == 0 and self.fine is not None:

            @pl.when(self.peers.me == 0)
            def _():
                top = self.fine[0]
                for d in range(1, self.peers.peers):
                    self.fine_copy(d).wait_recv()
                    top = top + self.fine[d]
                for n in range(self.pieces):
                    total[0:1, self.lanes(n)] = top[n : n + 1, :]

        return total[self.rows(c), :]

    def drain(self):
        for c in range(CHUNKS):
            for kind in (PASSED, DIRECT, SUMMED):
                self.copy(kind, c).wait_send()
        if self.fine is not None:
            for d in range(1, self.peers.peers):

                @pl.when(self.peers.at(d) == 0)
                def _():
                    self.fine_copy(d).wait_send()


class Share:
    def __init__(self, peers, full, sems):
        self.peers, self.full, self.sems = peers, full, sems
        self.step = full.shape[1] // CHUNKS

    def copy(self, kind, c):
        peers = self.peers
        if kind == PASSED:
            source, target = peers.beside[c], peers.beside[1 - c]
        else:
            source, target = peers.me, peers.beside[kind]
        block = self.full.at[source, pl.ds(c * self.step, self.step)]
        return pltpu.make_async_remote_copy(
            src_ref=block,
            dst_ref=block,
            send_sem=self.sems.at[0, kind, c],
            recv_sem=self.sems.at[1, kind, c],
            device_id={"tensor": target},
        )

    def start(self, c, value):
        self.full[self.peers.me, c * self.step : (c + 1) * self.step, :] = value
        for kind in range(2):
            self.copy(kind, c).start()

    def finish(self):
        for c in range(CHUNKS):
            self.copy(c, c).wait_recv()
            self.copy(PASSED, c).start()
        for c in range(CHUNKS):
            self.copy(1 - c, c).wait_recv()
            self.copy(PASSED, c).wait_recv()
            for kind in range(3):
                self.copy(kind, c).wait_send()


def relay_rows(src, land, sems, c, relay_to):
    step = src.shape[0] // CHUNKS
    rows = pl.ds(c * step, step)
    return pltpu.make_async_remote_copy(
        src_ref=src.at[rows],
        dst_ref=land.at[rows],
        send_sem=sems.at[0, c],
        recv_sem=sems.at[1, c],
        device_id={"stage": relay_to},
    )


def first_kernel(peers_n, h, gain, full, share_sems, extra=None):
    peers = Peers(peers_n)
    peers.enter(extra=extra)
    if extra is not None:
        extra.start()
    share = Share(peers, full, share_sems)
    for c in range(CHUNKS):
        rows = slice(c * share.step, (c + 1) * share.step)
        share.start(c, normed_rows(h[rows, :].astype(f32), gain[...]).astype(bf16))
    share.finish()
    if extra is not None:
        extra.finish()


def forward_mid_kernel(
    peers_n, part, h, gain, middle, full, send, land, fine, total, sems, fine_sems, share_sems, extra=None):
    peers = Peers(peers_n)
    peers.enter(extra=extra)
    if extra is not None:
        extra.start()
    reduced = Sum(peers, part, send, land, sems, fine, fine_sems)
    share = Share(peers, full, share_sems)
    reduced.start()
    for c in range(CHUNKS):
        rows = reduced.rows(c)
        value = h[rows, :].astype(f32) + reduced.finish(c, total)
        middle[rows, :] = value
        share.start(c, normed_rows(value, gain[...]).astype(bf16))
    share.finish()
    reduced.drain()
    if extra is not None:
        extra.finish()


def forward_end_kernel(
    peers_n,
    part,
    middle,
    gain,
    own,
    y,
    h,
    full,
    send,
    land,
    fine,
    total,
    relayed,
    sems,
    fine_sems,
    share_sems,
    relay_sems,
):
    peers = Peers(peers_n)
    stage = lax.axis_index("stage")
    peers.enter(1)
    reduced = Sum(peers, part, send, land, sems, fine, fine_sems)
    share = Share(peers, full, share_sems)
    reduced.start()
    for c in range(CHUNKS):
        rows = reduced.rows(c)
        relay = relay_rows(y, relayed, relay_sems, c, 1)

        @pl.when(stage == 0)
        def _():
            y[rows, :] = (middle[rows, :] + reduced.finish(c, total)).astype(bf16)
            relay.start()
            h[rows, :] = own[rows, :]

        @pl.when(stage == 1)
        def _():
            y[rows, :] = (middle[rows, :] + reduced.finish(c, total)).astype(bf16)
            relay.wait_recv()
            h[rows, :] = relayed[rows, :]

        share.start(c, normed_rows(h[rows, :].astype(f32), gain[...]).astype(bf16))

    share.finish()

    @pl.when(stage == 0)
    def _():
        for c in range(CHUNKS):
            relay_rows(y, relayed, relay_sems, c, 1).wait_send()
    reduced.drain()


def forward_last_kernel(
    peers_n, part, middle, gy, y, full, send, land, fine, total, sems, fine_sems, share_sems
):
    peers = Peers(peers_n)
    peers.enter()
    reduced = Sum(peers, part, send, land, sems, fine, fine_sems)
    share = Share(peers, full, share_sems)
    reduced.start()
    for c in range(CHUNKS):
        share.start(c, gy[reduced.rows(c), :])
    for c in range(CHUNKS):
        rows = reduced.rows(c)
        y[rows, :] = (middle[rows, :] + reduced.finish(c, total)).astype(bf16)
    share.finish()
    reduced.drain()


def backward_mid_kernel(
    peers_n, part, gy, middle, gain, d_middle, gain_part, full, send, land, total, sems, share_sems, extra=None):
    peers = Peers(peers_n)
    peers.enter(extra=extra)
    if extra is not None:
        extra.start()
    reduced = Sum(peers, part, send, land, sems)
    share = Share(peers, full, share_sems)
    reduced.start()
    gains = jnp.zeros(gain_part.shape, f32)
    for c in range(CHUNKS):
        rows = reduced.rows(c)
        d_u, g = norm_back(reduced.finish(c, total), middle[rows, :], gain[...])
        value = gy[rows, :].astype(f32) + d_u
        d_middle[rows, :] = value
        gains = gains + g
        share.start(c, value.astype(bf16))
    gain_part[...] = gains
    share.finish()
    reduced.drain()
    if extra is not None:
        extra.finish()


def backward_end_kernel(
    peers_n,
    part,
    d_middle,
    h,
    gain,
    own,
    grad,
    gain_part,
    gy,
    full,
    send,
    land,
    total,
    relayed,
    sems,
    share_sems,
    relay_sems,
    extra=None,
):
    peers = Peers(peers_n)
    stage = lax.axis_index("stage")
    peers.enter(0, extra)
    reduced = Sum(peers, part, send, land, sems)
    share = Share(peers, full, share_sems)
    reduced.start()
    if extra is not None:
        extra.start()
    gain_part[...] = jnp.zeros(gain_part.shape, f32)

    def finish(c):
        rows = reduced.rows(c)
        d_u, g = norm_back(reduced.finish(c, total), h[rows, :].astype(f32), gain[...])
        grad[rows, :] = (d_middle[rows, :] + d_u).astype(bf16)
        gain_part[...] += g

    for c in range(CHUNKS):
        rows = reduced.rows(c)
        relay = relay_rows(grad, relayed, relay_sems, c, 0)

        @pl.when(stage == 1)
        def _():
            finish(c)
            relay.start()
            gy[rows, :] = own[rows, :]

        @pl.when(stage == 0)
        def _():
            finish(c)
            relay.wait_recv()
            gy[rows, :] = relayed[rows, :]

        share.start(c, gy[rows, :])

    share.finish()

    @pl.when(stage == 1)
    def _():
        for c in range(CHUNKS):
            relay_rows(grad, relayed, relay_sems, c, 0).wait_send()
    reduced.drain()
    if extra is not None:
        extra.finish()


def backward_last_kernel(
    peers_n, part, d_middle, h, gain, grad, gain_part, send, land, total, sems, extra=None):
    peers = Peers(peers_n)
    peers.enter(extra=extra)
    if extra is not None:
        extra.start()
    reduced = Sum(peers, part, send, land, sems)
    reduced.start()
    gains = jnp.zeros(gain_part.shape, f32)
    for c in range(CHUNKS):
        rows = reduced.rows(c)
        d_u, g = norm_back(reduced.finish(c, total), h[rows, :].astype(f32), gain[...])
        grad[rows, :] = (d_middle[rows, :] + d_u).astype(bf16)
        gains = gains + g
    gain_part[...] = gains
    reduced.drain()
    if extra is not None:
        extra.finish()


def in_vmem(count):
    return [pl.BlockSpec(memory_space=pltpu.VMEM)] * count


def kernel_call(body, outs, scratch, ident, *args, extra=None):
    outs = outs if isinstance(outs, list) else [outs]
    in_specs, out_specs = in_vmem(len(args)), in_vmem(len(outs))
    if extra is not None:
        kind, more_args, more_outs, more_scratch = extra
        sizes = [len(args), len(more_args), len(outs), len(more_outs), len(scratch)]
        own_body = body

        def body(*refs):
            cuts = [sum(sizes[:n]) for n in range(len(sizes) + 1)]
            parts = [refs[cuts[n] : cuts[n + 1]] for n in range(len(sizes))] + [refs[cuts[-1] :]]
            own_body(
                *parts[0], *parts[2], *parts[4], extra=kind(*parts[1], *parts[3], *parts[5])
            )

        anywhere = pl.BlockSpec(memory_space=pl.ANY)
        args, outs = args + tuple(more_args), outs + more_outs
        scratch = scratch + more_scratch
        in_specs = in_specs + [anywhere] * len(more_args)
        out_specs = out_specs + [anywhere] * len(more_outs)
    results = pl.pallas_call(
        body,
        out_shape=outs,
        in_specs=in_specs,
        out_specs=out_specs,
        scratch_shapes=scratch,
        compiler_params=pltpu.CompilerParams(
            collective_id=ident, has_side_effects=True, vmem_limit_bytes=40 * 1024 * 1024
        ),
    )(*args)
    return results[0] if len(results) == 1 else list(results)


def shape(dims, kind):
    return jax.ShapeDtypeStruct(dims, kind)


class Rows:
    def __init__(self, rows, width, peers):
        self.rows, self.width, self.peers = rows, width, peers
        self.slice_b = shape((rows, width), bf16)
        self.slice_f = shape((rows, width), f32)
        self.gain_f = shape((1, width), f32)
        self.full = shape((peers, rows, width), bf16)
        self.pair = pltpu.SemaphoreType.DMA((2, peers - 1))
        self.many = pltpu.SemaphoreType.DMA((2, 3, CHUNKS))
        self.reduce = [
            pltpu.VMEM((3, CHUNKS, rows // CHUNKS, width), bf16),
            pltpu.VMEM((3, CHUNKS, rows // CHUNKS, width), bf16),
        ]
        self.fine = [pltpu.VMEM((peers, width // LANES, LANES), f32)]
        self.total = [pltpu.VMEM((rows, width), f32)]
        self.relayed = [pltpu.VMEM((rows, width), bf16)]
        self.relay = pltpu.SemaphoreType.DMA((2, CHUNKS))

    def parts(self, part):
        return part.reshape(self.peers, self.rows, self.width)

    def flat(self, full):
        return full.reshape(self.peers * self.rows, self.width)

    def first(self, h, gain, extra):
        body = partial(first_kernel, self.peers)
        full, *more = kernel_call(body, self.full, [self.many], 1, h, gain, extra=extra)
        return self.flat(full), *more

    def forward_mid(self, part, h, gain, ident=3, extra=None):
        middle, full, *more = kernel_call(
            partial(forward_mid_kernel, self.peers),
            [self.slice_f, self.full],
            self.reduce + self.fine + self.total + [self.many, self.pair, self.many],
            ident,
            self.parts(part),
            h,
            gain,
            extra=extra,
        )
        return middle, self.flat(full), *more

    def forward_end(self, part, middle, gain, own):
        y, h, full = kernel_call(
            partial(forward_end_kernel, self.peers),
            [self.slice_b, self.slice_b, self.full],
            self.reduce
            + self.fine
            + self.total
            + self.relayed
            + [self.many, self.pair, self.many, self.relay],
            4,
            self.parts(part),
            middle,
            gain,
            own,
        )
        return y, h, self.flat(full)

    def forward_last(self, part, middle, gy):
        y, full = kernel_call(
            partial(forward_last_kernel, self.peers),
            [self.slice_b, self.full],
            self.reduce + self.fine + self.total + [self.many, self.pair, self.many],
            5,
            self.parts(part),
            middle,
            gy,
        )
        return y, self.flat(full)

    def backward_mid(self, part, gy, middle, gain, ident=6, extra=None):
        d_middle, gain_part, full, *more = kernel_call(
            partial(backward_mid_kernel, self.peers),
            [self.slice_f, self.gain_f, self.full],
            self.reduce + self.total + [self.many] * 2,
            ident,
            self.parts(part),
            gy,
            middle,
            gain,
            extra=extra,
        )
        return d_middle, gain_part, self.flat(full), *more

    def backward_end(self, part, d_middle, h, gain, own, ident=7, extra=None):
        grad, gain_part, gy, full, *more = kernel_call(
            partial(backward_end_kernel, self.peers),
            [self.slice_b, self.gain_f, self.slice_b, self.full],
            self.reduce + self.total + self.relayed + [self.many] * 2 + [self.relay],
            ident,
            self.parts(part),
            d_middle,
            h,
            gain,
            own,
            extra=extra,
        )
        return grad, gain_part, gy, self.flat(full), *more

    def backward_last(self, part, d_middle, h, gain, extra=None):
        return kernel_call(
            partial(backward_last_kernel, self.peers),
            [self.slice_b, self.gain_f],
            self.reduce + self.total + [self.many],
            8,
            self.parts(part),
            d_middle,
            h,
            gain,
            extra=extra,
        )


PAD = 16


class Chain:
    def __init__(self, ranges, half):
        self.ranges, self.half = ranges, half
        self.s, self.q = lax.axis_index("section"), lax.axis_index("q")
        self.me = self.s * half + self.q

    def after(self, d):
        return lax.rem(self.q + d, self.half)

    def before(self, d):
        return self.s * self.half + lax.rem(self.q + self.half - d, self.half)

    def enter(self, extra=None):
        signals = {("q", d): (None, {"q": self.after(d)}) for d in range(1, self.half)}
        signals["core"] = (None, {"section": 1 - self.s})
        greet(signals, dict.fromkeys(signals), extra)

    def along(self, land, sems, d):
        return pltpu.make_async_remote_copy(
            src_ref=land.at[self.me],
            dst_ref=land.at[self.me],
            send_sem=sems.at[0, d],
            recv_sem=sems.at[1, d],
            device_id={"q": self.after(d)},
        )

    def across(self, land, sems, d):
        return pltpu.make_async_remote_copy(
            src_ref=land.at[self.before(d)],
            dst_ref=land.at[self.before(d)],
            send_sem=sems.at[2, d],
            recv_sem=sems.at[3, d],
            device_id={"section": 1 - self.s},
        )

    def start(self, land, sems, state, through):
        high = state.shape[0]
        land[self.me, 0:high, :] = state.astype(bf16)
        land[self.me, high : high + PAD, :] = jnp.broadcast_to(
            through, (PAD, through.shape[1])
        ).astype(bf16)
        for d in range(1, self.half):
            self.along(land, sems, d).start()
        self.across(land, sems, 0).start()

    def forward(self, land, sems):
        for d in range(1, self.half):
            self.along(land, sems, d).wait_recv()
            self.across(land, sems, d).start()

    def finish(self, land, sems, high, later):
        for d in range(1, self.half):
            self.along(land, sems, d).wait_send()
        for d in range(self.half):
            self.across(land, sems, d).wait()

        def step(n, state):
            place = self.ranges - 1 - n if later else n
            taken = (place > self.me) if later else (place < self.me)
            through = land[place, high : high + PAD, :].astype(f32)[0:1, :]
            joined = through * state + land[place, 0:high, :].astype(f32)
            return jnp.where(taken, joined, state)

        zero = jnp.zeros((high, land.shape[2]), f32)
        state = zero
        for n in range(self.ranges):
            state = step(n, state)
        return state


def triangle(size):
    row = lax.broadcasted_iota(jnp.int32, (size, size), 0)
    col = lax.broadcasted_iota(jnp.int32, (size, size), 1)
    return row, col


def scores_of(q, k, c, fine):
    row, col = triangle(SPAN)
    middle = c[SPAN // 2 : SPAN // 2 + 1, :]
    up, down = jnp.exp(c - middle), jnp.exp(middle - c)
    a, b = q * up, k * down
    own = jnp.sum(q * k, axis=1, keepdims=True)
    if fine:
        scores = lax.dot_general(
            a, b, (((1,), (1,)), ((), ())), precision=HIGH, preferred_element_type=f32
        )
    a, b = a.astype(bf16), b.astype(bf16)
    if not fine:
        scores = dot_right(a, b)
    return jnp.where(row > col, scores, 0.0).astype(bf16), own, a, b, up, down


class Cuts:
    def __init__(self, key_dim, value_dim, rank):
        self.key, self.value = key_dim, value_dim
        self.q = slice(0, key_dim)
        self.k = slice(key_dim, 2 * key_dim)
        self.v = slice(2 * key_dim, 2 * key_dim + value_dim)
        self.og = slice(2 * key_dim + value_dim, 2 * key_dim + 2 * value_dim)
        self.begin = 2 * key_dim + 2 * value_dim
        self.width = self.begin + LANES * (-(-rank // LANES))
        self.rank = slice(self.begin, self.width)


def rounded(array):
    return array.astype(bf16).astype(f32)


def log_sigmoid(u):
    return jnp.minimum(u, 0.0) - jnp.log1p(jnp.exp(-jnp.abs(u)))


def mixer_forward_kernel(
    ranges, half, cuts, cat, up, bias, inner_ref, c_ref, l_ref, s_ref,
    moved, out, land, sems, extra=None,
):
    chain = Chain(ranges, half)
    chain.enter(extra)
    length = cat.shape[0]
    spans = length // SPAN
    scale = cuts.key ** (-0.5)
    row, col = triangle(SPAN)
    lower = (row >= col).astype(f32)
    state = jnp.zeros((cuts.value, cuts.key), f32)
    reach = jnp.zeros((1, cuts.key), f32)
    for i in range(spans):
        rows = slice(i * SPAN, (i + 1) * SPAN)
        logits = (
            jnp.dot(cat[rows, cuts.rank], up[...], precision=HIGH, preferred_element_type=f32)
            + bias[...]
        )
        l_ref[rows, :] = logits
        decay = log_sigmoid(logits) * (1.0 / GATE_SCALE)
        c = jnp.dot(lower, decay, precision=HIGH, preferred_element_type=f32)
        c_ref[rows, :] = c
        last = c[SPAN - 1 : SPAN, :]
        fading = (rounded(cat[rows, cuts.k]) * jnp.exp(last - c)).astype(bf16)
        step = dot_left(cat[rows, cuts.v].astype(bf16), fading)
        moved[i] = step
        state = jnp.exp(last) * state + step
        reach = reach + last
    chain.start(land, sems, state, jnp.exp(reach))
    if extra is not None:
        extra.start()
    for i in range(spans):
        rows = slice(i * SPAN, (i + 1) * SPAN)
        q = rounded(cat[rows, cuts.q]) * scale
        k = rounded(cat[rows, cuts.k])
        scores, own, *_ = scores_of(q, k, c_ref[rows, :], True)
        v = cat[rows, cuts.v].astype(bf16)
        out[rows, :] = dot_plain(scores, v) + own * v.astype(f32)
    chain.forward(land, sems)
    state = chain.finish(land, sems, cuts.value, False)
    for i in range(spans):
        rows = slice(i * SPAN, (i + 1) * SPAN)
        c = c_ref[rows, :]
        held = state.astype(bf16)
        s_ref[i] = held
        q = (rounded(cat[rows, cuts.q]) * scale * jnp.exp(c)).astype(bf16)
        inner_ref[rows, :] = out[rows, :] + dot_right(q, held)
        state = jnp.exp(c[SPAN - 1 : SPAN, :]) * state + moved[i]
    s_ref[spans] = state.astype(bf16)
    if extra is not None:
        extra.finish()


def mixer_backward_kernel(
    ranges, half, cuts, dgated_ref, inner_ref, cat, up, hg_ref, c_ref, l_ref, s_ref,
    dcat, hgp_ref, dup_ref, dbias_ref, pulled, o_ref, dqs, dks, dvs, land, sems, extra=None,
):
    chain = Chain(ranges, half)
    chain.enter(extra)
    length = cat.shape[0]
    spans = length // SPAN
    scale = cuts.key ** (-0.5)
    row, col = triangle(SPAN)
    upper = (row <= col).astype(f32)
    state = jnp.zeros((cuts.value, cuts.key), f32)
    reach = jnp.zeros((1, cuts.key), f32)
    hg = hg_ref[...]
    head_part = jnp.zeros((1, cuts.value), f32)
    for i in reversed(range(spans)):
        rows = slice(i * SPAN, (i + 1) * SPAN)
        inner, og, dgated = inner_ref[rows, :], cat[rows, cuts.og], dgated_ref[rows, :]
        r = lax.rsqrt(jnp.mean(inner * inner, axis=-1, keepdims=True) + HEAD_EPS)
        sg = 1.0 / (1.0 + jnp.exp(-og))
        d_norm = dgated * (og * sg)
        unit = inner * r
        head_part = head_part + jnp.sum(d_norm * unit, axis=0, keepdims=True)
        w = d_norm * hg
        d_inner = r * w - inner * (r * r * r) * jnp.mean(w * inner, axis=-1, keepdims=True)
        dog = dgated * unit * hg * (sg * (1.0 + og * (1.0 - sg)))
        dcat[rows, cuts.og] = dog.astype(bf16)
        o_ref[rows, :] = d_inner
        o = d_inner.astype(bf16)
        c = c_ref[rows, :]
        q = (rounded(cat[rows, cuts.q]) * scale * jnp.exp(c)).astype(bf16)
        step = dot_left(o, q)
        pulled[i] = step
        last = c[SPAN - 1 : SPAN, :]
        state = jnp.exp(last) * state + step
        reach = reach + last
    hgp_ref[...] = head_part
    chain.start(land, sems, state, jnp.exp(reach))
    if extra is not None:
        extra.start()
    for i in range(spans):
        rows = slice(i * SPAN, (i + 1) * SPAN)
        q = rounded(cat[rows, cuts.q]) * scale
        k = rounded(cat[rows, cuts.k])
        scores, own, a, b, gain_up, gain_down = scores_of(q, k, c_ref[rows, :], False)
        d_inner, v = o_ref[rows, :], cat[rows, cuts.v].astype(bf16)
        o = d_inner.astype(bf16)
        d_own = jnp.sum(d_inner * v.astype(f32), axis=1, keepdims=True)
        d_scores = jnp.where(row > col, dot_right(o, v), 0.0).astype(bf16)
        dvs[rows, :] = dot_left(scores, o) + own * d_inner
        dqs[rows, :] = (
            d_own * k
            + gain_up * dot_plain(d_scores, b)
            + jnp.exp(c_ref[rows, :]) * dot_plain(o, s_ref[i])
        )
        dks[rows, :] = d_own * q + gain_down * dot_left(d_scores, a)
    chain.forward(land, sems)
    state = chain.finish(land, sems, cuts.value, True)
    d_up = jnp.zeros(dup_ref.shape, f32)
    d_bias = jnp.zeros(dbias_ref.shape, f32)
    for i in reversed(range(spans)):
        rows = slice(i * SPAN, (i + 1) * SPAN)
        c = c_ref[rows, :]
        last = c[SPAN - 1 : SPAN, :]
        fade = jnp.exp(last - c)
        held = state.astype(bf16)
        k = rounded(cat[rows, cuts.k])
        dk = dks[rows, :] + fade * dot_plain(cat[rows, cuts.v].astype(bf16), held)
        dv = dvs[rows, :] + dot_right((k * fade).astype(bf16), held)
        dq = dqs[rows, :]
        dcat[rows, cuts.q] = (dq * scale).astype(bf16)
        dcat[rows, cuts.k] = dk.astype(bf16)
        dcat[rows, cuts.v] = dv.astype(bf16)
        ended = jnp.sum(state * s_ref[i + 1].astype(f32), axis=0, keepdims=True)
        terms = rounded(cat[rows, cuts.q]) * scale * dq - k * dk
        d_decay = jnp.dot(upper, terms, precision=HIGH, preferred_element_type=f32) + ended
        d_logits = d_decay * (1.0 / (1.0 + jnp.exp(l_ref[rows, :]))) * (1.0 / GATE_SCALE)
        d_bias = d_bias + jnp.sum(d_logits, axis=0, keepdims=True)
        d_up = d_up + lax.dot_general(
            cat[rows, cuts.rank], d_logits, (((0,), (0,)), ((), ())),
            precision=HIGH, preferred_element_type=f32,
        )
        d_rank = lax.dot_general(
            d_logits, up[...], (((1,), (1,)), ((), ())),
            precision=HIGH, preferred_element_type=f32,
        )
        dcat[rows, cuts.rank] = d_rank.astype(bf16)
        state = jnp.exp(last) * state + pulled[i]
    dup_ref[...] = d_up
    dbias_ref[...] = d_bias
    if extra is not None:
        extra.finish()


def mixer_forward(ranges, half, cuts, cat, up, bias, ident=9, extra=None):
    length = cat.shape[0]
    spans = length // SPAN
    return kernel_call(
        partial(mixer_forward_kernel, ranges, half, cuts),
        [
            shape((length, cuts.value), f32),
            shape((length, cuts.key), f32),
            shape((length, cuts.key), f32),
            shape((spans + 1, cuts.value, cuts.key), bf16),
        ],
        [
            pltpu.VMEM((spans, cuts.value, cuts.key), f32),
            pltpu.VMEM((length, cuts.value), f32),
            pltpu.VMEM((ranges, cuts.value + PAD, cuts.key), bf16),
            pltpu.SemaphoreType.DMA((4, half)),
        ],
        ident,
        cat, up, bias,
        extra=extra,
    )


def mixer_backward(
    ranges, half, cuts, dgated, inner, cat, up, hg, c, logits, s, ident=10, extra=None
):
    length = cat.shape[0]
    spans = length // SPAN
    return kernel_call(
        partial(mixer_backward_kernel, ranges, half, cuts),
        [
            shape((length, cuts.width), bf16),
            shape((1, cuts.value), f32),
            shape(up.shape, f32),
            shape((1, cuts.key), f32),
        ],
        [
            pltpu.VMEM((spans, cuts.value, cuts.key), f32),
            pltpu.VMEM((length, cuts.value), f32),
            pltpu.VMEM((length, cuts.key), f32),
            pltpu.VMEM((length, cuts.key), f32),
            pltpu.VMEM((length, cuts.value), f32),
            pltpu.VMEM((ranges, cuts.value + PAD, cuts.key), bf16),
            pltpu.SemaphoreType.DMA((4, half)),
        ],
        ident,
        dgated, inner, cat, up, hg, c, logits, s,
        extra=extra,
    )


class Ranges:
    def __init__(self, half):
        self.half = half
        self.s, self.l = lax.axis_index("section"), lax.axis_index("stage")
        self.q = lax.axis_index("q")
        self.stays = self.s == self.l

    def enter(self, cores):
        barrier = pltpu.get_barrier_semaphore()
        for d in range(1, self.half):
            pl.semaphore_signal(barrier, inc=1, device_id={"q": self.after(d)})
        count = self.half - 1
        if cores:
            pl.semaphore_signal(barrier, inc=1, device_id={"section": 1 - self.s})
            count = count + 1

        @pl.when(self.stays)
        def _():
            pl.semaphore_wait(barrier, count)

        @pl.when(jnp.logical_not(self.stays))
        def _():
            pl.semaphore_signal(barrier, inc=1, device_id={"section": self.l, "stage": self.s})
            pl.semaphore_wait(barrier, count + 1)

    def after(self, d):
        return lax.rem(self.q + d, self.half)

    def before(self, d):
        return lax.rem(self.q + self.half - d, self.half)

    def at(self, section, q, rows):
        return pl.ds(pl.multiple_of((section * self.half + q) * rows, rows), rows)


def gather_kernel(half, count, *refs):
    ins, outs, bounce = refs[:count], refs[count : 2 * count], refs[2 * count : 3 * count]
    swap_sems, z_sems, core_sems, keep_sems = refs[3 * count :]
    r = Ranges(half)
    r.enter(True)

    def held(i):
        rows = ins[i].shape[0]
        return outs[i].at[r.at(r.s, r.q, rows)]

    def swap(i):
        rows = ins[i].shape[0]
        return pltpu.make_async_remote_copy(
            src_ref=ins[i],
            dst_ref=outs[i].at[r.at(r.l, r.q, rows)],
            send_sem=swap_sems.at[0, i],
            recv_sem=swap_sems.at[1, i],
            device_id={"section": r.l, "stage": r.s},
        )

    def along(i, d, src):
        return pltpu.make_async_remote_copy(
            src_ref=src,
            dst_ref=held(i),
            send_sem=z_sems.at[0, i, d - 1],
            recv_sem=z_sems.at[1, i, d - 1],
            device_id={"q": r.after(d)},
        )

    def across(i, d, src):
        rows = ins[i].shape[0]
        return pltpu.make_async_remote_copy(
            src_ref=src,
            dst_ref=outs[i].at[r.at(r.s, r.before(d), rows)],
            send_sem=core_sems.at[0, i, d],
            recv_sem=core_sems.at[1, i, d],
            device_id={"section": 1 - r.s},
        )

    def load(i):
        return pltpu.make_async_copy(ins[i], bounce[i], keep_sems.at[0, i])

    def keep(i):
        return pltpu.make_async_copy(bounce[i], held(i), keep_sems.at[1, i])

    @pl.when(r.stays)
    def _():
        for i in range(count):
            for d in range(1, half):
                along(i, d, ins[i]).start()
            across(i, 0, ins[i]).start()
            load(i).start()
        for i in range(count):
            load(i).wait()
            keep(i).start()

    @pl.when(jnp.logical_not(r.stays))
    def _():
        for i in range(count):
            swap(i).start()

    for i in range(count):
        rows = ins[i].shape[0]

        @pl.when(jnp.logical_not(r.stays))
        def _():
            swap(i).wait_recv()
            for d in range(1, half):
                along(i, d, held(i)).start()
            across(i, 0, held(i)).start()

        for d in range(1, half):
            along(i, d, ins[i]).wait_recv()
            across(i, d, outs[i].at[r.at(r.s, r.before(d), rows)]).start()

    for i in range(count):

        @pl.when(r.stays)
        def _():
            keep(i).wait()

        @pl.when(jnp.logical_not(r.stays))
        def _():
            swap(i).wait_send()

        for d in range(1, half):
            along(i, d, ins[i]).wait_send()
        for d in range(half):
            across(i, d, ins[i]).wait()


def gather_weights(half, ident, *shards_in):
    count = len(shards_in)
    anywhere = pl.BlockSpec(memory_space=pl.ANY)
    return pl.pallas_call(
        partial(gather_kernel, half, count),
        out_shape=[shape((2 * half * a.shape[0], a.shape[1]), a.dtype) for a in shards_in],
        in_specs=[anywhere] * count,
        out_specs=[anywhere] * count,
        scratch_shapes=[pltpu.VMEM(a.shape, a.dtype) for a in shards_in]
        + [
            pltpu.SemaphoreType.DMA((2, count)),
            pltpu.SemaphoreType.DMA((2, count, half - 1)),
            pltpu.SemaphoreType.DMA((2, count, half)),
            pltpu.SemaphoreType.DMA((2, count)),
        ],
        compiler_params=pltpu.CompilerParams(
            collective_id=ident, has_side_effects=True, vmem_limit_bytes=40 * 1024 * 1024
        ),
    )(*shards_in)


class GatherStart:
    def __init__(self, half, home, whole, bounce, swap_sems, z_sems, core_sems, keep_sems):
        r = self.r = Ranges(half)
        rows = home.shape[0]
        self.half = half
        moves = jnp.logical_not(r.stays)
        self.signals = {("q", d): (None, {"q": r.after(d)}) for d in range(1, half)}
        self.signals["core"] = (None, {"section": 1 - r.s})
        self.signals["swap"] = (moves, {"section": r.l, "stage": r.s})
        self.waits = {name: condition for name, (condition, _) in self.signals.items()}
        held = whole.at[r.at(r.s, r.q, rows)]
        self.swap = pltpu.make_async_remote_copy(
            src_ref=home,
            dst_ref=whole.at[r.at(r.l, r.q, rows)],
            send_sem=swap_sems.at[0],
            recv_sem=swap_sems.at[1],
            device_id={"section": r.l, "stage": r.s},
        )
        self.along = [
            pltpu.make_async_remote_copy(
                src_ref=home,
                dst_ref=held,
                send_sem=z_sems.at[0, d - 1],
                recv_sem=z_sems.at[1, d - 1],
                device_id={"q": r.after(d)},
            )
            for d in range(1, half)
        ]
        self.across = pltpu.make_async_remote_copy(
            src_ref=home,
            dst_ref=held,
            send_sem=core_sems.at[0],
            recv_sem=core_sems.at[1],
            device_id={"section": 1 - r.s},
        )
        self.load = pltpu.make_async_copy(home, bounce, keep_sems.at[0])
        self.keep = pltpu.make_async_copy(bounce, held, keep_sems.at[1])

    def start(self):
        @pl.when(self.r.stays)
        def _():
            for copy in self.along:
                copy.start()
            self.across.start()
            self.load.start()

        @pl.when(jnp.logical_not(self.r.stays))
        def _():
            self.swap.start()

    def finish(self):
        @pl.when(self.r.stays)
        def _():
            self.load.wait()
            self.keep.start()
            for copy in self.along:
                copy.wait()
            self.across.wait_send()
            self.keep.wait()

        @pl.when(jnp.logical_not(self.r.stays))
        def _():
            self.swap.wait()
            self.across.wait_recv()


def gather_start(half, home):
    return (
        partial(GatherStart, half),
        [home],
        [shape((2 * half * home.shape[0], home.shape[1]), home.dtype)],
        [
            pltpu.VMEM(home.shape, home.dtype),
            pltpu.SemaphoreType.DMA((2,)),
            pltpu.SemaphoreType.DMA((2, half - 1)),
            pltpu.SemaphoreType.DMA((2,)),
            pltpu.SemaphoreType.DMA((2,)),
        ],
    )


def gather_end_kernel(half, count, rows, *refs):
    outs = refs[count : 2 * count]
    z_sems, core_sems = refs[2 * count :]
    r = Ranges(half)
    r.enter(True)

    def piece(i, q):
        return outs[i].at[r.at(r.s, q, rows)]

    def along(i, d):
        return pltpu.make_async_remote_copy(
            src_ref=piece(i, r.q),
            dst_ref=piece(i, r.q),
            send_sem=z_sems.at[0, i, d - 1],
            recv_sem=z_sems.at[1, i, d - 1],
            device_id={"q": r.after(d)},
        )

    def across(i, d):
        return pltpu.make_async_remote_copy(
            src_ref=piece(i, r.before(d)),
            dst_ref=piece(i, r.before(d)),
            send_sem=core_sems.at[0, i, d],
            recv_sem=core_sems.at[1, i, d],
            device_id={"section": 1 - r.s},
        )

    @pl.when(r.stays)
    def _():
        for i in range(count):
            for d in range(1, half):
                across(i, d).start()
        for i in range(count):
            for d in range(1, half):
                across(i, d).wait()
            across(i, 0).wait_recv()

    @pl.when(jnp.logical_not(r.stays))
    def _():
        for i in range(count):
            for d in range(1, half):
                along(i, d).start()
        for i in range(count):
            across(i, 0).start()
        for i in range(count):
            for d in range(1, half):
                along(i, d).wait_recv()
                across(i, d).start()
        for i in range(count):
            for d in range(1, half):
                along(i, d).wait_send()
                across(i, d).wait()
            across(i, 0).wait_send()


def gather_end(half, ident, *begun):
    count = len(begun)
    rows = begun[0].shape[0] // (2 * half)
    anywhere = pl.BlockSpec(memory_space=pl.ANY)
    return pl.pallas_call(
        partial(gather_end_kernel, half, count, rows),
        out_shape=[shape(a.shape, a.dtype) for a in begun],
        in_specs=[anywhere] * count,
        out_specs=[anywhere] * count,
        scratch_shapes=[
            pltpu.SemaphoreType.DMA((2, count, half - 1)),
            pltpu.SemaphoreType.DMA((2, count, half)),
        ],
        input_output_aliases={i: i for i in range(count)},
        compiler_params=pltpu.CompilerParams(collective_id=ident, has_side_effects=True),
    )(*begun)


class AlongStart:
    def __init__(self, half, rows, *refs):
        r = self.r = Ranges(half)
        self.signals = {("q", d): (None, {"q": r.after(d)}) for d in range(1, half)}
        self.swap = None
        if len(refs) == 3:
            total, away, sems = refs
        else:
            total, summed, away, landed, sems, swap_sems = refs
            self.moves = jnp.logical_not(r.stays)
            self.signals["swap"] = (self.moves, {"section": r.l, "stage": r.s})
            self.swap = pltpu.make_async_remote_copy(
                src_ref=summed,
                dst_ref=landed,
                send_sem=swap_sems.at[0],
                recv_sem=swap_sems.at[1],
                device_id={"section": r.l, "stage": r.s},
            )
        self.waits = {name: condition for name, (condition, _) in self.signals.items()}
        self.copies = [
            pltpu.make_async_remote_copy(
                src_ref=total.at[r.at(0, r.after(d), rows)],
                dst_ref=away.at[d - 1],
                send_sem=sems.at[0, d - 1],
                recv_sem=sems.at[1, d - 1],
                device_id={"q": r.after(d)},
            )
            for d in range(1, half)
        ]

    def start(self):
        for copy in self.copies:
            copy.start()
        if self.swap is not None:

            @pl.when(self.moves)
            def _():
                self.swap.start()

    def finish(self):
        for copy in self.copies:
            copy.wait()
        if self.swap is not None:

            @pl.when(self.moves)
            def _():
                self.swap.wait()


def along_start(half, total, summed=None):
    rows = total.shape[0] // half
    away = shape((half - 1, rows, total.shape[1]), total.dtype)
    sems = pltpu.SemaphoreType.DMA((2, half - 1))
    kind = partial(AlongStart, half, rows)
    if summed is None:
        return kind, [total], [away], [sems]
    landed = shape(summed.shape, summed.dtype)
    return kind, [total, summed], [away, landed], [sems, pltpu.SemaphoreType.DMA((2,))]


class HomeStart:
    def __init__(self, half, src, landed, sems):
        r = Ranges(half)
        self.moves = jnp.logical_not(r.stays)
        self.signals = {"swap": (self.moves, {"section": r.l, "stage": r.s})}
        self.waits = {"swap": self.moves}
        self.copy = pltpu.make_async_remote_copy(
            src_ref=src,
            dst_ref=landed,
            send_sem=sems.at[0],
            recv_sem=sems.at[1],
            device_id={"section": r.l, "stage": r.s},
        )

    def start(self):
        @pl.when(self.moves)
        def _():
            self.copy.start()

    def finish(self):
        @pl.when(self.moves)
        def _():
            self.copy.wait()


def home_start(half, array):
    sems = [pltpu.SemaphoreType.DMA((2,))]
    return partial(HomeStart, half), [array], [shape(array.shape, array.dtype)], sems


def finish_kernel(half, count, come, places, lanes, *refs):
    totals, aways = refs[:count], refs[count : count + come]
    refs = refs[count + come :]
    rows_in, small = refs[:places], refs[places]
    refs = refs[places + 1 :]
    outs, full, down, small_own, small_sum = (
        refs[:count],
        refs[count : count + places],
        refs[count + places],
        refs[count + places + 1],
        refs[count + places + 2],
    )
    refs = refs[count + places + 3 :]
    mine, got = refs[:count], refs[count : 2 * count]
    small_mine, small_got, small_land, down_send, down_land, held = refs[
        2 * count : 2 * count + 6
    ]
    (
        swap_sems, z_sems, load_sems, away_sems, place_sems, keep_sems, share_sems, small_sems,
        pool_sems,
    ) = refs[2 * count + 6 :]
    peers_n = full[0].shape[1]
    r = Ranges(half)
    peers = Peers(peers_n)
    barrier = pltpu.get_barrier_semaphore()
    for d in range(1, peers_n):
        pl.semaphore_signal(barrier, inc=1, device_id={"tensor": peers.at(d)})
    for d in range(1, half):
        pl.semaphore_signal(barrier, inc=1, device_id={"q": r.after(d)})
    signals = peers_n + half - 2

    @pl.when(r.stays)
    def _():
        pl.semaphore_wait(barrier, signals)

    @pl.when(jnp.logical_not(r.stays))
    def _():
        pl.semaphore_signal(barrier, inc=1, device_id={"section": r.l, "stage": r.s})
        pl.semaphore_wait(barrier, signals + 1)

    def whole(i):
        return i < count - come

    def part(i, q):
        return totals[i].at[r.at(0, q, outs[i].shape[0])]

    def load_away(i):
        return pltpu.make_async_copy(aways[i - count + come], got[i], away_sems.at[i - count + come])

    def along(i, d):
        return pltpu.make_async_remote_copy(
            src_ref=part(i, r.after(d)),
            dst_ref=got[i].at[d - 1],
            send_sem=z_sems.at[0, i, d - 1],
            recv_sem=z_sems.at[1, i, d - 1],
            device_id={"q": r.after(d)},
        )

    def load(i):
        return pltpu.make_async_copy(part(i, r.q), mine[i], load_sems.at[i])

    def home(src, dst, sems):
        return pltpu.make_async_remote_copy(
            src_ref=src,
            dst_ref=dst,
            send_sem=sems.at[0],
            recv_sem=sems.at[1],
            device_id={"section": r.l, "stage": r.s},
        )

    def swap(i):
        return home(mine[i], outs[i], swap_sems.at[i])

    def place(j):
        return home(rows_in[j], held.at[j], place_sems.at[j])

    def shared(j, d, src):
        return pltpu.make_async_remote_copy(
            src_ref=src,
            dst_ref=full[j].at[:, peers.me],
            send_sem=share_sems.at[0, j, d - 1],
            recv_sem=share_sems.at[1, j, d - 1],
            device_id={"tensor": peers.at(d)},
        )

    def keep(j, src):
        return pltpu.make_async_copy(src, full[j].at[:, peers.me], keep_sems.at[j])

    def small_along(d):
        return pltpu.make_async_remote_copy(
            src_ref=small.at[r.after(d)],
            dst_ref=small_got.at[d - 1],
            send_sem=small_sems.at[0, d],
            recv_sem=small_sems.at[1, d],
            device_id={"q": r.after(d)},
        )

    def pool(n, d, src, dst):
        return pltpu.make_async_remote_copy(
            src_ref=src,
            dst_ref=dst,
            send_sem=pool_sems.at[0, n, d - 1],
            recv_sem=pool_sems.at[1, n, d - 1],
            device_id={"tensor": peers.at(d)},
        )

    for d in range(1, half):
        small_along(d).start()
    order = sorted(range(count), key=whole)
    ahead = [i for i in order if whole(i)]

    def begin(n):
        if n < len(ahead):
            for d in range(1, half):
                along(ahead[n], d).start()

    for n in range(WINDOW):
        begin(n)
    for i in order:
        load(i).start()
        if not whole(i):
            load_away(i).start()

    def show(j, src):
        keep(j, src).start()
        for d in range(1, peers_n):
            shared(j, d, src).start()

    @pl.when(r.stays)
    def _():
        for j in range(places):
            show(j, rows_in[j])

    @pl.when(jnp.logical_not(r.stays))
    def _():
        show(0, rows_in[0])
        for j in range(1, places):
            place(j).start()

    for i in order:
        load(i).wait()
        if whole(i):
            for d in range(1, half):
                along(i, d).wait_recv()
            begin(ahead.index(i) + WINDOW)
        else:
            load_away(i).wait()

        @pl.loop(0, outs[i].shape[0] // STRIP)
        def _(n):
            strip = pl.ds(pl.multiple_of(n * STRIP, STRIP), STRIP)
            total = mine[i][strip, :].astype(f32)
            for d in range(1, half):
                total = total + got[i][d - 1, strip, :].astype(f32)
            mine[i][strip, :] = total.astype(bf16)

        @pl.when(r.stays)
        def _():
            @pl.loop(0, outs[i].shape[0] // STRIP)
            def _(n):
                strip = pl.ds(pl.multiple_of(n * STRIP, STRIP), STRIP)
                outs[i][strip, :] = mine[i][strip, :]

        @pl.when(jnp.logical_not(r.stays))
        def _():
            swap(i).start()

    total = small[r.q]
    for d in range(1, half):
        small_along(d).wait()
        total = total + small_got[d - 1]
    small_mine[...] = total

    @pl.when(r.stays)
    def _():
        small_own[...] = total

    @pl.when(jnp.logical_not(r.stays))
    def _():
        home(small_mine, small_own, small_sems.at[:, 0]).start()
        for j in range(1, places):
            place(j).wait_recv()
            show(j, held.at[j])
        home(small_mine, small_own, small_sems.at[:, 0]).wait()
        for i in range(count):
            swap(i).wait()
        for j in range(1, places):
            place(j).wait_send()

    down_send[...] = outs[0][:, lanes]
    for d in range(1, peers_n):
        pool(0, d, small_own, small_land.at[d - 1]).start()
        pool(1, d, down_send, down_land.at[d - 1]).start()
    total = small_own[...]
    pooled = down_send[...].astype(f32)
    for d in range(1, peers_n):
        pool(0, d, small_own, small_land.at[d - 1]).wait()
        pool(1, d, down_send, down_land.at[d - 1]).wait()
        total = total + small_land[d - 1]
        pooled = pooled + down_land[d - 1].astype(f32)
    small_sum[...] = total
    down[...] = pooled
    for i in range(count):
        if whole(i):
            for d in range(1, half):
                along(i, d).wait_send()
    for j in range(places):
        keep(j, rows_in[j]).wait()
        for d in range(1, peers_n):
            shared(j, d, rows_in[j]).wait()


def finish(half, peers, ident, totals, aways, rows_in, small, lanes):
    count, come, places = len(totals), len(aways), len(rows_in)
    high = totals[0].shape[0] // half
    micro, rows, width = rows_in[0].shape
    wide = lanes.stop - lanes.start
    anywhere = pl.BlockSpec(memory_space=pl.ANY)
    vmem = pl.BlockSpec(memory_space=pltpu.VMEM)
    tile = small.shape[1:]
    return pl.pallas_call(
        partial(finish_kernel, half, count, come, places, lanes),
        out_shape=[shape((high, a.shape[1]), bf16) for a in totals]
        + [shape((micro, peers, rows, width), bf16)] * places
        + [shape((high, wide), f32), shape(tile, f32), shape(tile, f32)],
        in_specs=[anywhere] * (count + come) + [vmem] * (places + 1),
        out_specs=[vmem] * count + [anywhere] * places + [vmem] * 3,
        scratch_shapes=[pltpu.VMEM((high, a.shape[1]), bf16) for a in totals]
        + [pltpu.VMEM((half - 1, high, a.shape[1]), bf16) for a in totals]
        + [
            pltpu.VMEM(tile, f32),
            pltpu.VMEM((half - 1,) + tile, f32),
            pltpu.VMEM((peers - 1,) + tile, f32),
            pltpu.VMEM((high, wide), bf16),
            pltpu.VMEM((peers - 1, high, wide), bf16),
            pltpu.VMEM((places, micro, rows, width), bf16),
            pltpu.SemaphoreType.DMA((count, 2)),
            pltpu.SemaphoreType.DMA((2, count, half - 1)),
            pltpu.SemaphoreType.DMA((count,)),
            pltpu.SemaphoreType.DMA((max(come, 1),)),
            pltpu.SemaphoreType.DMA((places, 2)),
            pltpu.SemaphoreType.DMA((places,)),
            pltpu.SemaphoreType.DMA((2, places, peers - 1)),
            pltpu.SemaphoreType.DMA((2, half)),
            pltpu.SemaphoreType.DMA((2, 2, peers - 1)),
        ],
        compiler_params=pltpu.CompilerParams(
            collective_id=ident, has_side_effects=True, vmem_limit_bytes=48 * 1024 * 1024
        ),
    )(*totals, *aways, *rows_in, small)


def swapped(array):
    moved = swap_moved(array)
    stays = lax.axis_index("section") == lax.axis_index("stage")
    return jnp.where(stays, array, moved)


def swap_moved(array):
    return lax.ppermute(array, ("section", "stage"), [(1, 2), (2, 1)])


def exchanged(array, axis):
    return lax.ppermute(array, axis, [(0, 1), (1, 0)])


def core_sum(left, right):
    high = left.shape[1] // 2
    section = lax.axis_index("section")

    def rows_for(who):
        return dot_left(lax.dynamic_slice_in_dim(left, who * high, high, 1), right)

    theirs = exchanged(rows_for(1 - section).astype(bf16), "section")
    return (rows_for(section) + theirs.astype(f32)).astype(bf16)


def tiles_of(array, lead, low):
    width = -(-array.shape[1] // (low * LANES)) * LANES
    array = jnp.pad(array, ((0, 0), (0, low * width - array.shape[1])))
    return array.reshape(lead, low, width)


def shards(
    inputs,
    cotangent,
    query_proj,
    key_proj,
    value_proj,
    outgate_proj,
    output_proj,
    decay_down,
    decay_up,
    decay_bias,
    head_gain,
    mixer_gain,
    feed_gain,
    feed_gate,
    feed_up,
    feed_down,
):
    micro, length, width = inputs.shape
    peers = lax.axis_size("tensor")
    half = lax.axis_size("q")
    ranges = 2 * half
    stage = lax.axis_index("stage")
    me = lax.axis_index("tensor")
    rows = length // peers
    rank = decay_down.shape[2]
    cuts = Cuts(query_proj.shape[2], value_proj.shape[2], rank)
    sizes = (ranges, half, cuts)

    def own_rows(array):
        return swapped(lax.dynamic_slice_in_dim(array, me * rows, rows, 1))

    own_in = own_rows(inputs)
    small = [decay_up[0], decay_bias[0], head_gain[0], mixer_gain[0], feed_gain[0]]
    counts = [a.size for a in small]
    ends = [sum(counts[:n]) for n in range(len(counts) + 1)]
    small = tiles_of(jnp.concatenate([a.reshape(1, -1) for a in small], axis=1), 1, 16)[0]
    lanes = cuts.width - cuts.begin
    cat = jnp.concatenate(
        [query_proj[0], key_proj[0], value_proj[0], outgate_proj[0], decay_down[0]], axis=1
    )
    cat = jnp.pad(cat, ((0, 0), (0, cuts.width - cat.shape[1])))
    packed, cat, output = gather_weights(half, 11, small, cat, output_proj[0])
    packed = packed.reshape(ranges, -1).astype(f32)
    up_w, bias_w, head_w, mixer_w, feed_w = (
        packed[:, ends[n] : ends[n + 1]] for n in range(len(counts))
    )
    w = dict(
        up=jnp.pad(up_w.reshape(-1, rank).T, ((0, lanes - rank), (0, 0))),
        bias=bias_w.reshape(1, -1),
        head_gain=head_w.reshape(1, -1),
        mixer_gain=mixer_w.reshape(1, -1),
        feed_gain=feed_w.reshape(1, -1),
    )
    w["cat"], w["output"] = cat, output
    homes = [feed_gate[0], feed_up[0], feed_down[0]]
    own_cot = own_rows(cotangent)

    calls = Rows(rows, width, peers)
    kept, ys = [], []
    h = jnp.where(stage == 0, own_in[0], jnp.zeros_like(own_in[0]))
    normed, gate = calls.first(h, w["mixer_gain"], gather_start(half, homes[0]))
    for step in range(micro + 1):
        cat_v = dot_plain(normed, w["cat"])
        inner, cumul, logits, states, *upper = mixer_forward(
            ranges, half, cuts, cat_v, w["up"], w["bias"],
            **(dict(ident=14, extra=gather_start(half, homes[1])) if step == 0 else {}),
        )
        gated = head_output(inner, cat_v[:, cuts.og], w["head_gain"]).astype(bf16)
        middle, feed_in, *lower = calls.forward_mid(
            dot_right(gated, w["output"]), h, w["feed_gain"],
            **(dict(ident=15, extra=gather_start(half, homes[2])) if step == 0 else {}),
        )
        if step == 0:
            w["gate"], w["upper"], w["lower"] = gather_end(half, 12, gate, *upper, *lower)
        gate_v = dot_plain(feed_in, w["gate"])
        upper_v = dot_plain(feed_in, w["upper"])
        hidden = (jax.nn.silu(gate_v) * upper_v).astype(bf16)
        kept.append(
            dict(
                h=h, normed=normed, cat=cat_v, inner=inner, gated=gated, cumul=cumul,
                logits=logits, states=states, middle=middle, feed_in=feed_in, gate_v=gate_v,
                upper_v=upper_v, hidden=hidden,
            )
        )
        part = dot_right(hidden, w["lower"])
        if step < micro:
            y, h, normed = calls.forward_end(
                part, middle, w["mixer_gain"], own_in[min(step + 1, micro - 1)]
            )
        else:
            gy = jnp.where(stage == 1, own_cot[micro - 1], jnp.zeros_like(own_cot[0]))
            y, d_feed = calls.forward_last(part, middle, gy)
        ys.append(y)

    grads, saved = [], []

    def picked(zero, one):
        return jnp.where(stage == 0, zero, one)

    def rows_of(name):
        items = [item[name] for item in (kept if name in kept[0] else saved[::-1])]
        return jnp.concatenate([picked(items[m], items[m + 1]) for m in range(micro)])

    def with_away(total, away):
        place, high = lax.axis_index("q"), total.shape[0] // half
        own = lax.dynamic_slice_in_dim(total, place * high, high, 0)
        return (own.astype(f32) + jnp.sum(away.astype(f32), axis=0)).astype(bf16)

    worked = picked(jnp.stack(ys[:micro]), jnp.stack(ys[1:]))

    for step in range(micro + 1):
        now = kept[micro - step]
        d_hidden = dot_plain(d_feed, w["lower"])
        sig = jax.nn.sigmoid(now["gate_v"])
        d_gate = (
            d_hidden * now["upper_v"] * (sig * (1.0 + now["gate_v"] * (1.0 - sig)))
        ).astype(bf16)
        d_upper = (d_hidden * (now["gate_v"] * sig)).astype(bf16)
        part = dot_right(d_gate, w["gate"]) + dot_right(d_upper, w["upper"])
        saved.append(dict(d_feed=d_feed, d_gate=d_gate, d_upper=d_upper))
        if step == micro:
            feed_in = rows_of("feed_in")
            feed_totals = [
                core_sum(feed_in, rows_of("d_gate")),
                core_sum(feed_in, rows_of("d_upper")),
                core_sum(rows_of("d_feed"), rows_of("hidden")),
            ]
            feed_totals, part = lax.optimization_barrier((feed_totals, part))
        last = step == micro
        d_middle, feed_part, d_mixed, *away_0 = calls.backward_mid(
            part, gy, now["middle"], w["feed_gain"],
            **(dict(ident=16, extra=along_start(half, feed_totals[0])) if last else {}),
        )
        if last:
            gate_sum = with_away(feed_totals[0], away_0[0])
        d_gated = dot_plain(d_mixed, w["output"])
        d_cat, head_part, up_part, bias_part, *away_1 = mixer_backward(
            ranges, half, cuts, d_gated, now["inner"], now["cat"], w["up"], w["head_gain"],
            now["cumul"], now["logits"], now["states"],
            **(dict(ident=17, extra=along_start(half, feed_totals[1], gate_sum)) if last else {}),
        )
        part = dot_right(d_cat, w["cat"])
        saved[-1].update(d_mixed=d_mixed, d_cat=d_cat)
        if step < micro:
            later = micro - 2 - step
            own = own_cot[later] if later >= 0 else jnp.zeros_like(own_cot[0])
            grad, mixer_part, gy, d_feed, *more = calls.backward_end(
                part, d_middle, now["h"], w["mixer_gain"], own,
                **(dict(ident=18, extra=home_start(half, worked)) if step == 0 else {}),
            )
            if step == 0:
                outputs_in = jnp.where(lax.axis_index("section") == stage, worked, more[0])
        else:
            upper_sum = with_away(feed_totals[1], away_1[0])
            grad, mixer_part, *away_2 = calls.backward_last(
                part, d_middle, now["h"], w["mixer_gain"],
                along_start(half, feed_totals[2], upper_sum),
            )
        grads.append(grad)
        saved[-1].update(
            head=head_part, mixer=mixer_part, feed=feed_part, up=up_part, bias=bias_part
        )

    def sum_of(name):
        return sum(item[name] for item in saved)

    totals = [
        core_sum(rows_of("normed"), rows_of("d_cat")),
        core_sum(rows_of("d_mixed"), rows_of("gated")),
    ] + feed_totals[2:]
    small_grads = [
        sum_of("up")[:rank].T,
        sum_of("bias"),
        sum_of("head"),
        sum_of("mixer"),
        sum_of("feed"),
    ]
    small_grads = tiles_of(
        jnp.concatenate([g.reshape(ranges, -1) for g in small_grads], axis=1), ranges, 8
    )
    section = lax.axis_index("section")
    theirs = exchanged(
        lax.dynamic_slice_in_dim(small_grads, (1 - section) * half, half, 0), "section"
    )
    small_grads = lax.dynamic_slice_in_dim(small_grads, section * half, half, 0) + theirs

    places = [outputs_in, picked(jnp.stack(grads[:0:-1]), jnp.stack(grads[micro - 1 :: -1]))]
    cat_grad, output_grad, lower_grad, outputs, input_grads, down, own, pooled = finish(
        half, peers, 13, totals, away_2[:1], places, small_grads, cuts.rank
    )
    stays = section == stage
    gate_grad = jnp.where(stays, gate_sum, away_1[1]).astype(f32)
    upper_grad = jnp.where(stays, upper_sum, away_2[1]).astype(f32)
    cat_grad, output_grad, lower_grad, input_grads = (
        g.astype(f32) for g in (cat_grad, output_grad, lower_grad, input_grads)
    )
    own, pooled = own.reshape(-1), pooled.reshape(-1)

    def piece(n, like):
        return (own if n < 2 else pooled)[ends[n] : ends[n + 1]].reshape(like.shape)

    return (
        outputs.reshape(1, micro, length, width),
        input_grads.reshape(1, micro, length, width),
        cat_grad[None, :, cuts.q],
        cat_grad[None, :, cuts.k],
        cat_grad[None, :, cuts.v],
        cat_grad[None, :, cuts.og],
        output_grad[None],
        down[None, :, :rank],
        piece(0, decay_up),
        piece(1, decay_bias),
        piece(2, head_gain),
        piece(3, mixer_gain),
        piece(4, feed_gain),
        gate_grad[None],
        upper_grad[None],
        lower_grad[None],
    )


def solution(mesh):
    sections, ranges, peers = (mesh.shape[a] for a in ("section", "seq", "tensor"))
    staged = Mesh(
        mesh.devices.reshape(sections, 2, ranges // 2, peers), ("section", "stage", "q", "tensor")
    )
    seq = ("stage", "q")
    whole = P("section", seq, "tensor")
    row = P("section", seq)
    rows = P("section", None, seq, None)
    tokens = P(None, seq, None)
    narrow = P("section", seq, None)
    return jax.shard_map(
        shards,
        mesh=staged,
        in_specs=(tokens, tokens)
        + (whole,) * 5
        + (narrow, whole, whole, row, row, row)
        + (whole,) * 3,
        out_specs=(rows, rows) + (whole,) * 5 + (narrow, whole, whole, row, row, row) + (whole,) * 3,
        check_vma=False,
    )
```

time: 2100 us -> 1250 us (0.60)
  waiting for transfers between devices: 1040 us -> 0.02 us
  Pallas kernels: 644 us -> 971 us
  starting transfers between devices: 76.2 us -> 7.73 us
  matrix products: 222 us -> 165 us
    reduce_scatter x8 -> x0, waiting for transfers between devices: 418 us -> none  [home(): lax.psum_scatter(whole.astype(bf16), GROUP, scatter_dimension=0, tiled=True)]
    all_gather x10 -> x0, waiting for transfers between devices: 396 us -> none  [the longest x8 310 us: work_weights(): lax.all_gather(swapped(w), GROUP, axis=0, tiled=True)]
    pallas_call x26 -> x28, Pallas kernels: 644 us -> 971 us  [the longest x25 687 us: kernel_call(): pl.pallas_call(body, out_shape=outs, in_specs=in_specs, out_specs=out_spe...]
    ppermute x22 -> x8, waiting for transfers between devices: 227 us -> 0.02 us  [the longest x6 0.02 us: exchanged(): return lax.ppermute(array, axis, [(0, 1), (1, 0)])]
    ppermute x22 -> x8, starting transfers between devices: 74.8 us -> 7.73 us  [the longest x2 6.58 us: swap_moved(): return lax.ppermute(array, ('section', 'stage'), [(1, 2), (2, 1)])]
    dot_general x36 -> x20, matrix products: 68.9 us -> 48.8 us  [dot_right(): lax.dot_general(left, right, (((1,), (1,)), ((), ())), preferred_element_...]
    dot_general x9 -> x10, matrix products: 60.5 us -> 44.3 us  [dot_left(): lax.dot_general(left, right, (((0,), (0,)), ((), ())), preferred_element_...]
    dot_general x36 -> x20, matrix products: 85.7 us -> 72.1 us  [dot_plain(): return jnp.dot(left, right, preferred_element_type=f32)]
  transfers between devices with their start and end apart: 42 -> 8, of which waited for: 23 -> 0; matrix products, arithmetic and copies ran while one was open for 6% -> 9% of each run, Pallas kernels for 4% -> 43%
where the time goes in v2:
time: 1250 us; the launch traced here: 1240 us
  Pallas kernels  971 us (78%)
  matrix products  165 us (13%)
  local copies, waits for them, and re-layouts  52.7 us (4%)
  other arithmetic  34.8 us (3%)
    pallas_call x25, Pallas kernels, kernel_call(): pl.pallas_call(body, out_shape=outs, in_specs=in_specs, out_specs=out_spe...  687 us
    pallas_call x1, Pallas kernels, finish(): pl.pallas_call(partial(finish_kernel, half, count, come, places, lanes),...  124 us
    pallas_call x1, Pallas kernels, gather_weights(): pl.pallas_call(partial(gather_kernel, half, count), out_shape=[shape((2 *...  103 us
    dot_general x20, matrix products, dot_plain(): return jnp.dot(left, right, preferred_element_type=f32)  72.1 us
    pallas_call x1, Pallas kernels, gather_end(): pl.pallas_call(partial(gather_end_kernel, half, count, rows), out_shape=[...  56.1 us
    dot_general x20, matrix products, dot_right(): lax.dot_general(left, right, (((1,), (1,)), ((), ())), preferred_element_...  48.8 us
    dot_general x10, matrix products, dot_left(): lax.dot_general(left, right, (((0,), (0,)), ((), ())), preferred_element_...  44.3 us
    unnamed x485, local copies, waits for them, and re-layouts  42.1 us
  transfers between devices with their start and end apart: 8, of which 0 were waited for; matrix products, arithmetic and copies ran while one was open for 9% of the time, Pallas kernels for 43%

profile of v2, /device:TPU:24, one launch (start us, length us, event | category | flops | bytes accessed | tf_op | source)
XLA Modules:
  0.0 1235.8 jit_solution(15754631735627416546)
XLA Ops:
  0.7 2.2 constant_dynamic-slice_fusion.2
  5.0 2.1 constant_dynamic-slice_fusion.1
  7.1 4.5 collective-permute-start.1
  12.8 103.4 %shard_map.279 = (bf16[64,256]{1,0:T(8,128)(2,1)S(1)}, bf16[2048,1664]{1,0:T(8,128)(2,1)S(1)}, bf16[2048,512]{1,0:T(8,128)(2,1)S(1)}) custom-call(bf16[16,256]{1,0:T(8,128)(2,1)S(1)} %squeeze_reshape.3.refs_0_, bf16[512,1664]{1,0:T(8,128)(2,1)S(1)} %pad.17.refs_1_, bf16[512,512]{1,0:T(8,128)(2,1)S(1)} %bitcast.314), custom_call_target="tpu_custom_call" | custom-call | tf_op jit(solution)/shard_map/pallas_call | solution.py:1042
  116.2 2.8 copy-done.134
  122.0 35.8 %shard_map.280 = (bf16[4,64,2048]{2,1,0:T(8,128)(2,1)S(1)}, bf16[2048,1408]{1,0:T(8,128)(2,1)S(1)}) custom-call(bf16[64,2048]{1,0:T(8,128)(2,1)S(1)} %get-tuple-element.314.refs_0_.refs_1_.refs_2_, f32[1,2048]{1,0:T(1,128)S(1)} %bitcast.306, bf16[512,1408]{1,0:T(8,128)(2,1)S(1)} %bitcast.268), custom_call_target="tpu_custom_call" | custom-call | tf_op jit(solution)/shard_map/pallas_call | solution.py:468
  157.8 7.5 fusion.60.refs_0_.refs_2_
  165.3 39.9 %shard_map.281 = (f32[256,512]{1,0:T(8,128)S(1)}, f32[256,256]{1,0:T(8,128)S(1)}, f32[256,256]{1,0:T(8,128)S(1)}, bf16[5,512,256]{2,1,0:T(8,128)(2,1)S(1)}, bf16[2048,1408]{1,0:T(8,128)(2,1)S(1)}) custom-call(f32[256,1664]{1,0:T(8,128)S(1)} %fusion.60.refs_0_.refs_2_, f32[128,256]{1,0:T(8,128)S(1)} %pad.18.refs_1_.up.refs_3_, ...), custom_call_target="tpu_custom_call" | custom-call | tf_op jit(solution)/shard_map/pallas_call | solution.py:468
  209.3 36.7 %shard_map.282 = (f32[64,2048]{1,0:T(8,128)S(1)}, bf16[4,64,2048]{2,1,0:T(8,128)(2,1)S(1)}, bf16[2048,1408]{1,0:T(8,128)(2,1)S(1)}) custom-call(f32[4,64,2048]{2,1,0:T(8,128)S(1)} %bitcast.227, bf16[64,2048]{1,0:T(8,128)(2,1)S(1)} %get-tuple-element.314.refs_0_.refs_1_.refs_2_, f32[1,2048]{1,0:T(1,128)S(1)} %bitcast.298, bf16[512,1408]{1,0:T(8,128)(2,1)S(1)} %bitcast.269), custom_call_target="tpu_custom_call" | custom-call | tf_op jit(solution)/shard_map/pallas_call | solution.py:468
  246.1 2.5 copy-done.7
  249.6 56.1 %shard_map.283 = (bf16[2048,1408]{1,0:T(8,128)(2,1)}, bf16[2048,1408]{1,0:T(8,128)(2,1)}, bf16[2048,1408]{1,0:T(8,128)(2,1)}) custom-call(bf16[2048,1408]{1,0:T(8,128)(2,1)} %copy-done.4, bf16[2048,1408]{1,0:T(8,128)(2,1)} %copy-done.5, bf16[2048,1408]{1,0:T(8,128)(2,1)} %copy-done.7), custom_call_target="tpu_custom_call", output_to_operand_aliasing={{0}: (0, {}), {1}: (1, {}), {2}: (2, {})} | custom-call | tf_op jit(solution)/shard_map/pallas_call | solution.py:1200
  305.7 4.9 fusion.62
  310.6 3.0 multiply_convert_fusion.11
  315.5 34.5 %shard_map.284 = (bf16[64,2048]{1,0:T(8,128)(2,1)S(1)}, bf16[64,2048]{1,0:T(8,128)(2,1)S(1)}, bf16[4,64,2048]{2,1,0:T(8,128)(2,1)S(1)}) custom-call(f32[4,64,2048]{2,1,0:T(8,128)S(1)} %bitcast.262, f32[64,2048]{1,0:T(8,128)S(1)} %get-tuple-element.133.middle.refs_2_, f32[1,2048]{1,0:T(1,128)S(1)} %bitcast.307, bf16[64,2048]{1,0:T(8,128)(2,1)S(1)} %get-tuple-element.313.own), custom_call_target="tpu_custom_call" | custom-call | tf_op jit(solution)/shard_map/pallas_call | solution.py:468
  350.7 5.4 fusion.64.cat
  356.1 10.7 shard_map.285
  368.9 25.1 %shard_map.286 = (f32[64,2048]{1,0:T(8,128)S(1)}, bf16[4,64,2048]{2,1,0:T(8,128)(2,1)S(1)}) custom-call(f32[4,64,2048]{2,1,0:T(8,128)S(1)} %bitcast.229, bf16[64,2048]{1,0:T(8,128)(2,1)S(1)} %get-tuple-element.136.h, f32[1,2048]{1,0:T(1,128)S(1)} %bitcast.299), custom_call_target="tpu_custom_call" | custom-call | tf_op jit(solution)/shard_map/pallas_call | solution.py:468
  396.6 3.3 broadcast_select_fusion.20
  401.8 28.9 %shard_map.287 = (bf16[64,2048]{1,0:T(8,128)(2,1)S(1)}, bf16[64,2048]{1,0:T(8,128)(2,1)S(1)}, bf16[4,64,2048]{2,1,0:T(8,128)(2,1)S(1)}) custom-call(f32[4,64,2048]{2,1,0:T(8,128)S(1)} %bitcast.263, f32[64,2048]{1,0:T(8,128)S(1)} %get-tuple-element.138.middle, f32[1,2048]{1,0:T(1,128)S(1)} %bitcast.308, bf16[64,2048]{1,0:T(8,128)(2,1)S(1)} %get-tuple-element.312.own), custom_call_target="tpu_custom_call" | custom-call | tf_op jit(solution)/shard_map/pallas_call | solution.py:468
  432.3 5.0 fusion.68.cat
  437.3 11.0 shard_map.288
  450.5 24.6 %shard_map.289 = (f32[64,2048]{1,0:T(8,128)S(1)}, bf16[4,64,2048]{2,1,0:T(8,128)(2,1)S(1)}) custom-call(f32[4,64,2048]{2,1,0:T(8,128)S(1)} %bitcast.230, bf16[64,2048]{1,0:T(8,128)(2,1)S(1)} %get-tuple-element.141.h, f32[1,2048]{1,0:T(1,128)S(1)} %bitcast.300), custom_call_target="tpu_custom_call" | custom-call | tf_op jit(solution)/shard_map/pallas_call | solution.py:468
  477.9 3.3 broadcast_select_fusion.19
  483.1 28.9 %shard_map.290 = (bf16[64,2048]{1,0:T(8,128)(2,1)S(1)}, bf16[64,2048]{1,0:T(8,128)(2,1)S(1)}, bf16[4,64,2048]{2,1,0:T(8,128)(2,1)S(1)}) custom-call(f32[4,64,2048]{2,1,0:T(8,128)S(1)} %bitcast.264, f32[64,2048]{1,0:T(8,128)S(1)} %get-tuple-element.143.middle, f32[1,2048]{1,0:T(1,128)S(1)} %bitcast.309, bf16[64,2048]{1,0:T(8,128)(2,1)S(1)} %get-tuple-element.312.own), custom_call_target="tpu_custom_call" | custom-call | tf_op jit(solution)/shard_map/pallas_call | solution.py:468
  512.0 5.6 fusion.72.cat
  517.6 10.6 shard_map.291
  530.3 24.8 %shard_map.292 = (f32[64,2048]{1,0:T(8,128)S(1)}, bf16[4,64,2048]{2,1,0:T(8,128)(2,1)S(1)}) custom-call(f32[4,64,2048]{2,1,0:T(8,128)S(1)} %bitcast.228, bf16[64,2048]{1,0:T(8,128)(2,1)S(1)} %get-tuple-element.146.h.refs_2_, f32[1,2048]{1,0:T(1,128)S(1)} %bitcast.301), custom_call_target="tpu_custom_call" | custom-call | tf_op jit(solution)/shard_map/pallas_call | solution.py:468
  557.9 3.3 broadcast_select_fusion.18
  567.6 19.9 %shard_map.293 = (bf16[64,2048]{1,0:T(8,128)(2,1)S(1)}, bf16[4,64,2048]{2,1,0:T(8,128)(2,1)S(1)}) custom-call(f32[4,64,2048]{2,1,0:T(8,128)S(1)} %bitcast.258, f32[64,2048]{1,0:T(8,128)S(1)} %get-tuple-element.148.middle, bf16[64,2048]{1,0:T(8,128)(2,1)S(1)} %get-tuple-element.311.gy), custom_call_target="tpu_custom_call" | custom-call | tf_op jit(solution)/shard_map/pallas_call | solution.py:468
  587.5 6.0 multiply_convert_fusion.6
  597.2 21.6 %shard_map.294 = (f32[64,2048]{1,0:T(8,128)S(1)}, f32[1,2048]{1,0:T(1,128)S(1)}, bf16[4,64,2048]{2,1,0:T(8,128)(2,1)S(1)}) custom-call(f32[4,64,2048]{2,1,0:T(8,128)S(1)} %bitcast.259, bf16[64,2048]{1,0:T(8,128)(2,1)S(1)} %get-tuple-element.311.gy, f32[64,2048]{1,0:T(8,128)S(1)} %get-tuple-element.148.middle, f32[1,2048]{1,0:T(1,128)S(1)} %bitcast.302), custom_call_target="tpu_custom_call" | custom-call | tf_op jit(solution)/shard_map/pallas_call | solution.py:468
  620.7 14.5 %shard_map.295 = (bf16[256,1664]{1,0:T(8,128)(2,1)S(1)}, f32[1,512]{1,0:T(1,128)S(1)}, f32[128,256]{1,0:T(8,128)S(1)}, f32[1,256]{1,0:T(1,128)S(1)}) custom-call(f32[256,512]{1,0:T(8,128)S(1)} %fusion.77.dgated_ref, f32[256,512]{1,0:T(8,128)S(1)} %get-tuple-element.145.inner_ref, f32[256,1664]{1,0:T(8,128)S(1)} %fusion.72.cat, ...), custom_call_target="tpu_custom_call" | custom-call | tf_op jit(solution)/shard_map/pallas_call | solution.py:468
  636.3 5.4 fusion.78
  641.9 24.2 %shard_map.296 = (bf16[64,2048]{1,0:T(8,128)(2,1)S(1)}, f32[1,2048]{1,0:T(1,128)S(1)}, bf16[64,2048]{1,0:T(8,128)(2,1)S(1)}, bf16[4,64,2048]{2,1,0:T(8,128)(2,1)S(1)}, bf16[3,64,2048]{2,1,0:T(8,128)(2,1)S(1)}) custom-call(f32[4,64,2048]{2,1,0:T(8,128)S(1)} %bitcast.265, f32[64,2048]{1,0:T(8,128)S(1)} %get-tuple-element.155.refs_1_, ...), custom_call_target="tpu_custom_call" | custom-call | tf_op jit(solution)/shard_map/pallas_call | solution.py:468
  666.2 7.2 broadcast_select_fusion.21
  675.2 4.5 convolution_add_fusion.2
  679.7 21.9 %shard_map.297 = (f32[64,2048]{1,0:T(8,128)S(1)}, f32[1,2048]{1,0:T(1,128)S(1)}, bf16[4,64,2048]{2,1,0:T(8,128)(2,1)S(1)}) custom-call(f32[4,64,2048]{2,1,0:T(8,128)S(1)} %bitcast.260, bf16[64,2048]{1,0:T(8,128)(2,1)S(1)} %get-tuple-element.161.gy, f32[64,2048]{1,0:T(8,128)S(1)} %get-tuple-element.143.middle, f32[1,2048]{1,0:T(1,128)S(1)} %bitcast.303), custom_call_target="tpu_custom_call" | custom-call | tf_op jit(solution)/shard_map/pallas_call | solution.py:468
  703.5 23.3 %shard_map.298 = (bf16[256,1664]{1,0:T(8,128)(2,1)S(1)}, f32[1,512]{1,0:T(1,128)S(1)}, f32[128,256]{1,0:T(8,128)S(1)}, f32[1,256]{1,0:T(1,128)S(1)}) custom-call(f32[256,512]{1,0:T(8,128)S(1)} %fusion.80.dgated_ref, f32[256,512]{1,0:T(8,128)S(1)} %get-tuple-element.140.inner_ref, f32[256,1664]{1,0:T(8,128)S(1)} %fusion.68.cat, ...), custom_call_target="tpu_custom_call" | custom-call | tf_op jit(solution)/shard_map/pallas_call | solution.py:468
  728.0 5.4 fusion.81
  733.5 32.7 %shard_map.299 = (bf16[64,2048]{1,0:T(8,128)(2,1)S(1)}, f32[1,2048]{1,0:T(1,128)S(1)}, bf16[64,2048]{1,0:T(8,128)(2,1)S(1)}, bf16[4,64,2048]{2,1,0:T(8,128)(2,1)S(1)}) custom-call(f32[4,64,2048]{2,1,0:T(8,128)S(1)} %bitcast.255, f32[64,2048]{1,0:T(8,128)S(1)} %get-tuple-element.167.d_middle, bf16[64,2048]{1,0:T(8,128)(2,1)S(1)} %copy-done.31, ...), custom_call_target="tpu_custom_call" | custom-call | tf_op jit(solution)/shard_map/pallas_call | solution.py:468
  766.9 7.0 broadcast_select_fusion.22
  777.5 21.6 %shard_map.300 = (f32[64,2048]{1,0:T(8,128)S(1)}, f32[1,2048]{1,0:T(1,128)S(1)}, bf16[4,64,2048]{2,1,0:T(8,128)(2,1)S(1)}) custom-call(f32[4,64,2048]{2,1,0:T(8,128)S(1)} %bitcast.261, bf16[64,2048]{1,0:T(8,128)(2,1)S(1)} %get-tuple-element.169.gy, f32[64,2048]{1,0:T(8,128)S(1)} %get-tuple-element.138.middle, f32[1,2048]{1,0:T(1,128)S(1)} %bitcast.304), custom_call_target="tpu_custom_call" | custom-call | tf_op jit(solution)/shard_map/pallas_call | solution.py:468
  800.8 12.0 shard_map.301
  815.0 5.4 fusion.84
  820.5 35.2 %shard_map.302 = (bf16[64,2048]{1,0:T(8,128)(2,1)S(1)}, f32[1,2048]{1,0:T(1,128)S(1)}, bf16[64,2048]{1,0:T(8,128)(2,1)S(1)}, bf16[4,64,2048]{2,1,0:T(8,128)(2,1)S(1)}) custom-call(f32[4,64,2048]{2,1,0:T(8,128)S(1)} %bitcast.256, f32[64,2048]{1,0:T(8,128)S(1)} %copy-done.78, bf16[64,2048]{1,0:T(8,128)(2,1)S(1)} %get-tuple-element.136.h, ...), custom_call_target="tpu_custom_call" | custom-call | tf_op jit(solution)/shard_map/pallas_call | solution.py:468
  858.2 2.3 broadcast_select_fusion.23
  862.3 4.0 convolution_convert_fusion.3
  866.3 4.0 convolution_convert_fusion.2
  872.9 4.0 convolution_convert_fusion.1
  884.4 4.7 add_convert_fusion.3.refs_4_
  889.1 4.7 add_convert_fusion.2.refs_8_
  893.9 7.2 add_convert_fusion.1.refs_4_.refs_2_
  901.1 34.3 %shard_map.303 = (f32[64,2048]{1,0:T(8,128)S(1)}, f32[1,2048]{1,0:T(1,128)S(1)}, bf16[4,64,2048]{2,1,0:T(8,128)(2,1)S(1)}, bf16[1,512,1408]{2,1,0:T(8,128)(2,1)S(1)}) custom-call(f32[4,64,2048]{2,1,0:T(8,128)S(1)} %bitcast.257, bf16[64,2048]{1,0:T(8,128)(2,1)S(1)} %copy-done.94, f32[64,2048]{1,0:T(8,128)S(1)} %copy-done.14, f32[1,2048]{1,0:T(1,128)S(1)} %bitcast.305, ...), custom_call_target="tpu_custom_call" | custom-call | tf_op jit(solution)/shard_map/pallas_call | solution.py:468
  939.2 56.0 %shard_map.304 = (bf16[256,1664]{1,0:T(8,128)(2,1)S(1)}, f32[1,512]{1,0:T(1,128)S(1)}, f32[128,256]{1,0:T(8,128)S(1)}, f32[1,256]{1,0:T(1,128)S(1)}, bf16[1,512,...) custom-call(f32[256,512]{1,0:T(8,128)S(1)} %fusion.86.refs_0_, f32[256,512]{1,0:T(8,128)S(1)} %copy-done.9, ...), custom_call_target="tpu_custom_call" | custom-call | tf_op jit(solution)/shard_map/pallas_call | solution.py:468
  997.0 2.3 copy-done.138
  999.3 4.6 convolution_convert_fusion
  1008.7 2.2 fusion.refs_5_
  1010.9 5.2 fusion.87
  1016.3 58.8 %shard_map.305 = (bf16[64,2048]{1,0:T(8,128)(2,1)S(1)}, f32[1,2048]{1,0:T(1,128)S(1)}, bf16[1,512,1408]{2,1,0:T(8,128)(2,1)S(1)}, bf16[512,1408]{1,0:T(8,128)(2,1)S(1)}) custom-call(f32[4,64,2048]{2,1,0:T(8,128)S(1)} %bitcast.266, f32[64,2048]{1,0:T(8,128)S(1)} %copy-done.80, bf16[64,2048]{1,0:T(8,128)(2,1)S(1)} %copy-done.11, f32[1,2048]{1,0:T(1,128)S(1)} %bitcast.313, ...), custom_call_target="tpu_custom_call" | custom-call | tf_op jit(solution)/shard_map/pallas_call | solution.py:468
  1077.8 4.9 bitcast_convert_fusion.1
  1082.9 2.4 add_convert_fusion.4.refs_1_
  1085.8 6.8 add_convert_fusion.refs_0_
  1092.6 124.0 %shard_map.306 = (bf16[512,1664]{1,0:T(8,128)(2,1)}, bf16[512,512]{1,0:T(8,128)(2,1)S(1)}, bf16[512,1408]{1,0:T(8,128)(2,1)S(1)}, bf16[3,4,64,2048]{3,2,1,0:T(8,...) custom-call(bf16[1024,1664]{1,0:T(8,128)(2,1)} %add_convert_fusion.r, ...), custom_call_target="tpu_custom_call" | custom-call | tf_op jit(solution)/shard_map/pallas_call | solution.py:1524
  1222.3 5.4 convert.10
  (602 shorter events, 99.6 us)
Async XLA Ops:
  0.6 11.0 copy-start.157
  0.7 11.0 copy-start.158
  0.7 11.0 copy-start.155
  2.9 8.9 copy-start.156
  2.9 9.0 copy-start.168
  2.9 9.2 copy-start.169
  2.9 9.2 copy-start.170
  2.9 9.2 copy-start.171
  2.9 9.2 copy-start.172
  2.9 9.3 copy-start.167
  2.9 117.3 %collective-permute-start = (bf16[3,64,2048]{2,1,0:T(8,128)(2,1)}, bf16[3,64,2048]{2,1,0:T(8,128)(2,1)}, u32[]{:S(2)}, u32[]{:S(2)}) collective-permute-start(bf16[3,64,2048]{2,1,0:T(8,128)(2,1)} %constant_dynamic-slice_fusion.2), channel_id=1, source_target_pairs={{8,16},{16,8},{9,17},{17,9},{10,18},{18,10},{11,19},{19,11},{12,20... | collective-permute-start | bytes 2359304 | tf_op jit(solution)/shard_map/ppermute | solution.py:1563
  7.1 558.0 %collective-permute-start.1 = (bf16[3,64,2048]{2,1,0:T(8,128)(2,1)}, bf16[3,64,2048]{2,1,0:T(8,128)(2,1)}, u32[]{:S(2)}, u32[]{:S(2)}) collective-permute-start(bf16[3,64,2048]{2,1,0:T(8,128)(2,1)} %constant_dynamic-slice_fusion.1), channel_id=1, source_target_pairs={{8,16},{16,8},{9,17},{17,9},{10,18},{18,10},{11,19},{19,11},{12,20... | collective-permute-start | bytes 2359304 | tf_op jit(solution)/shard_map/ppermute | solution.py:1563
  120.2 328.3 %copy-start.165 = (f32[512]{0:T(512)}, f32[512]{0:T(512)S(1)}, u32[]{:S(2)}) copy-start(f32[512]{0:T(512)S(1)} %get-tuple-element.316) | copy-start | bytes 6148
  121.9 86.6 %copy-start.10 = (bf16[64,2048]{1,0:T(8,128)(2,1)}, bf16[64,2048]{1,0:T(8,128)(2,1)S(1)}, u32[]{:S(2)}) copy-start(bf16[64,2048]{1,0:T(8,128)(2,1)S(1)} %get-tuple-element.314.refs_0_.refs_1_.refs_2_) | copy-start | bytes 786436
  165.3 40.3 %copy-start.1 = (f32[256,1664]{1,0:T(8,128)}, f32[256,1664]{1,0:T(8,128)S(1)}, u32[]{:S(2)}) copy-start(f32[256,1664]{1,0:T(8,128)S(1)} %fusion.60.refs_0_.refs_2_) | copy-start | bytes 5111812
  249.6 65.9 %copy-start.13 = (f32[64,2048]{1,0:T(8,128)}, f32[64,2048]{1,0:T(8,128)S(1)}, u32[]{:S(2)}) copy-start(f32[64,2048]{1,0:T(8,128)S(1)} %get-tuple-element.133.middle.refs_2_) | copy-start | bytes 1572868
  305.7 8.0 slice-start.14
  315.5 78.5 %slice-start = ((s8[5767168]{0:T(1024)(128)(4,1)}), s8[4194304]{0:T(1024)(128)(4,1)S(1)}, s32[]{:S(2)}) async-start(s8[5767168]{0:T(1024)(128)(4,1)} %bitcast.231), calls=%async_computation | async-start | bytes 8388608
  350.7 43.3 %slice-start.1 = ((s8[5767168]{0:T(1024)(128)(4,1)}), s8[1572864]{0:T(1024)(128)(4,1)S(1)}, s32[]{:S(2)}) async-start(s8[5767168]{0:T(1024)(128)(4,1)} %bitcast.231), calls=%async_computation.1 | async-start | bytes 3145728
  356.1 10.9 copy-start.146
  368.9 27.0 %slice-start.2 = ((s8[5767168]{0:T(1024)(128)(4,1)}), s8[1572864]{0:T(1024)(128)(4,1)S(1)}, s32[]{:S(2)}) async-start(s8[5767168]{0:T(1024)(128)(4,1)} %bitcast.233), calls=%async_computation.2 | async-start | bytes 3145728
  431.4 19.1 %copy-start.30 = (bf16[64,2048]{1,0:T(8,128)(2,1)}, bf16[64,2048]{1,0:T(8,128)(2,1)S(1)}, u32[]{:S(2)}) copy-start(bf16[64,2048]{1,0:T(8,128)(2,1)S(1)} %get-tuple-element.141.h) | copy-start | bytes 786436
  450.5 26.5 %slice-start.4 = ((s8[5767168]{0:T(1024)(128)(4,1)}), s8[1572864]{0:T(1024)(128)(4,1)S(1)}, s32[]{:S(2)}) async-start(s8[5767168]{0:T(1024)(128)(4,1)} %bitcast.235), calls=%async_computation.4 | async-start | bytes 3145728
  512.0 18.3 %copy-start.63 = (bf16[64,2048]{1,0:T(8,128)(2,1)}, bf16[64,2048]{1,0:T(8,128)(2,1)S(1)}, u32[]{:S(2)}) copy-start(bf16[64,2048]{1,0:T(8,128)(2,1)S(1)} %get-tuple-element.146.h.refs_2_) | copy-start | bytes 786436
  517.6 10.8 copy-start.148
  517.6 10.8 copy-start.166
  529.5 27.5 %slice-start.6 = ((s8[5767168]{0:T(1024)(128)(4,1)}), s8[1572864]{0:T(1024)(128)(4,1)S(1)}, s32[]{:S(2)}) async-start(s8[5767168]{0:T(1024)(128)(4,1)} %bitcast.237), calls=%async_computation.6 | async-start | bytes 3145728
  566.7 28.6 %slice-start.8 = ((s8[5767168]{0:T(1024)(128)(4,1)}), s8[1572864]{0:T(1024)(128)(4,1)S(1)}, s32[]{:S(2)}) async-start(s8[5767168]{0:T(1024)(128)(4,1)} %bitcast.239), calls=%async_computation.8 | async-start | bytes 3145728
  587.5 7.9 slice-start.9
  618.9 16.3 %copy-start.106 = (f32[1,2048]{1,0:T(1,128)}, f32[1,2048]{1,0:T(1,128)S(1)}, u32[]{:S(2)}) copy-start(f32[1,2048]{1,0:T(1,128)S(1)} %get-tuple-element.212) | copy-start | bytes 24580
  641.9 24.3 %copy-start.176 = (bf16[256,1408]{1,0:T(8,128)(2,1)S(1)}, bf16[256,1408]{1,0:T(8,128)(2,1)}, u32[]{:S(2)}) copy-start(bf16[256,1408]{1,0:T(8,128)(2,1)} %copy-done.175) | copy-start | bytes 2162692
  641.9 24.3 %copy-start.182 = (bf16[256,1408]{1,0:T(8,128)(2,1)S(1)}, bf16[256,1408]{1,0:T(8,128)(2,1)}, u32[]{:S(2)}) copy-start(bf16[256,1408]{1,0:T(8,128)(2,1)} %copy-done.181) | copy-start | bytes 2162692
  701.7 25.1 %copy-start.110 = (f32[1,2048]{1,0:T(1,128)}, f32[1,2048]{1,0:T(1,128)S(1)}, u32[]{:S(2)}) copy-start(f32[1,2048]{1,0:T(1,128)S(1)} %get-tuple-element.213) | copy-start | bytes 24580
  728.0 47.7 %slice-start.10 = ((s8[5767168]{0:T(1024)(128)(4,1)}), s8[1572864]{0:T(1024)(128)(4,1)S(1)}, s32[]{:S(2)}) async-start(s8[5767168]{0:T(1024)(128)(4,1)} %bitcast.241), calls=%async_computation.10 | async-start | bytes 3145728
  733.4 33.4 %copy-start.178 = (bf16[256,1408]{1,0:T(8,128)(2,1)S(1)}, bf16[256,1408]{1,0:T(8,128)(2,1)}, u32[]{:S(2)}) copy-start(bf16[256,1408]{1,0:T(8,128)(2,1)} %copy-done.177) | copy-start | bytes 2162692
  733.4 33.4 %copy-start.184 = (bf16[256,1408]{1,0:T(8,128)(2,1)S(1)}, bf16[256,1408]{1,0:T(8,128)(2,1)}, u32[]{:S(2)}) copy-start(bf16[256,1408]{1,0:T(8,128)(2,1)} %copy-done.183) | copy-start | bytes 2162692
  766.9 8.8 slice-start.11
  799.2 13.6 %copy-start.77 = (f32[64,2048]{1,0:T(8,128)}, f32[64,2048]{1,0:T(8,128)S(1)}, u32[]{:S(2)}) copy-start(f32[64,2048]{1,0:T(8,128)S(1)} %get-tuple-element.175.d_middle) | copy-start | bytes 1572868
  799.2 13.6 %copy-start.114 = (f32[1,2048]{1,0:T(1,128)}, f32[1,2048]{1,0:T(1,128)S(1)}, u32[]{:S(2)}) copy-start(f32[1,2048]{1,0:T(1,128)S(1)} %get-tuple-element.214) | copy-start | bytes 24580
  799.2 57.3 %slice-start.22 = ((s8[5767168]{0:T(1024)(128)(4,1)}), s8[1572864]{0:T(1024)(128)(4,1)S(1)}, s32[]{:S(2)}) async-start(s8[5767168]{0:T(1024)(128)(4,1)} %bitcast.253), calls=%async_computation.22 | async-start | bytes 3145728
  815.0 41.5 %slice-start.23 = ((s8[5767168]{0:T(1024)(128)(4,1)}), s8[4194304]{0:T(1024)(128)(4,1)S(1)}, s32[]{:S(2)}) async-start(s8[5767168]{0:T(1024)(128)(4,1)} %bitcast.253), calls=%async_computation.23 | async-start | bytes 8388608
  820.4 35.3 %copy-start.54 = (bf16[4,64,2048]{2,1,0:T(8,128)(2,1)S(1)}, bf16[4,64,2048]{2,1,0:T(8,128)(2,1)}, u32[]{:S(2)}) copy-start(bf16[4,64,2048]{2,1,0:T(8,128)(2,1)} %copy-done.53) | copy-start | bytes 3145732
  866.3 18.0 %collective-permute-start.2 = (bf16[1024,1408]{1,0:T(8,128)(2,1)}, bf16[1024,1408]{1,0:T(8,128)(2,1)}, u32[]{:S(2)}, u32[]{:S(2)}) collective-permute-start(bf16[1024,1408]{1,0:T(8,128)(2,1)} %convolution_convert_fusion.3), channel_id=1, source_target_pairs={{0,16},{16,0},{1,17},{17,1},{2,18},{18,2},{3,19},{19,3},{4,20},{20... | collective-permute-start | bytes 8650760 | tf_op jit(solution)/shard_map/ppermute | solution.py:1567
  870.4 18.7 %collective-permute-start.3 = (bf16[1024,1408]{1,0:T(8,128)(2,1)}, bf16[1024,1408]{1,0:T(8,128)(2,1)}, u32[]{:S(2)}, u32[]{:S(2)}) collective-permute-start(bf16[1024,1408]{1,0:T(8,128)(2,1)} %convolution_convert_fusion.2), channel_id=1, source_target_pairs={{0,16},{16,0},{1,17},{17,1},{2,18},{18,2},{3,19},{19,3},{4,20},{20... | collective-permute-start | bytes 8650760 | tf_op jit(solution)/shard_map/ppermute | solution.py:1567
  876.9 17.0 %collective-permute-start.4 = (bf16[1024,1408]{1,0:T(8,128)(2,1)}, bf16[1024,1408]{1,0:T(8,128)(2,1)}, u32[]{:S(2)}, u32[]{:S(2)}) collective-permute-start(bf16[1024,1408]{1,0:T(8,128)(2,1)} %convolution_convert_fusion.1), channel_id=1, source_target_pairs={{0,16},{16,0},{1,17},{17,1},{2,18},{18,2},{3,19},{19,3},{4,20},{20... | collective-permute-start | bytes 8650760 | tf_op jit(solution)/shard_map/ppermute | solution.py:1567
  893.8 43.7 %copy-start.3 = (bf16[1024,1408]{1,0:T(8,128)(2,1)}, bf16[1024,1408]{1,0:T(8,128)(2,1)S(1)}, u32[]{:S(2)}) copy-start(bf16[1024,1408]{1,0:T(8,128)(2,1)S(1)} %add_convert_fusion.2.refs_8_) | copy-start | bytes 8650756
  901.1 34.3 %copy-start.50 = (bf16[4,64,2048]{2,1,0:T(8,128)(2,1)S(1)}, bf16[4,64,2048]{2,1,0:T(8,128)(2,1)}, u32[]{:S(2)}) copy-start(bf16[4,64,2048]{2,1,0:T(8,128)(2,1)} %copy-done.49) | copy-start | bytes 3145732
  901.1 34.3 %copy-start.52 = (bf16[4,64,2048]{2,1,0:T(8,128)(2,1)S(1)}, bf16[4,64,2048]{2,1,0:T(8,128)(2,1)}, u32[]{:S(2)}) copy-start(bf16[4,64,2048]{2,1,0:T(8,128)(2,1)} %copy-done.51) | copy-start | bytes 3145732
  939.2 56.0 %copy-start.67 = (bf16[256,1664]{1,0:T(8,128)(2,1)S(1)}, bf16[256,1664]{1,0:T(8,128)(2,1)}, u32[]{:S(2)}) copy-start(bf16[256,1664]{1,0:T(8,128)(2,1)} %copy-done.66) | copy-start | bytes 2555908
  939.2 56.0 %copy-start.69 = (bf16[256,1664]{1,0:T(8,128)(2,1)S(1)}, bf16[256,1664]{1,0:T(8,128)(2,1)}, u32[]{:S(2)}) copy-start(bf16[256,1664]{1,0:T(8,128)(2,1)} %copy-done.68) | copy-start | bytes 2555908
  939.2 56.0 %copy-start.71 = (bf16[256,1664]{1,0:T(8,128)(2,1)S(1)}, bf16[256,1664]{1,0:T(8,128)(2,1)}, u32[]{:S(2)}) copy-start(bf16[256,1664]{1,0:T(8,128)(2,1)} %copy-done.70) | copy-start | bytes 2555908
  1003.9 81.4 %collective-permute-start.5 = (bf16[1024,1664]{1,0:T(8,128)(2,1)}, bf16[1024,1664]{1,0:T(8,128)(2,1)}, u32[]{:S(2)}, u32[]{:S(2)}) collective-permute-start(bf16[1024,1664]{1,0:T(8,128)(2,1)} %convolution_convert_fusion), channel_id=1, source_target_pairs={{0,16},{16,0},{1,17},{17,1},{2,18},{18,2},{3,19},{19,3},{4,20},{20... | collective-permute-start | bytes 10223624 | tf_op jit(solution)/shard_map/ppermute | solution.py:1567
  1007.1 75.8 %collective-permute-start.6 = (bf16[1024,512]{1,0:T(8,128)(2,1)}, bf16[1024,512]{1,0:T(8,128)(2,1)}, u32[]{:S(2)}, u32[]{:S(2)}) collective-permute-start(bf16[1024,512]{1,0:T(8,128)(2,1)} %fusion.18), channel_id=1, source_target_pairs={{0,16},{16,0},{1,17},{17,1},{2,18},{18,2},{3,19},{19,3},{4,20},{20... | collective-permute-start | bytes 3145736 | tf_op jit(solution)/shard_map/ppermute | solution.py:1567
  1016.2 61.1 %copy-start.107 = (f32[1,2048]{1,0:T(1,128)S(1)}, f32[1,2048]{1,0:T(1,128)}, u32[]{:S(2)}) copy-start(f32[1,2048]{1,0:T(1,128)} %copy-done.106) | copy-start | bytes 24580
  1016.2 61.1 %copy-start.109 = (f32[1,2048]{1,0:T(1,128)S(1)}, f32[1,2048]{1,0:T(1,128)}, u32[]{:S(2)}) copy-start(f32[1,2048]{1,0:T(1,128)} %copy-done.108) | copy-start | bytes 24580
  1016.2 61.1 %copy-start.111 = (f32[1,2048]{1,0:T(1,128)S(1)}, f32[1,2048]{1,0:T(1,128)}, u32[]{:S(2)}) copy-start(f32[1,2048]{1,0:T(1,128)} %copy-done.110) | copy-start | bytes 24580
  1016.2 61.1 %copy-start.113 = (f32[1,2048]{1,0:T(1,128)S(1)}, f32[1,2048]{1,0:T(1,128)}, u32[]{:S(2)}) copy-start(f32[1,2048]{1,0:T(1,128)} %copy-done.112) | copy-start | bytes 24580
  1016.2 61.1 %copy-start.115 = (f32[1,2048]{1,0:T(1,128)S(1)}, f32[1,2048]{1,0:T(1,128)}, u32[]{:S(2)}) copy-start(f32[1,2048]{1,0:T(1,128)} %copy-done.114) | copy-start | bytes 24580
  1016.2 61.1 %copy-start.117 = (f32[1,2048]{1,0:T(1,128)S(1)}, f32[1,2048]{1,0:T(1,128)}, u32[]{:S(2)}) copy-start(f32[1,2048]{1,0:T(1,128)} %copy-done.116) | copy-start | bytes 24580
  1016.2 61.1 %copy-start.119 = (f32[1,2048]{1,0:T(1,128)S(1)}, f32[1,2048]{1,0:T(1,128)}, u32[]{:S(2)}) copy-start(f32[1,2048]{1,0:T(1,128)} %copy-done.118) | copy-start | bytes 24580
  1016.2 61.2 %copy-start.123 = (f32[1,512]{1,0:T(1,128)S(1)}, f32[1,512]{1,0:T(1,128)}, u32[]{:S(2)}) copy-start(f32[1,512]{1,0:T(1,128)} %copy-done.122) | copy-start | bytes 6148
  1016.2 61.2 %copy-start.125 = (f32[1,512]{1,0:T(1,128)S(1)}, f32[1,512]{1,0:T(1,128)}, u32[]{:S(2)}) copy-start(f32[1,512]{1,0:T(1,128)} %copy-done.124) | copy-start | bytes 6148
  1016.3 61.2 %copy-start.127 = (f32[1,512]{1,0:T(1,128)S(1)}, f32[1,512]{1,0:T(1,128)}, u32[]{:S(2)}) copy-start(f32[1,512]{1,0:T(1,128)} %copy-done.126) | copy-start | bytes 6148
  1077.6 5.2 collective-permute-start.7
  (180 other events, 569.0 us)

commit v3 on v2

--- a/solution.py
+++ b/solution.py
@@ -12,6 +12,7 @@
 LANES = 128
 STRIP = 64
 CHUNKS = 2
+ORDER = (1, 0)
 DIRECT, SUMMED, PASSED = 0, 1, 2
 WINDOW = 2
 
@@ -129,10 +130,10 @@
 
     def start(self):
         peers = self.peers
-        for c in range(CHUNKS):
+        for c in ORDER:
             self.send[PASSED, c] = self.part[peers.opposite, self.rows(c), :].astype(bf16)
             self.copy(PASSED, c).start()
-        for c in range(CHUNKS):
+        for c in ORDER:
             self.send[DIRECT, c] = self.part[peers.beside[c], self.rows(c), :].astype(bf16)
             self.copy(DIRECT, c).start()
         if self.fine is not None:
@@ -144,7 +145,7 @@
                 def _():
                     self.fine_copy(d).start()
 
-        for c in range(CHUNKS):
+        for c in ORDER:
             self.copy(PASSED, c).wait_recv()
             own = self.part[peers.beside[1 - c], self.rows(c), :].astype(f32)
             self.send[SUMMED, c] = (own + self.land[PASSED, c].astype(f32)).astype(bf16)
@@ -170,7 +171,7 @@
         return total[self.rows(c), :]
 
     def drain(self):
-        for c in range(CHUNKS):
+        for c in ORDER:
             for kind in (PASSED, DIRECT, SUMMED):
                 self.copy(kind, c).wait_send()
         if self.fine is not None:
@@ -207,10 +208,10 @@
             self.copy(kind, c).start()
 
     def finish(self):
-        for c in range(CHUNKS):
+        for c in ORDER:
             self.copy(c, c).wait_recv()
             self.copy(PASSED, c).start()
-        for c in range(CHUNKS):
+        for c in ORDER:
             self.copy(1 - c, c).wait_recv()
             self.copy(PASSED, c).wait_recv()
             for kind in range(3):
@@ -235,7 +236,7 @@
     if extra is not None:
         extra.start()
     share = Share(peers, full, share_sems)
-    for c in range(CHUNKS):
+    for c in ORDER:
         rows = slice(c * share.step, (c + 1) * share.step)
         share.start(c, normed_rows(h[rows, :].astype(f32), gain[...]).astype(bf16))
     share.finish()
@@ -252,7 +253,7 @@
     reduced = Sum(peers, part, send, land, sems, fine, fine_sems)
     share = Share(peers, full, share_sems)
     reduced.start()
-    for c in range(CHUNKS):
+    for c in ORDER:
         rows = reduced.rows(c)
         value = h[rows, :].astype(f32) + reduced.finish(c, total)
         middle[rows, :] = value
@@ -288,7 +289,7 @@
     reduced = Sum(peers, part, send, land, sems, fine, fine_sems)
     share = Share(peers, full, share_sems)
     reduced.start()
-    for c in range(CHUNKS):
+    for c in ORDER:
         rows = reduced.rows(c)
         relay = relay_rows(y, relayed, relay_sems, c, 1)
 
@@ -310,7 +311,7 @@
 
     @pl.when(stage == 0)
     def _():
-        for c in range(CHUNKS):
+        for c in ORDER:
             relay_rows(y, relayed, relay_sems, c, 1).wait_send()
     reduced.drain()
 
@@ -323,9 +324,9 @@
     reduced = Sum(peers, part, send, land, sems, fine, fine_sems)
     share = Share(peers, full, share_sems)
     reduced.start()
-    for c in range(CHUNKS):
+    for c in ORDER:
         share.start(c, gy[reduced.rows(c), :])
-    for c in range(CHUNKS):
+    for c in ORDER:
         rows = reduced.rows(c)
         y[rows, :] = (middle[rows, :] + reduced.finish(c, total)).astype(bf16)
     share.finish()
@@ -342,7 +343,7 @@
     share = Share(peers, full, share_sems)
     reduced.start()
     gains = jnp.zeros(gain_part.shape, f32)
-    for c in range(CHUNKS):
+    for c in ORDER:
         rows = reduced.rows(c)
         d_u, g = norm_back(reduced.finish(c, total), middle[rows, :], gain[...])
         value = gy[rows, :].astype(f32) + d_u
@@ -374,16 +375,13 @@
     sems,
     share_sems,
     relay_sems,
-    extra=None,
 ):
     peers = Peers(peers_n)
     stage = lax.axis_index("stage")
-    peers.enter(0, extra)
+    peers.enter(0)
     reduced = Sum(peers, part, send, land, sems)
     share = Share(peers, full, share_sems)
     reduced.start()
-    if extra is not None:
-        extra.start()
     gain_part[...] = jnp.zeros(gain_part.shape, f32)
 
     def finish(c):
@@ -392,7 +390,7 @@
         grad[rows, :] = (d_middle[rows, :] + d_u).astype(bf16)
         gain_part[...] += g
 
-    for c in range(CHUNKS):
+    for c in ORDER:
         rows = reduced.rows(c)
         relay = relay_rows(grad, relayed, relay_sems, c, 0)
 
@@ -414,11 +412,9 @@
 
     @pl.when(stage == 1)
     def _():
-        for c in range(CHUNKS):
+        for c in ORDER:
             relay_rows(grad, relayed, relay_sems, c, 0).wait_send()
     reduced.drain()
-    if extra is not None:
-        extra.finish()
 
 
 def backward_last_kernel(
@@ -430,7 +426,7 @@
     reduced = Sum(peers, part, send, land, sems)
     reduced.start()
     gains = jnp.zeros(gain_part.shape, f32)
-    for c in range(CHUNKS):
+    for c in ORDER:
         rows = reduced.rows(c)
         d_u, g = norm_back(reduced.finish(c, total), h[rows, :].astype(f32), gain[...])
         grad[rows, :] = (d_middle[rows, :] + d_u).astype(bf16)
@@ -567,20 +563,19 @@
         )
         return d_middle, gain_part, self.flat(full), *more
 
-    def backward_end(self, part, d_middle, h, gain, own, ident=7, extra=None):
-        grad, gain_part, gy, full, *more = kernel_call(
+    def backward_end(self, part, d_middle, h, gain, own):
+        grad, gain_part, gy, full = kernel_call(
             partial(backward_end_kernel, self.peers),
             [self.slice_b, self.gain_f, self.slice_b, self.full],
             self.reduce + self.total + self.relayed + [self.many] * 2 + [self.relay],
-            ident,
+            7,
             self.parts(part),
             d_middle,
             h,
             gain,
             own,
-            extra=extra,
-        )
-        return grad, gain_part, gy, self.flat(full), *more
+        )
+        return grad, gain_part, gy, self.flat(full)
 
     def backward_last(self, part, d_middle, h, gain, extra=None):
         return kernel_call(
@@ -1578,6 +1573,15 @@
     return (rows_for(section) + theirs.astype(f32)).astype(bf16)
 
 
+def range_sum(total):
+    if lax.axis_size("q") != 2:
+        return lax.psum_scatter(total, "q", scatter_dimension=0, tiled=True)
+    place, high = lax.axis_index("q"), total.shape[0] // 2
+    away = exchanged(lax.dynamic_slice_in_dim(total, (1 - place) * high, high, 0), "q")
+    own = lax.dynamic_slice_in_dim(total, place * high, high, 0)
+    return (own.astype(f32) + away.astype(f32)).astype(bf16)
+
+
 def tiles_of(array, lead, low):
     width = -(-array.shape[1] // (low * LANES)) * LANES
     array = jnp.pad(array, ((0, 0), (0, low * width - array.shape[1])))
@@ -1707,41 +1711,47 @@
         saved.append(dict(d_feed=d_feed, d_gate=d_gate, d_upper=d_upper))
         if step == micro:
             feed_in = rows_of("feed_in")
+            gate_total = core_sum(feed_in, rows_of("d_gate"))
+            gate_total, feed_in, d_feed_rows = lax.optimization_barrier(
+                (gate_total, feed_in, rows_of("d_feed"))
+            )
             feed_totals = [
-                core_sum(feed_in, rows_of("d_gate")),
+                gate_total,
                 core_sum(feed_in, rows_of("d_upper")),
-                core_sum(rows_of("d_feed"), rows_of("hidden")),
+                core_sum(d_feed_rows, rows_of("hidden")),
             ]
-            feed_totals, part = lax.optimization_barrier((feed_totals, part))
+            gate_sum = range_sum(feed_totals[0])
+            feed_totals, gate_sum, part = lax.optimization_barrier((feed_totals, gate_sum, part))
         last = step == micro
         d_middle, feed_part, d_mixed, *away_0 = calls.backward_mid(
             part, gy, now["middle"], w["feed_gain"],
-            **(dict(ident=16, extra=along_start(half, feed_totals[0])) if last else {}),
-        )
+            **(dict(ident=16, extra=along_start(half, feed_totals[1], gate_sum)) if last else {}),
+            **(dict(ident=18, extra=home_start(half, worked)) if step == 1 else {}),
+        )
+        if step == 1:
+            outputs_in = jnp.where(lax.axis_index("section") == stage, worked, away_0[0])
         if last:
-            gate_sum = with_away(feed_totals[0], away_0[0])
+            upper_sum = with_away(feed_totals[1], away_0[0])
         d_gated = dot_plain(d_mixed, w["output"])
         d_cat, head_part, up_part, bias_part, *away_1 = mixer_backward(
             ranges, half, cuts, d_gated, now["inner"], now["cat"], w["up"], w["head_gain"],
             now["cumul"], now["logits"], now["states"],
-            **(dict(ident=17, extra=along_start(half, feed_totals[1], gate_sum)) if last else {}),
+            **(dict(ident=17, extra=along_start(half, feed_totals[2], upper_sum)) if last else {}),
         )
         part = dot_right(d_cat, w["cat"])
         saved[-1].update(d_mixed=d_mixed, d_cat=d_cat)
         if step < micro:
             later = micro - 2 - step
             own = own_cot[later] if later >= 0 else jnp.zeros_like(own_cot[0])
-            grad, mixer_part, gy, d_feed, *more = calls.backward_end(
+            grad, mixer_part, gy, d_feed = calls.backward_end(
                 part, d_middle, now["h"], w["mixer_gain"], own,
-                **(dict(ident=18, extra=home_start(half, worked)) if step == 0 else {}),
             )
-            if step == 0:
-                outputs_in = jnp.where(lax.axis_index("section") == stage, worked, more[0])
         else:
-            upper_sum = with_away(feed_totals[1], away_1[0])
+            lower_sum = with_away(feed_totals[2], away_1[0])
+            output_total = core_sum(rows_of("d_mixed"), rows_of("gated"))
             grad, mixer_part, *away_2 = calls.backward_last(
                 part, d_middle, now["h"], w["mixer_gain"],
-                along_start(half, feed_totals[2], upper_sum),
+                along_start(half, output_total, lower_sum),
             )
         grads.append(grad)
         saved[-1].update(
@@ -1753,8 +1763,8 @@
 
     totals = [
         core_sum(rows_of("normed"), rows_of("d_cat")),
-        core_sum(rows_of("d_mixed"), rows_of("gated")),
-    ] + feed_totals[2:]
+        output_total,
+    ]
     small_grads = [
         sum_of("up")[:rank].T,
         sum_of("bias"),
@@ -1772,14 +1782,15 @@
     small_grads = lax.dynamic_slice_in_dim(small_grads, section * half, half, 0) + theirs
 
     places = [outputs_in, picked(jnp.stack(grads[:0:-1]), jnp.stack(grads[micro - 1 :: -1]))]
-    cat_grad, output_grad, lower_grad, outputs, input_grads, down, own, pooled = finish(
+    cat_grad, output_grad, outputs, input_grads, down, own, pooled = finish(
         half, peers, 13, totals, away_2[:1], places, small_grads, cuts.rank
     )
     stays = section == stage
-    gate_grad = jnp.where(stays, gate_sum, away_1[1]).astype(f32)
-    upper_grad = jnp.where(stays, upper_sum, away_2[1]).astype(f32)
-    cat_grad, output_grad, lower_grad, input_grads = (
-        g.astype(f32) for g in (cat_grad, output_grad, lower_grad, input_grads)
+    gate_grad = jnp.where(stays, gate_sum, away_0[1]).astype(f32)
+    upper_grad = jnp.where(stays, upper_sum, away_1[1]).astype(f32)
+    lower_grad = jnp.where(stays, lower_sum, away_2[1]).astype(f32)
+    cat_grad, output_grad, input_grads = (
+        g.astype(f32) for g in (cat_grad, output_grad, input_grads)
     )
     own, pooled = own.reshape(-1), pooled.reshape(-1)
 

time: 1250 us -> 1230 us (0.984)
  Pallas kernels: 971 us -> 935 us
  waiting for transfers between devices: 0.02 us -> 26.1 us
    ppermute x6 -> x7, waiting for transfers between devices: 0.02 us -> 26.1 us  [exchanged(): return lax.ppermute(array, axis, [(0, 1), (1, 0)])]
    pallas_call x1, Pallas kernels: 124 us -> 99.7 us  [finish(): pl.pallas_call(partial(finish_kernel, half, count, come, places, lanes),...]
    unnamed x485 -> x517, local copies, waits for them, and re-layouts: 42.1 us -> 44.3 us
  transfers between devices with their start and end apart: 8 -> 9, of which waited for: 0 -> 2; matrix products, arithmetic and copies ran while one was open for 9% -> 8% of each run, Pallas kernels for 43% -> 41%
where the time goes in v3:
time: 1230 us; the launch traced here: 1220 us
  Pallas kernels  935 us (76%)
  matrix products  157 us (13%)
  local copies, waits for them, and re-layouts  54.1 us (4%)
  other arithmetic  37.3 us (3%)
  waiting for transfers between devices  26.1 us (2%)
    pallas_call x25, Pallas kernels, kernel_call(): pl.pallas_call(body, out_shape=outs, in_specs=in_specs, out_specs=out_spe...  676 us
    pallas_call x1, Pallas kernels, gather_weights(): pl.pallas_call(partial(gather_kernel, half, count), out_shape=[shape((2 *...  103 us
    pallas_call x1, Pallas kernels, finish(): pl.pallas_call(partial(finish_kernel, half, count, come, places, lanes),...  99.7 us
    dot_general x20, matrix products, dot_plain(): return jnp.dot(left, right, preferred_element_type=f32)  70.5 us
    pallas_call x1, Pallas kernels, gather_end(): pl.pallas_call(partial(gather_end_kernel, half, count, rows), out_shape=[...  56 us
    dot_general x20, matrix products, dot_right(): lax.dot_general(left, right, (((1,), (1,)), ((), ())), preferred_element_...  46.4 us
    unnamed x517, local copies, waits for them, and re-layouts  44.3 us
    dot_general x10, matrix products, dot_left(): lax.dot_general(left, right, (((0,), (0,)), ((), ())), preferred_element_...  39.6 us
  transfers between devices with their start and end apart: 9, of which 2 were waited for; matrix products, arithmetic and copies ran while one was open for 8% of the time, Pallas kernels for 41%

profile of v3, /device:TPU:24, one launch (start us, length us, event | category | flops | bytes accessed | tf_op | source)
XLA Modules:
  0.0 1221.6 jit_solution(7496045930498165422)
XLA Ops:
  6.2 4.5 collective-permute-start.1
  12.0 103.2 %shard_map.279 = (bf16[64,256]{1,0:T(8,128)(2,1)S(1)}, bf16[2048,1664]{1,0:T(8,128)(2,1)S(1)}, bf16[2048,512]{1,0:T(8,128)(2,1)S(1)}) custom-call(bf16[16,256]{1,0:T(8,128)(2,1)S(1)} %squeeze_reshape.3.refs_0_, bf16[512,1664]{1,0:T(8,128)(2,1)S(1)} %pad.17.refs_1_, bf16[512,512]{1,0:T(8,128)(2,1)S(1)} %bitcast.306), custom_call_target="tpu_custom_call" | custom-call | tf_op jit(solution)/shard_map/pallas_call | solution.py:1037
  115.2 2.8 copy-done.160
  121.6 35.7 %shard_map.280 = (bf16[4,64,2048]{2,1,0:T(8,128)(2,1)S(1)}, bf16[2048,1408]{1,0:T(8,128)(2,1)S(1)}) custom-call(bf16[64,2048]{1,0:T(8,128)(2,1)S(1)} %get-tuple-element.320.refs_0_.refs_1_.refs_2_, f32[1,2048]{1,0:T(1,128)S(1)} %bitcast.290, bf16[512,1408]{1,0:T(8,128)(2,1)S(1)} %bitcast.260), custom_call_target="tpu_custom_call" | custom-call | tf_op jit(solution)/shard_map/pallas_call | solution.py:464
  157.3 2.5 copy-done.5
  159.8 5.4 fusion.60.refs_0_.refs_2_
  165.2 39.9 %shard_map.281 = (f32[256,512]{1,0:T(8,128)S(1)}, f32[256,256]{1,0:T(8,128)S(1)}, f32[256,256]{1,0:T(8,128)S(1)}, bf16[5,512,256]{2,1,0:T(8,128)(2,1)S(1)}, bf16[2048,1408]{1,0:T(8,128)(2,1)S(1)}) custom-call(f32[256,1664]{1,0:T(8,128)S(1)} %fusion.60.refs_0_.refs_2_, f32[128,256]{1,0:T(8,128)S(1)} %pad.18.refs_1_.up.refs_3_, ...), custom_call_target="tpu_custom_call" | custom-call | tf_op jit(solution)/shard_map/pallas_call | solution.py:464
  205.1 2.5 copy-done.6
  209.9 36.8 %shard_map.282 = (f32[64,2048]{1,0:T(8,128)S(1)}, bf16[4,64,2048]{2,1,0:T(8,128)(2,1)S(1)}, bf16[2048,1408]{1,0:T(8,128)(2,1)S(1)}) custom-call(f32[4,64,2048]{2,1,0:T(8,128)S(1)} %bitcast.227, bf16[64,2048]{1,0:T(8,128)(2,1)S(1)} %get-tuple-element.320.refs_0_.refs_1_.refs_2_, f32[1,2048]{1,0:T(1,128)S(1)} %bitcast.298, bf16[512,1408]{1,0:T(8,128)(2,1)S(1)} %bitcast.261), custom_call_target="tpu_custom_call" | custom-call | tf_op jit(solution)/shard_map/pallas_call | solution.py:464
  246.7 2.5 copy-done.8
  250.1 56.0 %shard_map.283 = (bf16[2048,1408]{1,0:T(8,128)(2,1)}, bf16[2048,1408]{1,0:T(8,128)(2,1)}, bf16[2048,1408]{1,0:T(8,128)(2,1)}) custom-call(bf16[2048,1408]{1,0:T(8,128)(2,1)} %copy-done.5, bf16[2048,1408]{1,0:T(8,128)(2,1)} %copy-done.6, bf16[2048,1408]{1,0:T(8,128)(2,1)} %copy-done.8), custom_call_target="tpu_custom_call", output_to_operand_aliasing={{0}: (0, {}), {1}: (1, {}), {2}: (2, {})} | custom-call | tf_op jit(solution)/shard_map/pallas_call | solution.py:1195
  306.2 4.9 fusion.62
  311.1 3.0 multiply_convert_fusion.11
  316.0 34.6 %shard_map.284 = (bf16[64,2048]{1,0:T(8,128)(2,1)S(1)}, bf16[64,2048]{1,0:T(8,128)(2,1)S(1)}, bf16[4,64,2048]{2,1,0:T(8,128)(2,1)S(1)}) custom-call(f32[4,64,2048]{2,1,0:T(8,128)S(1)} %bitcast.255, f32[64,2048]{1,0:T(8,128)S(1)} %get-tuple-element.136.middle.refs_2_, f32[1,2048]{1,0:T(1,128)S(1)} %bitcast.291, bf16[64,2048]{1,0:T(8,128)(2,1)S(1)} %copy-done.56), custom_call_target="tpu_custom_call" | custom-call | tf_op jit(solution)/shard_map/pallas_call | solution.py:464
  351.5 5.1 fusion.64.cat
  356.7 10.7 shard_map.285
  369.5 24.7 %shard_map.286 = (f32[64,2048]{1,0:T(8,128)S(1)}, bf16[4,64,2048]{2,1,0:T(8,128)(2,1)S(1)}) custom-call(f32[4,64,2048]{2,1,0:T(8,128)S(1)} %bitcast.229, bf16[64,2048]{1,0:T(8,128)(2,1)S(1)} %get-tuple-element.139.h, f32[1,2048]{1,0:T(1,128)S(1)} %bitcast.299), custom_call_target="tpu_custom_call" | custom-call | tf_op jit(solution)/shard_map/pallas_call | solution.py:464
  396.1 3.2 broadcast_select_fusion.20
  401.1 28.7 %shard_map.287 = (bf16[64,2048]{1,0:T(8,128)(2,1)S(1)}, bf16[64,2048]{1,0:T(8,128)(2,1)S(1)}, bf16[4,64,2048]{2,1,0:T(8,128)(2,1)S(1)}) custom-call(f32[4,64,2048]{2,1,0:T(8,128)S(1)} %bitcast.256, f32[64,2048]{1,0:T(8,128)S(1)} %get-tuple-element.141.middle, f32[1,2048]{1,0:T(1,128)S(1)} %bitcast.292, bf16[64,2048]{1,0:T(8,128)(2,1)S(1)} %get-tuple-element.318.own), custom_call_target="tpu_custom_call" | custom-call | tf_op jit(solution)/shard_map/pallas_call | solution.py:464
  431.5 5.0 fusion.68.cat
  436.5 10.9 shard_map.288
  449.6 24.5 %shard_map.289 = (f32[64,2048]{1,0:T(8,128)S(1)}, bf16[4,64,2048]{2,1,0:T(8,128)(2,1)S(1)}) custom-call(f32[4,64,2048]{2,1,0:T(8,128)S(1)} %bitcast.230, bf16[64,2048]{1,0:T(8,128)(2,1)S(1)} %get-tuple-element.144.h, f32[1,2048]{1,0:T(1,128)S(1)} %bitcast.300), custom_call_target="tpu_custom_call" | custom-call | tf_op jit(solution)/shard_map/pallas_call | solution.py:464
  476.0 3.3 broadcast_select_fusion.19
  479.3 3.2 fusion.71
  484.1 28.8 %shard_map.290 = (bf16[64,2048]{1,0:T(8,128)(2,1)S(1)}, bf16[64,2048]{1,0:T(8,128)(2,1)S(1)}, bf16[4,64,2048]{2,1,0:T(8,128)(2,1)S(1)}) custom-call(f32[4,64,2048]{2,1,0:T(8,128)S(1)} %bitcast.257, f32[64,2048]{1,0:T(8,128)S(1)} %get-tuple-element.146.middle.refs_2_, f32[1,2048]{1,0:T(1,128)S(1)} %bitcast.293, bf16[64,2048]{1,0:T(8,128)(2,1)S(1)} %get-tuple-element.318.own), custom_call_target="tpu_custom_call" | custom-call | tf_op jit(solution)/shard_map/pallas_call | solution.py:464
  514.6 5.0 fusion.72.cat
  519.6 10.7 shard_map.291
  532.6 24.7 %shard_map.292 = (f32[64,2048]{1,0:T(8,128)S(1)}, bf16[4,64,2048]{2,1,0:T(8,128)(2,1)S(1)}) custom-call(f32[4,64,2048]{2,1,0:T(8,128)S(1)} %bitcast.228, bf16[64,2048]{1,0:T(8,128)(2,1)S(1)} %get-tuple-element.149.h, f32[1,2048]{1,0:T(1,128)S(1)} %bitcast.301), custom_call_target="tpu_custom_call" | custom-call | tf_op jit(solution)/shard_map/pallas_call | solution.py:464
  559.1 3.2 broadcast_select_fusion.18
  569.0 20.0 %shard_map.293 = (bf16[64,2048]{1,0:T(8,128)(2,1)S(1)}, bf16[4,64,2048]{2,1,0:T(8,128)(2,1)S(1)}) custom-call(f32[4,64,2048]{2,1,0:T(8,128)S(1)} %bitcast.252, f32[64,2048]{1,0:T(8,128)S(1)} %get-tuple-element.151.middle, bf16[64,2048]{1,0:T(8,128)(2,1)S(1)} %get-tuple-element.317.gy), custom_call_target="tpu_custom_call" | custom-call | tf_op jit(solution)/shard_map/pallas_call | solution.py:464
  589.0 5.9 multiply_convert_fusion.6
  598.7 21.2 %shard_map.294 = (f32[64,2048]{1,0:T(8,128)S(1)}, f32[1,2048]{1,0:T(1,128)S(1)}, bf16[4,64,2048]{2,1,0:T(8,128)(2,1)S(1)}) custom-call(f32[4,64,2048]{2,1,0:T(8,128)S(1)} %bitcast.253, bf16[64,2048]{1,0:T(8,128)(2,1)S(1)} %get-tuple-element.317.gy, f32[64,2048]{1,0:T(8,128)S(1)} %get-tuple-element.151.middle, f32[1,2048]{1,0:T(1,128)S(1)} %bitcast.302), custom_call_target="tpu_custom_call" | custom-call | tf_op jit(solution)/shard_map/pallas_call | solution.py:464
  622.0 14.4 %shard_map.295 = (bf16[256,1664]{1,0:T(8,128)(2,1)S(1)}, f32[1,512]{1,0:T(1,128)S(1)}, f32[128,256]{1,0:T(8,128)S(1)}, f32[1,256]{1,0:T(1,128)S(1)}) custom-call(f32[256,512]{1,0:T(8,128)S(1)} %fusion.77.dgated_ref, f32[256,512]{1,0:T(8,128)S(1)} %copy-done.10, f32[256,1664]{1,0:T(8,128)S(1)} %fusion.72.cat, f32[128,256]{1,0:T(8,128)S(1)} %pad.18.refs_1_.up.refs_3_, ...), custom_call_target="tpu_custom_call" | custom-call | tf_op jit(solution)/shard_map/pallas_call | solution.py:464
  636.5 5.4 fusion.78
  642.0 24.3 %shard_map.296 = (bf16[64,2048]{1,0:T(8,128)(2,1)S(1)}, f32[1,2048]{1,0:T(1,128)S(1)}, bf16[64,2048]{1,0:T(8,128)(2,1)S(1)}, bf16[4,64,2048]{2,1,0:T(8,128)(2,1)S(1)}) custom-call(f32[4,64,2048]{2,1,0:T(8,128)S(1)} %bitcast.250, f32[64,2048]{1,0:T(8,128)S(1)} %copy-done.98, bf16[64,2048]{1,0:T(8,128)(2,1)S(1)} %copy-done.43, f32[1,2048]{1,0:T(1,128)S(1)} %bitcast.294, ...), custom_call_target="tpu_custom_call" | custom-call | tf_op jit(solution)/shard_map/pallas_call | solution.py:464
  666.4 7.5 broadcast_select_fusion.21
  678.7 23.5 %shard_map.297 = (f32[64,2048]{1,0:T(8,128)S(1)}, f32[1,2048]{1,0:T(1,128)S(1)}, bf16[4,64,2048]{2,1,0:T(8,128)(2,1)S(1)}, bf16[3,64,2048]{2,1,0:T(8,128)(2,1)S(1)}) custom-call(f32[4,64,2048]{2,1,0:T(8,128)S(1)} %bitcast.247, bf16[64,2048]{1,0:T(8,128)(2,1)S(1)} %get-tuple-element.160.refs_1_, f32[64,2048]{1,0:T(8,128)S(1)} %copy-done.21, ...), custom_call_target="tpu_custom_call" | custom-call | tf_op jit(solution)/shard_map/pallas_call | solution.py:464
  705.1 15.4 %shard_map.298 = (bf16[256,1664]{1,0:T(8,128)(2,1)S(1)}, f32[1,512]{1,0:T(1,128)S(1)}, f32[128,256]{1,0:T(8,128)S(1)}, f32[1,256]{1,0:T(1,128)S(1)}) custom-call(f32[256,512]{1,0:T(8,128)S(1)} %fusion.80.dgated_ref, f32[256,512]{1,0:T(8,128)S(1)} %get-tuple-element.143.inner_ref, f32[256,1664]{1,0:T(8,128)S(1)} %fusion.68.cat, ...), custom_call_target="tpu_custom_call" | custom-call | tf_op jit(solution)/shard_map/pallas_call | solution.py:464
  720.6 5.4 fusion.81
  726.1 29.4 %shard_map.299 = (bf16[64,2048]{1,0:T(8,128)(2,1)S(1)}, f32[1,2048]{1,0:T(1,128)S(1)}, bf16[64,2048]{1,0:T(8,128)(2,1)S(1)}, bf16[4,64,2048]{2,1,0:T(8,128)(2,1)S(1)}) custom-call(f32[4,64,2048]{2,1,0:T(8,128)S(1)} %bitcast.248, f32[64,2048]{1,0:T(8,128)S(1)} %copy-done.96, bf16[64,2048]{1,0:T(8,128)(2,1)S(1)} %copy-done.41, f32[1,2048]{1,0:T(1,128)S(1)} %bitcast.295, ...), custom_call_target="tpu_custom_call" | custom-call | tf_op jit(solution)/shard_map/pallas_call | solution.py:464
  755.5 7.2 broadcast_select_fusion.22
  766.5 21.5 %shard_map.300 = (f32[64,2048]{1,0:T(8,128)S(1)}, f32[1,2048]{1,0:T(1,128)S(1)}, bf16[4,64,2048]{2,1,0:T(8,128)(2,1)S(1)}) custom-call(f32[4,64,2048]{2,1,0:T(8,128)S(1)} %bitcast.254, bf16[64,2048]{1,0:T(8,128)(2,1)S(1)} %get-tuple-element.172.gy, f32[64,2048]{1,0:T(8,128)S(1)} %copy-done.23, f32[1,2048]{1,0:T(1,128)S(1)} %bitcast.304), custom_call_target="tpu_custom_call" | custom-call | tf_op jit(solution)/shard_map/pallas_call | solution.py:464
  789.8 12.2 shard_map.301
  804.9 35.0 %shard_map.302 = (bf16[64,2048]{1,0:T(8,128)(2,1)S(1)}, f32[1,2048]{1,0:T(1,128)S(1)}, bf16[64,2048]{1,0:T(8,128)(2,1)S(1)}, bf16[4,64,2048]{2,1,0:T(8,128)(2,1)S(1)}) custom-call(f32[4,64,2048]{2,1,0:T(8,128)S(1)} %bitcast.249, f32[64,2048]{1,0:T(8,128)S(1)} %get-tuple-element.178.d_middle, bf16[64,2048]{1,0:T(8,128)(2,1)S(1)} %get-tuple-element.139.h, ...), custom_call_target="tpu_custom_call" | custom-call | tf_op jit(solution)/shard_map/pallas_call | solution.py:464
  840.0 3.6 broadcast_select_fusion.23
  845.7 4.0 convolution_convert_fusion.3
  849.6 2.4 broadcast_select_fusion.5
  856.7 4.5 add_convert_fusion.3
  861.3 4.0 convolution_convert_fusion.2
  865.8 4.0 convolution_convert_fusion.1
  878.5 25.6 %collective-permute-done.5 = bf16[512,1408]{1,0:T(8,128)(2,1)S(1)} collective-permute-done((bf16[512,1408]{1,0:T(8,128)(2,1)S(1)}, bf16[512,1408]{1,0:T(8,128)(2,1)S(1)}, u32[]{:S(2)}, u32[]{:S(2)}) %collective-permute-start.5) | collective-permute-done | bytes 1441824 | tf_op jit(solution)/shard_map/ppermute | solution.py:1562
  904.5 4.6 add_convert_fusion.2.refs_4_
  909.2 2.7 add_convert_fusion.1.refs_8_
  911.9 48.9 %shard_map.303 = (f32[64,2048]{1,0:T(8,128)S(1)}, f32[1,2048]{1,0:T(1,128)S(1)}, bf16[4,64,2048]{2,1,0:T(8,128)(2,1)S(1)}, bf16[1,512,1408]{2,1,0:T(8,128)(2,1)S(1)}, bf16[512,1408]{1,0:T(8,128)(2,1)S(1)}) custom-call(f32[4,64,2048]{2,1,0:T(8,128)S(1)} %bitcast.258, bf16[64,2048]{1,0:T(8,128)(2,1)S(1)} %copy-done.110, f32[64,2048]{1,0:T(8,128)S(1)} %copy-done.25, ...), custom_call_target="tpu_custom_call" | custom-call | tf_op jit(solution)/shard_map/pallas_call | solution.py:464
  965.0 64.8 %shard_map.304 = (bf16[256,1664]{1,0:T(8,128)(2,1)S(1)}, f32[1,512]{1,0:T(1,128)S(1)}, f32[128,256]{1,0:T(8,128)S(1)}, f32[1,256]{1,0:T(1,128)S(1)}, bf16[1,512,...) custom-call(f32[256,512]{1,0:T(8,128)S(1)} %fusion.86.refs_0_, f32[256,512]{1,0:T(8,128)S(1)} %copy-done.12, ...), custom_call_target="tpu_custom_call" | custom-call | tf_op jit(solution)/shard_map/pallas_call | solution.py:464
  1031.1 7.3 fusion.87
  1038.4 4.5 convolution_convert_fusion
  1049.2 3.3 bitcast_convert_fusion.2
  1055.0 35.0 %shard_map.305 = (bf16[64,2048]{1,0:T(8,128)(2,1)S(1)}, f32[1,2048]{1,0:T(1,128)S(1)}, bf16[1,512,512]{2,1,0:T(8,128)(2,1)S(1)}, bf16[512,1408]{1,0:T(8,128)(2,1)S(1)}) custom-call(f32[4,64,2048]{2,1,0:T(8,128)S(1)} %bitcast.251, f32[64,2048]{1,0:T(8,128)S(1)} %copy-done.100, bf16[64,2048]{1,0:T(8,128)(2,1)S(1)} %copy-done.16, f32[1,2048]{1,0:T(1,128)S(1)} %bitcast.297, ...), custom_call_target="tpu_custom_call" | custom-call | tf_op jit(solution)/shard_map/pallas_call | solution.py:464
  1092.8 4.9 bitcast_convert_fusion
  1098.0 7.0 add_convert_fusion.refs_0_
  1105.0 99.7 %shard_map.306 = (bf16[512,1664]{1,0:T(8,128)(2,1)S(1)}, bf16[512,512]{1,0:T(8,128)(2,1)S(1)}, bf16[3,4,64,2048]{3,2,1,0:T(8,128)(2,1)}, bf16[3,4,64,2048]{3,2,1...) custom-call(bf16[1024,1664]{1,0:T(8,128)(2,1)} %add_convert_fusion.refs_0_, ...), custom_call_target="tpu_custom_call" | custom-call | tf_op jit(solution)/shard_map/pallas_call | solution.py:1519
  1208.9 5.4 convert.10
  1217.4 4.0 copy.57
  (635 shorter events, 102.7 us)
Async XLA Ops:
  0.6 10.1 copy-start.180
  0.7 10.2 copy-start.178
  0.7 10.1 copy-start.181
  2.0 8.9 copy-start.179
  2.0 9.0 copy-start.190
  2.0 9.2 copy-start.191
  2.0 9.2 copy-start.192
  2.0 9.2 copy-start.193
  2.0 9.1 copy-start.194
  2.0 9.3 copy-start.189
  2.0 117.1 %collective-permute-start = (bf16[3,64,2048]{2,1,0:T(8,128)(2,1)S(1)}, bf16[3,64,2048]{2,1,0:T(8,128)(2,1)}, u32[]{:S(2)}, u32[]{:S(2)}) collective-permute-start(bf16[3,64,2048]{2,1,0:T(8,128)(2,1)S(1)} %constant_dynamic-slice_fusion.3), channel_id=1, source_target_pairs={{8,16},{16,8},{9,17},{17,9},{10,18},{18,10},{11,19},{19,11},{12,20... | collective-permute-start | bytes 2359304 | tf_op jit(solution)/shard_map/ppermute | solution.py:1558
  6.2 560.3 %collective-permute-start.1 = (bf16[3,64,2048]{2,1,0:T(8,128)(2,1)}, bf16[3,64,2048]{2,1,0:T(8,128)(2,1)}, u32[]{:S(2)}, u32[]{:S(2)}) collective-permute-start(bf16[3,64,2048]{2,1,0:T(8,128)(2,1)} %constant_dynamic-slice_fusion.2), channel_id=1, source_target_pairs={{8,16},{16,8},{9,17},{17,9},{10,18},{18,10},{11,19},{19,11},{12,20... | collective-permute-start | bytes 2359304 | tf_op jit(solution)/shard_map/ppermute | solution.py:1558
  118.4 46.8 %copy-start.129 = (f32[1,256]{1,0:T(1,128)}, f32[1,256]{1,0:T(1,128)S(1)}, u32[]{:S(2)}) copy-start(f32[1,256]{1,0:T(1,128)S(1)} %reshape.240.refs_2_.bias) | copy-start | bytes 3076
  118.5 671.2 %copy-start.1 = (f32[128,256]{1,0:T(8,128)}, f32[128,256]{1,0:T(8,128)S(1)}, u32[]{:S(2)}) copy-start(f32[128,256]{1,0:T(8,128)S(1)} %pad.18.refs_1_.up.refs_3_) | copy-start | bytes 393220
  119.1 88.6 %copy-start.187 = (f32[512]{0:T(512)}, f32[512]{0:T(512)S(1)}, u32[]{:S(2)}) copy-start(f32[512]{0:T(512)S(1)} %get-tuple-element.322) | copy-start | bytes 6148
  121.6 87.6 %copy-start.15 = (bf16[64,2048]{1,0:T(8,128)(2,1)}, bf16[64,2048]{1,0:T(8,128)(2,1)S(1)}, u32[]{:S(2)}) copy-start(bf16[64,2048]{1,0:T(8,128)(2,1)S(1)} %get-tuple-element.320.refs_0_.refs_1_.refs_2_) | copy-start | bytes 786436
  165.2 42.8 %copy-start.3 = (f32[256,1664]{1,0:T(8,128)}, f32[256,1664]{1,0:T(8,128)S(1)}, u32[]{:S(2)}) copy-start(f32[256,1664]{1,0:T(8,128)S(1)} %fusion.60.refs_0_.refs_2_) | copy-start | bytes 5111812
  250.1 65.8 %copy-start.24 = (f32[64,2048]{1,0:T(8,128)}, f32[64,2048]{1,0:T(8,128)S(1)}, u32[]{:S(2)}) copy-start(f32[64,2048]{1,0:T(8,128)S(1)} %get-tuple-element.136.middle.refs_2_) | copy-start | bytes 1572868
  316.0 78.2 %slice-start = ((s8[5767168]{0:T(1024)(128)(4,1)}), s8[4194304]{0:T(1024)(128)(4,1)S(1)}, s32[]{:S(2)}) async-start(s8[5767168]{0:T(1024)(128)(4,1)} %bitcast.231), calls=%async_computation | async-start | bytes 8388608
  351.5 42.7 %slice-start.1 = ((s8[5767168]{0:T(1024)(128)(4,1)}), s8[1572864]{0:T(1024)(128)(4,1)S(1)}, s32[]{:S(2)}) async-start(s8[5767168]{0:T(1024)(128)(4,1)} %bitcast.231), calls=%async_computation.1 | async-start | bytes 3145728
  356.7 10.9 copy-start.171
  356.7 10.9 copy-start.188
  430.5 19.0 %copy-start.40 = (bf16[64,2048]{1,0:T(8,128)(2,1)}, bf16[64,2048]{1,0:T(8,128)(2,1)S(1)}, u32[]{:S(2)}) copy-start(bf16[64,2048]{1,0:T(8,128)(2,1)S(1)} %get-tuple-element.144.h) | copy-start | bytes 786436
  474.1 8.3 copy-start.20
  513.6 19.0 %copy-start.42 = (bf16[64,2048]{1,0:T(8,128)(2,1)}, bf16[64,2048]{1,0:T(8,128)(2,1)S(1)}, u32[]{:S(2)}) copy-start(bf16[64,2048]{1,0:T(8,128)(2,1)S(1)} %get-tuple-element.149.h) | copy-start | bytes 786436
  619.9 16.6 %copy-start.131 = (f32[1,2048]{1,0:T(1,128)}, f32[1,2048]{1,0:T(1,128)S(1)}, u32[]{:S(2)}) copy-start(f32[1,2048]{1,0:T(1,128)S(1)} %get-tuple-element.218) | copy-start | bytes 24580
  642.0 24.4 %copy-start.199 = (bf16[256,1408]{1,0:T(8,128)(2,1)S(1)}, bf16[256,1408]{1,0:T(8,128)(2,1)}, u32[]{:S(2)}) copy-start(bf16[256,1408]{1,0:T(8,128)(2,1)} %copy-done.198) | copy-start | bytes 2162692
  703.0 17.5 %copy-start.67 = (bf16[4,64,2048]{2,1,0:T(8,128)(2,1)}, bf16[4,64,2048]{2,1,0:T(8,128)(2,1)S(1)}, u32[]{:S(2)}) copy-start(bf16[4,64,2048]{2,1,0:T(8,128)(2,1)S(1)} %get-tuple-element.165) | copy-start | bytes 3145732
  703.1 17.5 %copy-start.135 = (f32[1,2048]{1,0:T(1,128)}, f32[1,2048]{1,0:T(1,128)S(1)}, u32[]{:S(2)}) copy-start(f32[1,2048]{1,0:T(1,128)S(1)} %get-tuple-element.219) | copy-start | bytes 24580
  726.0 29.5 %copy-start.197 = (bf16[256,1408]{1,0:T(8,128)(2,1)S(1)}, bf16[256,1408]{1,0:T(8,128)(2,1)}, u32[]{:S(2)}) copy-start(bf16[256,1408]{1,0:T(8,128)(2,1)} %copy-done.196) | copy-start | bytes 2162692
  726.0 29.5 %copy-start.202 = (bf16[256,1408]{1,0:T(8,128)(2,1)S(1)}, bf16[256,1408]{1,0:T(8,128)(2,1)}, u32[]{:S(2)}) copy-start(bf16[256,1408]{1,0:T(8,128)(2,1)} %copy-done.201) | copy-start | bytes 2162692
  762.8 39.9 %slice-start.16 = ((s8[6815744]{0:T(1024)(128)(4,1)}), s8[2621440]{0:T(1024)(128)(4,1)S(1)}, s32[]{:S(2)}) async-start(s8[6815744]{0:T(1024)(128)(4,1)} %bitcast.315), calls=%async_computation.16 | async-start | bytes 5242880
  764.7 38.1 %slice-start.17 = ((s8[6815744]{0:T(1024)(128)(4,1)}), s8[4194304]{0:T(1024)(128)(4,1)S(1)}, s32[]{:S(2)}) async-start(s8[6815744]{0:T(1024)(128)(4,1)} %bitcast.315), calls=%async_computation.17 | async-start | bytes 8388608
  788.0 14.0 %copy-start.139 = (f32[1,2048]{1,0:T(1,128)}, f32[1,2048]{1,0:T(1,128)S(1)}, u32[]{:S(2)}) copy-start(f32[1,2048]{1,0:T(1,128)S(1)} %get-tuple-element.220) | copy-start | bytes 24580
  802.7 37.3 %slice-start.14 = ((s8[5767168]{0:T(1024)(128)(4,1)}), s8[4194304]{0:T(1024)(128)(4,1)S(1)}, s32[]{:S(2)}) async-start(s8[5767168]{0:T(1024)(128)(4,1)} %bitcast.245), calls=%async_computation.14 | async-start | bytes 8388608
  802.7 37.2 %slice-start.15 = ((s8[5767168]{0:T(1024)(128)(4,1)}), s8[1572864]{0:T(1024)(128)(4,1)S(1)}, s32[]{:S(2)}) async-start(s8[5767168]{0:T(1024)(128)(4,1)} %bitcast.245), calls=%async_computation.15 | async-start | bytes 3145728
  802.7 37.2 %copy-start.233 = (f32[256,1408]{1,0:T(8,128)S(1)}, f32[256,1408]{1,0:T(8,128)}, u32[]{:S(2)}) copy-start(f32[256,1408]{1,0:T(8,128)} %get-tuple-element.328) | copy-start | bytes 4325380
  804.9 35.1 %copy-start.204 = (bf16[256,1408]{1,0:T(8,128)(2,1)S(1)}, bf16[256,1408]{1,0:T(8,128)(2,1)}, u32[]{:S(2)}) copy-start(bf16[256,1408]{1,0:T(8,128)(2,1)} %copy-done.203) | copy-start | bytes 2162692
  804.9 35.1 %copy-start.229 = (f32[256,1408]{1,0:T(8,128)S(1)}, f32[256,1408]{1,0:T(8,128)}, u32[]{:S(2)}) copy-start(f32[256,1408]{1,0:T(8,128)} %copy-done.228) | copy-start | bytes 4325380
  849.6 5.6 collective-permute-start.2
  865.3 39.2 %collective-permute-start.3 = (bf16[1024,1408]{1,0:T(8,128)(2,1)}, bf16[1024,1408]{1,0:T(8,128)(2,1)}, u32[]{:S(2)}, u32[]{:S(2)}) collective-permute-start(bf16[1024,1408]{1,0:T(8,128)(2,1)} %convolution_convert_fusion.2), channel_id=1, source_target_pairs={{0,16},{16,0},{1,17},{17,1},{2,18},{18,2},{3,19},{19,3},{4,20},{20... | collective-permute-start | bytes 8650760 | tf_op jit(solution)/shard_map/ppermute | solution.py:1562
  865.8 8.4 slice-start.2
  869.8 39.3 %collective-permute-start.4 = (bf16[1024,1408]{1,0:T(8,128)(2,1)}, bf16[1024,1408]{1,0:T(8,128)(2,1)S(1)}, u32[]{:S(2)}, u32[]{:S(2)}) collective-permute-start(bf16[1024,1408]{1,0:T(8,128)(2,1)} %convolution_convert_fusion.1), channel_id=1, source_target_pairs={{0,16},{16,0},{1,17},{17,1},{2,18},{18,2},{3,19},{19,3},{4,20},{20... | collective-permute-start | bytes 8650760 | tf_op jit(solution)/shard_map/ppermute | solution.py:1562
  870.0 34.0 %collective-permute-start.5 = (bf16[512,1408]{1,0:T(8,128)(2,1)S(1)}, bf16[512,1408]{1,0:T(8,128)(2,1)S(1)}, u32[]{:S(2)}, u32[]{:S(2)}) collective-permute-start(bf16[512,1408]{1,0:T(8,128)(2,1)S(1)} %constant_dynamic-slice_fusion.1), channel_id=1, source_target_pairs={{0,4},{4,0},{1,5},{5,1},{2,6},{6,2},{3,7},{7,3},{8,12},{12,8},{9,1... | collective-permute-start | bytes 4325384 | tf_op jit(solution)/shard_map/ppermute | solution.py:1562
  878.4 26.0 %copy-start.217 = (bf16[256,1408]{1,0:T(8,128)(2,1)S(1)}, bf16[256,1408]{1,0:T(8,128)(2,1)}, u32[]{:S(2)}) copy-start(bf16[256,1408]{1,0:T(8,128)(2,1)} %get-tuple-element.280) | copy-start | bytes 2162692
  878.4 26.0 %copy-start.219 = (bf16[256,1408]{1,0:T(8,128)(2,1)S(1)}, bf16[256,1408]{1,0:T(8,128)(2,1)}, u32[]{:S(2)}) copy-start(bf16[256,1408]{1,0:T(8,128)(2,1)} %get-tuple-element.278) | copy-start | bytes 2162692
  878.5 26.0 %copy-start.223 = (bf16[256,1408]{1,0:T(8,128)(2,1)S(1)}, bf16[256,1408]{1,0:T(8,128)(2,1)}, u32[]{:S(2)}) copy-start(bf16[256,1408]{1,0:T(8,128)(2,1)} %get-tuple-element.276) | copy-start | bytes 2162692
  911.9 49.0 %copy-start.64 = (bf16[4,64,2048]{2,1,0:T(8,128)(2,1)S(1)}, bf16[4,64,2048]{2,1,0:T(8,128)(2,1)}, u32[]{:S(2)}) copy-start(bf16[4,64,2048]{2,1,0:T(8,128)(2,1)} %copy-done.63) | copy-start | bytes 3145732
  911.9 49.0 %copy-start.68 = (bf16[4,64,2048]{2,1,0:T(8,128)(2,1)S(1)}, bf16[4,64,2048]{2,1,0:T(8,128)(2,1)}, u32[]{:S(2)}) copy-start(bf16[4,64,2048]{2,1,0:T(8,128)(2,1)} %copy-done.67) | copy-start | bytes 3145732
  911.9 49.0 %copy-start.70 = (bf16[4,64,2048]{2,1,0:T(8,128)(2,1)S(1)}, bf16[4,64,2048]{2,1,0:T(8,128)(2,1)}, u32[]{:S(2)}) copy-start(bf16[4,64,2048]{2,1,0:T(8,128)(2,1)} %copy-done.69) | copy-start | bytes 3145732
  965.0 64.9 %copy-start.85 = (bf16[256,1664]{1,0:T(8,128)(2,1)S(1)}, bf16[256,1664]{1,0:T(8,128)(2,1)}, u32[]{:S(2)}) copy-start(bf16[256,1664]{1,0:T(8,128)(2,1)} %copy-done.84) | copy-start | bytes 2555908
  965.0 64.9 %copy-start.87 = (bf16[256,1664]{1,0:T(8,128)(2,1)S(1)}, bf16[256,1664]{1,0:T(8,128)(2,1)}, u32[]{:S(2)}) copy-start(bf16[256,1664]{1,0:T(8,128)(2,1)} %copy-done.86) | copy-start | bytes 2555908
  965.0 64.9 %copy-start.89 = (bf16[256,1664]{1,0:T(8,128)(2,1)S(1)}, bf16[256,1664]{1,0:T(8,128)(2,1)}, u32[]{:S(2)}) copy-start(bf16[256,1664]{1,0:T(8,128)(2,1)} %copy-done.88) | copy-start | bytes 2555908
  1042.9 55.0 %collective-permute-start.6 = (bf16[1024,1664]{1,0:T(8,128)(2,1)}, bf16[1024,1664]{1,0:T(8,128)(2,1)}, u32[]{:S(2)}, u32[]{:S(2)}) collective-permute-start(bf16[1024,1664]{1,0:T(8,128)(2,1)} %convolution_convert_fusion), channel_id=1, source_target_pairs={{0,16},{16,0},{1,17},{17,1},{2,18},{18,2},{3,19},{19,3},{4,20},{20... | collective-permute-start | bytes 10223624 | tf_op jit(solution)/shard_map/ppermute | solution.py:1562
  1046.1 6.4 collective-permute-start.7
  1054.9 35.2 %copy-start.13 = (bf16[1024,512]{1,0:T(8,128)(2,1)}, bf16[1024,512]{1,0:T(8,128)(2,1)S(1)}, u32[]{:S(2)}) copy-start(bf16[1024,512]{1,0:T(8,128)(2,1)S(1)} %add_convert_fusion.5.refs_4_.refs_1_) | copy-start | bytes 3145732
  1055.0 37.1 %copy-start.132 = (f32[1,2048]{1,0:T(1,128)S(1)}, f32[1,2048]{1,0:T(1,128)}, u32[]{:S(2)}) copy-start(f32[1,2048]{1,0:T(1,128)} %copy-done.131) | copy-start | bytes 24580
  1055.0 37.1 %copy-start.134 = (f32[1,2048]{1,0:T(1,128)S(1)}, f32[1,2048]{1,0:T(1,128)}, u32[]{:S(2)}) copy-start(f32[1,2048]{1,0:T(1,128)} %copy-done.133) | copy-start | bytes 24580
  1055.0 37.1 %copy-start.136 = (f32[1,2048]{1,0:T(1,128)S(1)}, f32[1,2048]{1,0:T(1,128)}, u32[]{:S(2)}) copy-start(f32[1,2048]{1,0:T(1,128)} %copy-done.135) | copy-start | bytes 24580
  1055.0 37.1 %copy-start.138 = (f32[1,2048]{1,0:T(1,128)S(1)}, f32[1,2048]{1,0:T(1,128)}, u32[]{:S(2)}) copy-start(f32[1,2048]{1,0:T(1,128)} %copy-done.137) | copy-start | bytes 24580
  1055.0 37.1 %copy-start.140 = (f32[1,2048]{1,0:T(1,128)S(1)}, f32[1,2048]{1,0:T(1,128)}, u32[]{:S(2)}) copy-start(f32[1,2048]{1,0:T(1,128)} %copy-done.139) | copy-start | bytes 24580
  1055.0 37.1 %copy-start.142 = (f32[1,2048]{1,0:T(1,128)S(1)}, f32[1,2048]{1,0:T(1,128)}, u32[]{:S(2)}) copy-start(f32[1,2048]{1,0:T(1,128)} %copy-done.141) | copy-start | bytes 24580
  1055.0 37.1 %copy-start.144 = (f32[1,2048]{1,0:T(1,128)S(1)}, f32[1,2048]{1,0:T(1,128)}, u32[]{:S(2)}) copy-start(f32[1,2048]{1,0:T(1,128)} %copy-done.143) | copy-start | bytes 24580
  1092.4 5.5 collective-permute-start.8
  (197 other events, 614.9 us)

commit v4 on v3

--- a/solution.py
+++ b/solution.py
@@ -1644,9 +1644,8 @@
     )
     w["cat"], w["output"] = cat, output
     homes = [feed_gate[0], feed_up[0], feed_down[0]]
-    own_cot = own_rows(cotangent)
-
     calls = Rows(rows, width, peers)
+    held_cot = lax.dynamic_slice_in_dim(cotangent, me * rows, rows, 1)
     kept, ys = [], []
     h = jnp.where(stage == 0, own_in[0], jnp.zeros_like(own_in[0]))
     normed, gate = calls.first(h, w["mixer_gain"], gather_start(half, homes[0]))
@@ -1660,7 +1659,10 @@
         middle, feed_in, *lower = calls.forward_mid(
             dot_right(gated, w["output"]), h, w["feed_gain"],
             **(dict(ident=15, extra=gather_start(half, homes[2])) if step == 0 else {}),
-        )
+            **(dict(ident=19, extra=home_start(half, held_cot)) if step == 1 else {}),
+        )
+        if step == 1:
+            own_cot = jnp.where(lax.axis_index("section") == stage, held_cot, lower[0])
         if step == 0:
             w["gate"], w["upper"], w["lower"] = gather_end(half, 12, gate, *upper, *lower)
         gate_v = dot_plain(feed_in, w["gate"])

time: 1230 us -> 1220 us (level)
    unnamed x517 -> x473, local copies, waits for them, and re-layouts: 44.3 us -> 41.1 us
  transfers between devices with their start and end apart: 9 -> 8, of which waited for: 2 -> 2; matrix products, arithmetic and copies ran while one was open for 8% -> 3% of each run, Pallas kernels for 41% -> 10%
where the time goes in v4:
time: 1220 us; the launch traced here: 1210 us
  Pallas kernels  924 us (76%)
  matrix products  163 us (13%)
  local copies, waits for them, and re-layouts  51.5 us (4%)
  other arithmetic  36.6 us (3%)
  waiting for transfers between devices  27.7 us (2%)
    pallas_call x25, Pallas kernels, kernel_call(): pl.pallas_call(body, out_shape=outs, in_specs=in_specs, out_specs=out_spe...  677 us
    pallas_call x1, Pallas kernels, finish(): pl.pallas_call(partial(finish_kernel, half, count, come, places, lanes),...  99.6 us
    pallas_call x1, Pallas kernels, gather_weights(): pl.pallas_call(partial(gather_kernel, half, count), out_shape=[shape((2 *...  91.4 us
    dot_general x20, matrix products, dot_plain(): return jnp.dot(left, right, preferred_element_type=f32)  73.1 us
    pallas_call x1, Pallas kernels, gather_end(): pl.pallas_call(partial(gather_end_kernel, half, count, rows), out_shape=[...  56 us
    dot_general x20, matrix products, dot_right(): lax.dot_general(left, right, (((1,), (1,)), ((), ())), preferred_element_...  49.8 us
    unnamed x473, local copies, waits for them, and re-layouts  41.1 us
    dot_general x10, matrix products, dot_left(): lax.dot_general(left, right, (((0,), (0,)), ((), ())), preferred_element_...  40.5 us
  transfers between devices with their start and end apart: 8, of which 2 were waited for; matrix products, arithmetic and copies ran while one was open for 3% of the time, Pallas kernels for 10%

profile of v4, /device:TPU:24, one launch (start us, length us, event | category | flops | bytes accessed | tf_op | source)
XLA Modules:
  0.0 1211.1 jit_solution(12922679547554592909)
XLA Ops:
  7.9 91.4 %shard_map.279 = (bf16[64,256]{1,0:T(8,128)(2,1)S(1)}, bf16[2048,1664]{1,0:T(8,128)(2,1)S(1)}, bf16[2048,512]{1,0:T(8,128)(2,1)S(1)}) custom-call(bf16[16,256]{1,0:T(8,128)(2,1)S(1)} %squeeze_reshape.3.refs_0_, bf16[512,1664]{1,0:T(8,128)(2,1)S(1)} %pad.17.refs_1_, bf16[512,512]{1,0:T(8,128)(2,1)S(1)} %bitcast.312), custom_call_target="tpu_custom_call" | custom-call | tf_op jit(solution)/shard_map/pallas_call | solution.py:1037
  99.4 2.9 copy-done.133
  107.0 35.8 %shard_map.280 = (bf16[4,64,2048]{2,1,0:T(8,128)(2,1)S(1)}, bf16[2048,1408]{1,0:T(8,128)(2,1)S(1)}) custom-call(bf16[64,2048]{1,0:T(8,128)(2,1)S(1)} %get-tuple-element.322.refs_0_.refs_1_.refs_2_, f32[1,2048]{1,0:T(1,128)S(1)} %bitcast.296, bf16[512,1408]{1,0:T(8,128)(2,1)S(1)} %bitcast.266), custom_call_target="tpu_custom_call" | custom-call | tf_op jit(solution)/shard_map/pallas_call | solution.py:464
  142.8 7.5 fusion.60.refs_0_.refs_2_
  150.4 39.9 %shard_map.281 = (f32[256,512]{1,0:T(8,128)S(1)}, f32[256,256]{1,0:T(8,128)S(1)}, f32[256,256]{1,0:T(8,128)S(1)}, bf16[5,512,256]{2,1,0:T(8,128)(2,1)S(1)}, bf16[2048,1408]{1,0:T(8,128)(2,1)S(1)}) custom-call(f32[256,1664]{1,0:T(8,128)S(1)} %fusion.60.refs_0_.refs_2_, f32[128,256]{1,0:T(8,128)S(1)} %pad.18.refs_1_.up.refs_3_, f32[1,256]{1,0:T(1,128)S(1)} %copy-done.104, ...), custom_call_target="tpu_custom_call" | custom-call | tf_op jit(solution)/shard_map/pallas_call | solution.py:464
  194.3 36.7 %shard_map.282 = (f32[64,2048]{1,0:T(8,128)S(1)}, bf16[4,64,2048]{2,1,0:T(8,128)(2,1)S(1)}, bf16[2048,1408]{1,0:T(8,128)(2,1)S(1)}) custom-call(f32[4,64,2048]{2,1,0:T(8,128)S(1)} %bitcast.228, bf16[64,2048]{1,0:T(8,128)(2,1)S(1)} %get-tuple-element.322.refs_0_.refs_1_.refs_2_, f32[1,2048]{1,0:T(1,128)S(1)} %bitcast.304, bf16[512,1408]{1,0:T(8,128)(2,1)S(1)} %bitcast.267), custom_call_target="tpu_custom_call" | custom-call | tf_op jit(solution)/shard_map/pallas_call | solution.py:464
  231.1 2.5 copy-done.5
  235.4 56.0 %shard_map.283 = (bf16[2048,1408]{1,0:T(8,128)(2,1)}, bf16[2048,1408]{1,0:T(8,128)(2,1)}, bf16[2048,1408]{1,0:T(8,128)(2,1)}) custom-call(bf16[2048,1408]{1,0:T(8,128)(2,1)} %copy-done.2, bf16[2048,1408]{1,0:T(8,128)(2,1)} %copy-done.3, bf16[2048,1408]{1,0:T(8,128)(2,1)} %copy-done.5), custom_call_target="tpu_custom_call", output_to_operand_aliasing={{0}: (0, {}), {1}: (1, {}), {2}: (2, {})} | custom-call | tf_op jit(solution)/shard_map/pallas_call | solution.py:1195
  291.4 4.9 fusion.62
  296.4 3.0 multiply_convert_fusion.11
  301.3 34.5 %shard_map.284 = (bf16[64,2048]{1,0:T(8,128)(2,1)S(1)}, bf16[64,2048]{1,0:T(8,128)(2,1)S(1)}, bf16[4,64,2048]{2,1,0:T(8,128)(2,1)S(1)}) custom-call(f32[4,64,2048]{2,1,0:T(8,128)S(1)} %bitcast.261, f32[64,2048]{1,0:T(8,128)S(1)} %copy-done.13, f32[1,2048]{1,0:T(1,128)S(1)} %bitcast.297, bf16[64,2048]{1,0:T(8,128)(2,1)S(1)} %get-tuple-element.321.own), custom_call_target="tpu_custom_call" | custom-call | tf_op jit(solution)/shard_map/pallas_call | solution.py:464
  338.0 10.7 shard_map.285
  350.8 24.7 %shard_map.286 = (f32[64,2048]{1,0:T(8,128)S(1)}, bf16[4,64,2048]{2,1,0:T(8,128)(2,1)S(1)}, bf16[3,64,2048]{2,1,0:T(8,128)(2,1)S(1)}) custom-call(f32[4,64,2048]{2,1,0:T(8,128)S(1)} %bitcast.227, bf16[64,2048]{1,0:T(8,128)(2,1)S(1)} %get-tuple-element.140.refs_1_.h, f32[1,2048]{1,0:T(1,128)S(1)} %bitcast.305, ...), custom_call_target="tpu_custom_call" | custom-call | tf_op jit(solution)/shard_map/pallas_call | solution.py:464
  377.4 6.4 broadcast_select_fusion.20
  385.7 28.7 %shard_map.287 = (bf16[64,2048]{1,0:T(8,128)(2,1)S(1)}, bf16[64,2048]{1,0:T(8,128)(2,1)S(1)}, bf16[4,64,2048]{2,1,0:T(8,128)(2,1)S(1)}) custom-call(f32[4,64,2048]{2,1,0:T(8,128)S(1)} %bitcast.263, f32[64,2048]{1,0:T(8,128)S(1)} %get-tuple-element.142.middle, f32[1,2048]{1,0:T(1,128)S(1)} %bitcast.298, bf16[64,2048]{1,0:T(8,128)(2,1)S(1)} %get-tuple-element.320.own), custom_call_target="tpu_custom_call" | custom-call | tf_op jit(solution)/shard_map/pallas_call | solution.py:464
  416.1 5.0 fusion.68.cat
  421.1 10.9 shard_map.288
  434.2 24.5 %shard_map.289 = (f32[64,2048]{1,0:T(8,128)S(1)}, bf16[4,64,2048]{2,1,0:T(8,128)(2,1)S(1)}) custom-call(f32[4,64,2048]{2,1,0:T(8,128)S(1)} %bitcast.230, bf16[64,2048]{1,0:T(8,128)(2,1)S(1)} %get-tuple-element.145.h, f32[1,2048]{1,0:T(1,128)S(1)} %bitcast.306), custom_call_target="tpu_custom_call" | custom-call | tf_op jit(solution)/shard_map/pallas_call | solution.py:464
  461.3 3.4 broadcast_select_fusion.19
  466.6 28.9 %shard_map.290 = (bf16[64,2048]{1,0:T(8,128)(2,1)S(1)}, bf16[64,2048]{1,0:T(8,128)(2,1)S(1)}, bf16[4,64,2048]{2,1,0:T(8,128)(2,1)S(1)}) custom-call(f32[4,64,2048]{2,1,0:T(8,128)S(1)} %bitcast.262, f32[64,2048]{1,0:T(8,128)S(1)} %get-tuple-element.147.middle.refs_2_, f32[1,2048]{1,0:T(1,128)S(1)} %bitcast.299, bf16[64,2048]{1,0:T(8,128)(2,1)S(1)} %get-tuple-element.320.own), custom_call_target="tpu_custom_call" | custom-call | tf_op jit(solution)/shard_map/pallas_call | solution.py:464
  496.5 5.0 fusion.72.cat
  501.5 10.6 shard_map.291
  514.3 24.7 %shard_map.292 = (f32[64,2048]{1,0:T(8,128)S(1)}, bf16[4,64,2048]{2,1,0:T(8,128)(2,1)S(1)}) custom-call(f32[4,64,2048]{2,1,0:T(8,128)S(1)} %bitcast.229, bf16[64,2048]{1,0:T(8,128)(2,1)S(1)} %get-tuple-element.150.h, f32[1,2048]{1,0:T(1,128)S(1)} %bitcast.307), custom_call_target="tpu_custom_call" | custom-call | tf_op jit(solution)/shard_map/pallas_call | solution.py:464
  541.7 3.4 broadcast_select_fusion.18
  549.2 20.2 %shard_map.293 = (bf16[64,2048]{1,0:T(8,128)(2,1)S(1)}, bf16[4,64,2048]{2,1,0:T(8,128)(2,1)S(1)}) custom-call(f32[4,64,2048]{2,1,0:T(8,128)S(1)} %bitcast.258, f32[64,2048]{1,0:T(8,128)S(1)} %get-tuple-element.152.middle, bf16[64,2048]{1,0:T(8,128)(2,1)S(1)} %get-tuple-element.319.gy), custom_call_target="tpu_custom_call" | custom-call | tf_op jit(solution)/shard_map/pallas_call | solution.py:464
  570.1 5.9 multiply_convert_fusion.6
  579.8 21.2 %shard_map.294 = (f32[64,2048]{1,0:T(8,128)S(1)}, f32[1,2048]{1,0:T(1,128)S(1)}, bf16[4,64,2048]{2,1,0:T(8,128)(2,1)S(1)}) custom-call(f32[4,64,2048]{2,1,0:T(8,128)S(1)} %bitcast.259, bf16[64,2048]{1,0:T(8,128)(2,1)S(1)} %get-tuple-element.319.gy, f32[64,2048]{1,0:T(8,128)S(1)} %get-tuple-element.152.middle, f32[1,2048]{1,0:T(1,128)S(1)} %bitcast.308), custom_call_target="tpu_custom_call" | custom-call | tf_op jit(solution)/shard_map/pallas_call | solution.py:464
  602.8 14.5 %shard_map.295 = (bf16[256,1664]{1,0:T(8,128)(2,1)S(1)}, f32[1,512]{1,0:T(1,128)S(1)}, f32[128,256]{1,0:T(8,128)S(1)}, f32[1,256]{1,0:T(1,128)S(1)}) custom-call(f32[256,512]{1,0:T(8,128)S(1)} %fusion.77.dgated_ref, f32[256,512]{1,0:T(8,128)S(1)} %get-tuple-element.149.inner_ref, f32[256,1664]{1,0:T(8,128)S(1)} %fusion.72.cat, ...), custom_call_target="tpu_custom_call" | custom-call | tf_op jit(solution)/shard_map/pallas_call | solution.py:464
  617.4 5.4 fusion.78
  622.9 24.2 %shard_map.296 = (bf16[64,2048]{1,0:T(8,128)(2,1)S(1)}, f32[1,2048]{1,0:T(1,128)S(1)}, bf16[64,2048]{1,0:T(8,128)(2,1)S(1)}, bf16[4,64,2048]{2,1,0:T(8,128)(2,1)S(1)}) custom-call(f32[4,64,2048]{2,1,0:T(8,128)S(1)} %bitcast.256, f32[64,2048]{1,0:T(8,128)S(1)} %get-tuple-element.160.d_middle, bf16[64,2048]{1,0:T(8,128)(2,1)S(1)} %copy-done.40, ...), custom_call_target="tpu_custom_call" | custom-call | tf_op jit(solution)/shard_map/pallas_call | solution.py:464
  647.2 6.9 broadcast_select_fusion.21
  656.0 4.5 convolution_add_fusion.2
  660.8 24.1 %shard_map.297 = (f32[64,2048]{1,0:T(8,128)S(1)}, f32[1,2048]{1,0:T(1,128)S(1)}, bf16[4,64,2048]{2,1,0:T(8,128)(2,1)S(1)}, bf16[3,64,2048]{2,1,0:T(8,128)(2,1)S(1)}) custom-call(f32[4,64,2048]{2,1,0:T(8,128)S(1)} %bitcast.253, bf16[64,2048]{1,0:T(8,128)(2,1)S(1)} %get-tuple-element.162.refs_1_, f32[64,2048]{1,0:T(8,128)S(1)} %get-tuple-element.147.middle.refs_2_, ...), custom_call_target="tpu_custom_call" | custom-call | tf_op jit(solution)/shard_map/pallas_call | solution.py:464
  687.0 15.3 %shard_map.298 = (bf16[256,1664]{1,0:T(8,128)(2,1)S(1)}, f32[1,512]{1,0:T(1,128)S(1)}, f32[128,256]{1,0:T(8,128)S(1)}, f32[1,256]{1,0:T(1,128)S(1)}) custom-call(f32[256,512]{1,0:T(8,128)S(1)} %fusion.80.dgated_ref, f32[256,512]{1,0:T(8,128)S(1)} %get-tuple-element.144.inner_ref, f32[256,1664]{1,0:T(8,128)S(1)} %fusion.68.cat, ...), custom_call_target="tpu_custom_call" | custom-call | tf_op jit(solution)/shard_map/pallas_call | solution.py:464
  702.3 5.4 fusion.81
  707.8 29.2 %shard_map.299 = (bf16[64,2048]{1,0:T(8,128)(2,1)S(1)}, f32[1,2048]{1,0:T(1,128)S(1)}, bf16[64,2048]{1,0:T(8,128)(2,1)S(1)}, bf16[4,64,2048]{2,1,0:T(8,128)(2,1)S(1)}) custom-call(f32[4,64,2048]{2,1,0:T(8,128)S(1)} %bitcast.254, f32[64,2048]{1,0:T(8,128)S(1)} %get-tuple-element.172.d_middle, bf16[64,2048]{1,0:T(8,128)(2,1)S(1)} %get-tuple-element.145.h, ...), custom_call_target="tpu_custom_call" | custom-call | tf_op jit(solution)/shard_map/pallas_call | solution.py:464
  737.1 6.5 broadcast_select_fusion.22
  745.5 4.5 convolution_add_fusion.1
  750.0 21.5 %shard_map.300 = (f32[64,2048]{1,0:T(8,128)S(1)}, f32[1,2048]{1,0:T(1,128)S(1)}, bf16[4,64,2048]{2,1,0:T(8,128)(2,1)S(1)}) custom-call(f32[4,64,2048]{2,1,0:T(8,128)S(1)} %bitcast.260, bf16[64,2048]{1,0:T(8,128)(2,1)S(1)} %get-tuple-element.174.gy, f32[64,2048]{1,0:T(8,128)S(1)} %get-tuple-element.142.middle, f32[1,2048]{1,0:T(1,128)S(1)} %bitcast.310), custom_call_target="tpu_custom_call" | custom-call | tf_op jit(solution)/shard_map/pallas_call | solution.py:464
  773.3 12.1 shard_map.301
  787.3 5.4 fusion.84
  792.7 35.1 %shard_map.302 = (bf16[64,2048]{1,0:T(8,128)(2,1)S(1)}, f32[1,2048]{1,0:T(1,128)S(1)}, bf16[64,2048]{1,0:T(8,128)(2,1)S(1)}, bf16[4,64,2048]{2,1,0:T(8,128)(2,1)S(1)}) custom-call(f32[4,64,2048]{2,1,0:T(8,128)S(1)} %bitcast.255, f32[64,2048]{1,0:T(8,128)S(1)} %get-tuple-element.180.d_middle, bf16[64,2048]{1,0:T(8,128)(2,1)S(1)} %get-tuple-element.140.refs_1_.h, ...), custom_call_target="tpu_custom_call" | custom-call | tf_op jit(solution)/shard_map/pallas_call | solution.py:464
  827.9 2.5 broadcast_select_fusion.5
  830.4 5.0 broadcast_select_fusion.23
  837.8 4.0 convolution_convert_fusion.3
  847.5 4.5 add_convert_fusion.3
  852.1 2.9 convolution_convert_fusion.2
  855.6 4.0 convolution_convert_fusion.1
  868.1 25.7 %collective-permute-done.4 = bf16[512,1408]{1,0:T(8,128)(2,1)S(1)} collective-permute-done((bf16[512,1408]{1,0:T(8,128)(2,1)S(1)}, bf16[512,1408]{1,0:T(8,128)(2,1)S(1)}, u32[]{:S(2)}, u32[]{:S(2)}) %collective-permute-start.4) | collective-permute-done | bytes 1441824 | tf_op jit(solution)/shard_map/ppermute | solution.py:1562
  894.3 4.7 add_convert_fusion.2.refs_4_
  899.0 4.6 add_convert_fusion.1.refs_8_
  903.6 48.9 %shard_map.303 = (f32[64,2048]{1,0:T(8,128)S(1)}, f32[1,2048]{1,0:T(1,128)S(1)}, bf16[4,64,2048]{2,1,0:T(8,128)(2,1)S(1)}, bf16[1,512,1408]{2,1,0:T(8,128)(2,1)S(1)}, bf16[512,1408]{1,0:T(8,128)(2,1)S(1)}) custom-call(f32[4,64,2048]{2,1,0:T(8,128)S(1)} %bitcast.264, bf16[64,2048]{1,0:T(8,128)(2,1)S(1)} %get-tuple-element.186.refs_1_, ...), custom_call_target="tpu_custom_call" | custom-call | tf_op jit(solution)/shard_map/pallas_call | solution.py:464
  957.3 64.9 %shard_map.304 = (bf16[256,1664]{1,0:T(8,128)(2,1)S(1)}, f32[1,512]{1,0:T(1,128)S(1)}, f32[128,256]{1,0:T(8,128)S(1)}, f32[1,256]{1,0:T(1,128)S(1)}, bf16[1,512,...) custom-call(f32[256,512]{1,0:T(8,128)S(1)} %fusion.86.refs_0_, f32[256,512]{1,0:T(8,128)S(1)} %copy-done.7, ...), custom_call_target="tpu_custom_call" | custom-call | tf_op jit(solution)/shard_map/pallas_call | solution.py:464
  1022.5 3.0 copy-done.137
  1025.5 4.6 convolution_convert_fusion
  1036.8 3.4 fusion.87
  1040.7 3.3 bitcast_convert_fusion.1
  1044.1 2.4 add_convert_fusion.5.refs_4_.refs_1_
  1046.5 35.0 %shard_map.305 = (bf16[64,2048]{1,0:T(8,128)(2,1)S(1)}, f32[1,2048]{1,0:T(1,128)S(1)}, bf16[1,512,512]{2,1,0:T(8,128)(2,1)S(1)}, bf16[512,1408]{1,0:T(8,128)(2,1)S(1)}) custom-call(f32[4,64,2048]{2,1,0:T(8,128)S(1)} %bitcast.257, f32[64,2048]{1,0:T(8,128)S(1)} %copy-done.77, bf16[64,2048]{1,0:T(8,128)(2,1)S(1)} %copy-done.9, f32[1,2048]{1,0:T(1,128)S(1)} %bitcast.303, ...), custom_call_target="tpu_custom_call" | custom-call | tf_op jit(solution)/shard_map/pallas_call | solution.py:464
  1083.5 3.3 bitcast_convert_fusion
  1087.8 6.8 add_convert_fusion.refs_0_
  1094.6 99.6 %shard_map.306 = (bf16[512,1664]{1,0:T(8,128)(2,1)S(1)}, bf16[512,512]{1,0:T(8,128)(2,1)S(1)}, bf16[3,4,64,2048]{3,2,1,0:T(8,128)(2,1)}, bf16[3,4,64,2048]{3,2,1...) custom-call(bf16[1024,1664]{1,0:T(8,128)(2,1)} %add_convert_fusion.refs_0_, ...), custom_call_target="tpu_custom_call" | custom-call | tf_op jit(solution)/shard_map/pallas_call | solution.py:1519
  1198.4 5.4 convert.10
  1206.9 4.0 copy.57
  (594 shorter events, 100.2 us)
Async XLA Ops:
  2.9 102.2 %collective-permute-start = (bf16[3,64,2048]{2,1,0:T(8,128)(2,1)}, bf16[3,64,2048]{2,1,0:T(8,128)(2,1)}, u32[]{:S(2)}, u32[]{:S(2)}) collective-permute-start(bf16[3,64,2048]{2,1,0:T(8,128)(2,1)} %constant_dynamic-slice_fusion.3), channel_id=1, source_target_pairs={{8,16},{16,8},{9,17},{17,9},{10,18},{18,10},{11,19},{19,11},{12,20... | collective-permute-start | bytes 2359304 | tf_op jit(solution)/shard_map/ppermute | solution.py:1558
  103.9 86.5 %copy-start.159 = (f32[512]{0:T(512)}, f32[512]{0:T(512)S(1)}, u32[]{:S(2)}) copy-start(f32[512]{0:T(512)S(1)} %get-tuple-element.324) | copy-start | bytes 6148
  107.0 86.6 %copy-start.8 = (bf16[64,2048]{1,0:T(8,128)(2,1)}, bf16[64,2048]{1,0:T(8,128)(2,1)S(1)}, u32[]{:S(2)}) copy-start(bf16[64,2048]{1,0:T(8,128)(2,1)S(1)} %get-tuple-element.322.refs_0_.refs_1_.refs_2_) | copy-start | bytes 786436
  142.8 7.5 copy-start.2
  142.8 7.5 copy-start.53
  142.8 7.5 copy-start.15
  142.8 7.5 copy-start.104
  150.3 40.3 %copy-start = (f32[256,1664]{1,0:T(8,128)}, f32[256,1664]{1,0:T(8,128)S(1)}, u32[]{:S(2)}) copy-start(f32[256,1664]{1,0:T(8,128)S(1)} %fusion.60.refs_0_.refs_2_) | copy-start | bytes 5111812
  291.4 8.0 slice-start.12
  299.4 36.4 %slice-start.22 = ((s8[6815744]{0:T(1024)(128)(4,1)}), s8[4194304]{0:T(1024)(128)(4,1)S(1)}, s32[]{:S(2)}) async-start(s8[6815744]{0:T(1024)(128)(4,1)} %bitcast.321), calls=%async_computation.22 | async-start | bytes 8388608
  299.4 36.4 %slice-start.23 = ((s8[6815744]{0:T(1024)(128)(4,1)}), s8[2621440]{0:T(1024)(128)(4,1)S(1)}, s32[]{:S(2)}) async-start(s8[6815744]{0:T(1024)(128)(4,1)} %bitcast.321), calls=%async_computation.23 | async-start | bytes 5242880
  335.9 13.0 %copy-start.144 = (bf16[256,512]{1,0:T(8,128)(2,1)S(1)}, bf16[256,512]{1,0:T(8,128)(2,1)}, u32[]{:S(2)}) copy-start(bf16[256,512]{1,0:T(8,128)(2,1)} %copy-done.143) | copy-start | bytes 786436
  335.9 13.0 %copy-start.160 = (f32[512]{0:T(512)S(1)}, f32[512]{0:T(512)}, u32[]{:S(2)}) copy-start(f32[512]{0:T(512)} %copy-done.159) | copy-start | bytes 6148
  338.0 37.5 %slice-start = ((s8[5767168]{0:T(1024)(128)(4,1)}), s8[4194304]{0:T(1024)(128)(4,1)S(1)}, s32[]{:S(2)}) async-start(s8[5767168]{0:T(1024)(128)(4,1)} %bitcast.231), calls=%async_computation | async-start | bytes 8388608
  350.0 25.5 %slice-start.1 = ((s8[5767168]{0:T(1024)(128)(4,1)}), s8[1572864]{0:T(1024)(128)(4,1)S(1)}, s32[]{:S(2)}) async-start(s8[5767168]{0:T(1024)(128)(4,1)} %bitcast.231), calls=%async_computation.1 | async-start | bytes 3145728
  375.5 8.3 slice-start.14
  434.2 26.4 %slice-start.4 = ((s8[5767168]{0:T(1024)(128)(4,1)}), s8[1572864]{0:T(1024)(128)(4,1)S(1)}, s32[]{:S(2)}) async-start(s8[5767168]{0:T(1024)(128)(4,1)} %bitcast.235), calls=%async_computation.4 | async-start | bytes 3145728
  495.5 18.7 %copy-start.39 = (bf16[64,2048]{1,0:T(8,128)(2,1)}, bf16[64,2048]{1,0:T(8,128)(2,1)S(1)}, u32[]{:S(2)}) copy-start(bf16[64,2048]{1,0:T(8,128)(2,1)S(1)} %get-tuple-element.150.h) | copy-start | bytes 786436
  513.5 27.3 %slice-start.6 = ((s8[5767168]{0:T(1024)(128)(4,1)}), s8[1572864]{0:T(1024)(128)(4,1)S(1)}, s32[]{:S(2)}) async-start(s8[5767168]{0:T(1024)(128)(4,1)} %bitcast.237), calls=%async_computation.6 | async-start | bytes 3145728
  548.3 29.5 %slice-start.8 = ((s8[5767168]{0:T(1024)(128)(4,1)}), s8[1572864]{0:T(1024)(128)(4,1)S(1)}, s32[]{:S(2)}) async-start(s8[5767168]{0:T(1024)(128)(4,1)} %bitcast.239), calls=%async_computation.8 | async-start | bytes 3145728
  570.1 7.8 slice-start.9
  601.0 16.3 %copy-start.108 = (f32[1,2048]{1,0:T(1,128)}, f32[1,2048]{1,0:T(1,128)S(1)}, u32[]{:S(2)}) copy-start(f32[1,2048]{1,0:T(1,128)S(1)} %get-tuple-element.220) | copy-start | bytes 24580
  622.8 24.3 %copy-start.170 = (bf16[256,1408]{1,0:T(8,128)(2,1)S(1)}, bf16[256,1408]{1,0:T(8,128)(2,1)}, u32[]{:S(2)}) copy-start(bf16[256,1408]{1,0:T(8,128)(2,1)} %copy-done.169) | copy-start | bytes 2162692
  622.9 24.3 %copy-start.177 = (bf16[256,1408]{1,0:T(8,128)(2,1)S(1)}, bf16[256,1408]{1,0:T(8,128)(2,1)}, u32[]{:S(2)}) copy-start(bf16[256,1408]{1,0:T(8,128)(2,1)} %copy-done.176) | copy-start | bytes 2162692
  647.1 7.0 copy-start.94
  647.2 7.0 copy-start.106
  684.9 17.4 %copy-start.112 = (f32[1,2048]{1,0:T(1,128)}, f32[1,2048]{1,0:T(1,128)S(1)}, u32[]{:S(2)}) copy-start(f32[1,2048]{1,0:T(1,128)S(1)} %get-tuple-element.221) | copy-start | bytes 24580
  707.8 29.3 %copy-start.175 = (bf16[256,1408]{1,0:T(8,128)(2,1)S(1)}, bf16[256,1408]{1,0:T(8,128)(2,1)}, u32[]{:S(2)}) copy-start(bf16[256,1408]{1,0:T(8,128)(2,1)} %copy-done.174) | copy-start | bytes 2162692
  707.8 29.3 %copy-start.201 = (f32[256,1408]{1,0:T(8,128)S(1)}, f32[256,1408]{1,0:T(8,128)}, u32[]{:S(2)}) copy-start(f32[256,1408]{1,0:T(8,128)} %copy-done.200) | copy-start | bytes 4325380
  737.1 6.6 copy-start.96
  737.1 6.5 copy-start.110
  771.5 13.9 %copy-start.116 = (f32[1,2048]{1,0:T(1,128)}, f32[1,2048]{1,0:T(1,128)S(1)}, u32[]{:S(2)}) copy-start(f32[1,2048]{1,0:T(1,128)S(1)} %get-tuple-element.222) | copy-start | bytes 24580
  787.2 40.6 %copy-start.36 = (bf16[4,64,2048]{2,1,0:T(8,128)(2,1)S(1)}, bf16[4,64,2048]{2,1,0:T(8,128)(2,1)}, u32[]{:S(2)}) copy-start(bf16[4,64,2048]{2,1,0:T(8,128)(2,1)} %copy-done.35) | copy-start | bytes 3145732
  787.2 40.6 %copy-start.38 = (bf16[4,64,2048]{2,1,0:T(8,128)(2,1)S(1)}, bf16[4,64,2048]{2,1,0:T(8,128)(2,1)}, u32[]{:S(2)}) copy-start(bf16[4,64,2048]{2,1,0:T(8,128)(2,1)} %copy-done.37) | copy-start | bytes 3145732
  787.2 43.1 %slice-start.20 = ((s8[5767168]{0:T(1024)(128)(4,1)}), s8[4194304]{0:T(1024)(128)(4,1)S(1)}, s32[]{:S(2)}) async-start(s8[5767168]{0:T(1024)(128)(4,1)} %bitcast.251), calls=%async_computation.20 | async-start | bytes 8388608
  792.6 35.2 %copy-start.30 = (bf16[4,64,2048]{2,1,0:T(8,128)(2,1)S(1)}, bf16[4,64,2048]{2,1,0:T(8,128)(2,1)}, u32[]{:S(2)}) copy-start(bf16[4,64,2048]{2,1,0:T(8,128)(2,1)} %copy-done.28) | copy-start | bytes 3145732
  792.6 35.2 %copy-start.32 = (bf16[4,64,2048]{2,1,0:T(8,128)(2,1)S(1)}, bf16[4,64,2048]{2,1,0:T(8,128)(2,1)}, u32[]{:S(2)}) copy-start(bf16[4,64,2048]{2,1,0:T(8,128)(2,1)} %copy-done.31) | copy-start | bytes 3145732
  792.7 35.2 %copy-start.34 = (bf16[4,64,2048]{2,1,0:T(8,128)(2,1)S(1)}, bf16[4,64,2048]{2,1,0:T(8,128)(2,1)}, u32[]{:S(2)}) copy-start(bf16[4,64,2048]{2,1,0:T(8,128)(2,1)} %copy-done.33) | copy-start | bytes 3145732
  792.7 37.7 %slice-start.21 = ((s8[5767168]{0:T(1024)(128)(4,1)}), s8[1572864]{0:T(1024)(128)(4,1)S(1)}, s32[]{:S(2)}) async-start(s8[5767168]{0:T(1024)(128)(4,1)} %bitcast.251), calls=%async_computation.21 | async-start | bytes 3145728
  841.8 5.6 collective-permute-start.1
  855.0 39.2 %collective-permute-start.2 = (bf16[1024,1408]{1,0:T(8,128)(2,1)S(1)}, bf16[1024,1408]{1,0:T(8,128)(2,1)}, u32[]{:S(2)}, u32[]{:S(2)}) collective-permute-start(bf16[1024,1408]{1,0:T(8,128)(2,1)S(1)} %convolution_convert_fusion.2), channel_id=1, source_target_pairs={{0,16},{16,0},{1,17},{17,1},{2,18},{18,2},{3,19},{19,3},{4,20},{20... | collective-permute-start | bytes 8650760 | tf_op jit(solution)/shard_map/ppermute | solution.py:1562
  855.5 8.4 slice-start.2
  859.6 39.4 %collective-permute-start.3 = (bf16[1024,1408]{1,0:T(8,128)(2,1)}, bf16[1024,1408]{1,0:T(8,128)(2,1)}, u32[]{:S(2)}, u32[]{:S(2)}) collective-permute-start(bf16[1024,1408]{1,0:T(8,128)(2,1)} %convolution_convert_fusion.1), channel_id=1, source_target_pairs={{0,16},{16,0},{1,17},{17,1},{2,18},{18,2},{3,19},{19,3},{4,20},{20... | collective-permute-start | bytes 8650760 | tf_op jit(solution)/shard_map/ppermute | solution.py:1562
  859.8 34.0 %collective-permute-start.4 = (bf16[512,1408]{1,0:T(8,128)(2,1)S(1)}, bf16[512,1408]{1,0:T(8,128)(2,1)S(1)}, u32[]{:S(2)}, u32[]{:S(2)}) collective-permute-start(bf16[512,1408]{1,0:T(8,128)(2,1)S(1)} %constant_dynamic-slice_fusion.1), channel_id=1, source_target_pairs={{0,4},{4,0},{1,5},{5,1},{2,6},{6,2},{3,7},{7,3},{8,12},{12,8},{9,1... | collective-permute-start | bytes 4325384 | tf_op jit(solution)/shard_map/ppermute | solution.py:1562
  868.1 26.1 %copy-start.187 = (bf16[256,1408]{1,0:T(8,128)(2,1)S(1)}, bf16[256,1408]{1,0:T(8,128)(2,1)}, u32[]{:S(2)}) copy-start(bf16[256,1408]{1,0:T(8,128)(2,1)} %get-tuple-element.282) | copy-start | bytes 2162692
  868.1 26.1 %copy-start.189 = (bf16[256,1408]{1,0:T(8,128)(2,1)S(1)}, bf16[256,1408]{1,0:T(8,128)(2,1)}, u32[]{:S(2)}) copy-start(bf16[256,1408]{1,0:T(8,128)(2,1)} %get-tuple-element.280) | copy-start | bytes 2162692
  868.1 26.1 %copy-start.195 = (bf16[256,1408]{1,0:T(8,128)(2,1)S(1)}, bf16[256,1408]{1,0:T(8,128)(2,1)}, u32[]{:S(2)}) copy-start(bf16[256,1408]{1,0:T(8,128)(2,1)} %get-tuple-element.278) | copy-start | bytes 2162692
  903.6 49.0 %copy-start.58 = (bf16[4,64,2048]{2,1,0:T(8,128)(2,1)S(1)}, bf16[4,64,2048]{2,1,0:T(8,128)(2,1)}, u32[]{:S(2)}) copy-start(bf16[4,64,2048]{2,1,0:T(8,128)(2,1)} %copy-done.57) | copy-start | bytes 3145732
  903.6 49.0 %copy-start.64 = (bf16[4,64,2048]{2,1,0:T(8,128)(2,1)S(1)}, bf16[4,64,2048]{2,1,0:T(8,128)(2,1)}, u32[]{:S(2)}) copy-start(bf16[4,64,2048]{2,1,0:T(8,128)(2,1)} %copy-done.63) | copy-start | bytes 3145732
  903.6 49.0 %copy-start.66 = (bf16[4,64,2048]{2,1,0:T(8,128)(2,1)S(1)}, bf16[4,64,2048]{2,1,0:T(8,128)(2,1)}, u32[]{:S(2)}) copy-start(bf16[4,64,2048]{2,1,0:T(8,128)(2,1)} %copy-done.65) | copy-start | bytes 3145732
  957.3 64.9 %copy-start.68 = (bf16[256,1664]{1,0:T(8,128)(2,1)S(1)}, bf16[256,1664]{1,0:T(8,128)(2,1)}, u32[]{:S(2)}) copy-start(bf16[256,1664]{1,0:T(8,128)(2,1)} %copy-done.67) | copy-start | bytes 2555908
  957.3 64.9 %copy-start.70 = (bf16[256,1664]{1,0:T(8,128)(2,1)S(1)}, bf16[256,1664]{1,0:T(8,128)(2,1)}, u32[]{:S(2)}) copy-start(bf16[256,1664]{1,0:T(8,128)(2,1)} %copy-done.69) | copy-start | bytes 2555908
  957.3 64.9 %copy-start.72 = (bf16[256,1664]{1,0:T(8,128)(2,1)S(1)}, bf16[256,1664]{1,0:T(8,128)(2,1)}, u32[]{:S(2)}) copy-start(bf16[256,1664]{1,0:T(8,128)(2,1)} %copy-done.71) | copy-start | bytes 2555908
  1022.2 7.9 copy-start.18
  1022.5 7.6 copy-start.145
  1022.5 7.6 copy-start.147
  1022.5 7.6 copy-start.149
  1030.1 56.9 %collective-permute-start.5 = (bf16[1024,1664]{1,0:T(8,128)(2,1)}, bf16[1024,1664]{1,0:T(8,128)(2,1)}, u32[]{:S(2)}, u32[]{:S(2)}) collective-permute-start(bf16[1024,1664]{1,0:T(8,128)(2,1)} %convolution_convert_fusion), channel_id=1, source_target_pairs={{0,16},{16,0},{1,17},{17,1},{2,18},{18,2},{3,19},{19,3},{4,20},{20... | collective-permute-start | bytes 10223624 | tf_op jit(solution)/shard_map/ppermute | solution.py:1562
  1033.4 10.6 collective-permute-start.6
  1046.5 36.2 %copy-start.107 = (f32[1,2048]{1,0:T(1,128)S(1)}, f32[1,2048]{1,0:T(1,128)}, u32[]{:S(2)}) copy-start(f32[1,2048]{1,0:T(1,128)} %copy-done.106) | copy-start | bytes 24580
  1046.5 36.2 %copy-start.111 = (f32[1,2048]{1,0:T(1,128)S(1)}, f32[1,2048]{1,0:T(1,128)}, u32[]{:S(2)}) copy-start(f32[1,2048]{1,0:T(1,128)} %copy-done.110) | copy-start | bytes 24580
  1046.5 36.2 %copy-start.115 = (f32[1,2048]{1,0:T(1,128)S(1)}, f32[1,2048]{1,0:T(1,128)}, u32[]{:S(2)}) copy-start(f32[1,2048]{1,0:T(1,128)} %copy-done.114) | copy-start | bytes 24580
  1082.9 4.0 collective-permute-start.7
  1087.0 7.7 copy-start.10
  (174 other events, 535.7 us)
